TPU v7x, 32 devices: a whole 2x2x4 slice. The times are simulated.
32 devices in a mesh: fsdp: 8 (over z, core), tp: 4 (over y, x).
Axes of the slice: x: 2, y: 2, z: 4, core: 2. Of those that a mesh axis runs over, the one named last changes fastest.
Arguments:
- tokens: bfloat16 [8192, 2048], P(('fsdp', 'tp')), may hold values from -6 to 6
- cotangent: bfloat16 [8192, 2048], P(('fsdp', 'tp')), may hold values from -6 to 6
- routes: int32 [8192, 8], P('fsdp'), may hold values from 0 to 31, all different within a row; in each aligned block of 1024 rows (0 to 1023, 1024 to 2047, ...) at most 320 rows name the same one
- gain_attn: bfloat16 [2048], P('fsdp'), may hold values from 0.099609375 to 1.8984375
- w_query: bfloat16 [2048, 2048], P('fsdp', 'tp'), may hold values from -0.125 to 0.125
- w_key: bfloat16 [2048, 2048], P('fsdp', 'tp'), may hold values from -0.125 to 0.125
- w_value: bfloat16 [2048, 2048], P('fsdp', 'tp'), may hold values from -0.125 to 0.125
- gain_query: bfloat16 [2048], P('fsdp'), may hold values from 0.099609375 to 1.8984375
- gain_key: bfloat16 [2048], P('fsdp'), may hold values from 0.099609375 to 1.8984375
- w_out: bfloat16 [2048, 2048], P('tp', 'fsdp'), may hold values from -1 to 1
- gain_moe: bfloat16 [2048], P('fsdp'), may hold values from 0.099609375 to 1.8984375
- w_router: bfloat16 [2048, 32], P('fsdp'), may hold values from -0.0625 to 0.0625
- w_gate: bfloat16 [32, 2048, 1024], P('fsdp', None, 'tp'), may hold values from -0.125 to 0.125
- w_up: bfloat16 [32, 2048, 1024], P('fsdp', None, 'tp'), may hold values from -0.125 to 0.125
- w_down: bfloat16 [32, 1024, 2048], P('fsdp', 'tp'), may hold values from -4 to 4
Outputs:
- output: bfloat16 [8192, 2048], P(('fsdp', 'tp'))
- grad_tokens: float32 [8192, 2048], P(('fsdp', 'tp'))
- grad_gain_attn: float32 [2048], P('fsdp')
- grad_w_query: float32 [2048, 2048], P('fsdp', 'tp')
- grad_w_key: float32 [2048, 2048], P('fsdp', 'tp')
- grad_w_value: float32 [2048, 2048], P('fsdp', 'tp')
- grad_gain_query: float32 [2048], P('fsdp')
- grad_gain_key: float32 [2048], P('fsdp')
- grad_w_out: float32 [2048, 2048], P('tp', 'fsdp')
- grad_gain_moe: float32 [2048], P('fsdp')
- grad_w_router: float32 [2048, 32], P('fsdp')
- grad_w_gate: float32 [32, 2048, 1024], P('fsdp', None, 'tp')
- grad_w_up: float32 [32, 2048, 1024], P('fsdp', None, 'tp')
- grad_w_down: float32 [32, 1024, 2048], P('fsdp', 'tp')
Inputs may be any that keep to these rules, and one draw needn't show every extreme that they name: `routes`: within the 1024 rows of one index of fsdp (one aligned block), each row names 8 different experts and no expert is named by more than 320 rows; some expert is named by exactly 320 rows in some block of every draw.
All inputs are finite; a program needn't handle non-finite values.
Results may differ from a plain program's by a relative error of at most 0.02.
Values may be sent and summed in bfloat16 or wider, within the bound.
No kernel may reach another device: no remote copies, remote signals or barrier semaphores. Data moves between devices by JAX's collectives and lax.ppermute only.
A program may use at most 512 MiB of HBM per device.

v0:
```python
import jax
import jax.numpy as jnp
from jax import lax
from jax.sharding import PartitionSpec as P

HEAD_DIM = 128


EPSILON = 1e-05
ROPE_BASE = 10000.0


def gather_pieces(operand):
    return lax.all_gather(operand, "tp", axis=0, tiled=True)


def scatter_partial(operand):
    return lax.psum_scatter(operand, "tp", scatter_dimension=0, tiled=True)


def across_heads(operands):
    return lax.psum(operands, "tp")


def to_owners(operand):
    return lax.all_to_all(operand, "fsdp", split_axis=1, concat_axis=1, tiled=True)


def from_owners(operand):
    return lax.all_to_all(operand, "fsdp", split_axis=1, concat_axis=1, tiled=True)


def rope_tables(length, columns):
    halfway = columns // 2
    positions = jnp.arange(length).astype(jnp.float32)
    frequency = ROPE_BASE ** (-2.0 * jnp.arange(halfway).astype(jnp.float32) / columns)
    angles = positions[:, None] * frequency[None, :]
    angles = jnp.concatenate([angles, angles], axis=-1)
    return (jnp.cos(angles)[:, None, :], jnp.sin(angles)[:, None, :])


def rotate(tensor):
    halfway = tensor.shape[-1] // 2
    return jnp.concatenate([-tensor[..., halfway:], tensor[..., :halfway]], axis=-1)


def rotate_back(tensor):
    halfway = tensor.shape[-1] // 2
    return jnp.concatenate([tensor[..., halfway:], -tensor[..., :halfway]], axis=-1)


def norm_rows(tensor):
    row_scale = lax.rsqrt(jnp.mean(tensor * tensor, axis=-1, keepdims=True) + EPSILON)
    return (tensor * row_scale, row_scale)


def norm_back(normed, row_scale, grad_normed):
    return row_scale * (
        grad_normed - normed * jnp.mean(normed * grad_normed, axis=-1, keepdims=True)
    )


def shards(
    tokens,
    cotangent,
    routes,
    gain_attn,
    w_query,
    w_key,
    w_value,
    gain_query,
    gain_key,
    w_out,
    gain_moe,
    w_router,
    w_gate,
    w_up,
    w_down,
):
    tp_count = lax.axis_size("tp")
    tp_rank = lax.axis_index("tp")
    fsdp_count = lax.axis_size("fsdp")
    query_w, key_w, value_w, out_w, router_w, attn_gain, moe_gain, query_gain, key_gain = (
        lax.all_gather(w_query, "fsdp", axis=0, tiled=True),
        lax.all_gather(w_key, "fsdp", axis=0, tiled=True),
        lax.all_gather(w_value, "fsdp", axis=0, tiled=True),
        lax.all_gather(w_out, "fsdp", axis=1, tiled=True),
        lax.all_gather(w_router, "fsdp", axis=0, tiled=True),
        lax.all_gather(gain_attn, "fsdp", axis=0, tiled=True),
        lax.all_gather(gain_moe, "fsdp", axis=0, tiled=True),
        lax.all_gather(gain_query, "fsdp", axis=0, tiled=True),
        lax.all_gather(gain_key, "fsdp", axis=0, tiled=True),
    )
    model_width = tokens.shape[1]
    local_width = query_w.shape[1]
    seq_len = tokens.shape[0] * tp_count
    head_count = local_width // HEAD_DIM
    expert_count = router_w.shape[1]
    top_count = routes.shape[1]
    local_experts = w_gate.shape[0]
    scale_factor = HEAD_DIM ** (-0.5)
    column_start = tp_rank * local_width
    local_qgain = lax.dynamic_slice_in_dim(query_gain, column_start, local_width).astype(
        jnp.float32
    )
    local_kgain = lax.dynamic_slice_in_dim(key_gain, column_start, local_width).astype(jnp.float32)
    head_shape = (seq_len, head_count, HEAD_DIM)
    residual_in = tokens.astype(jnp.float32)
    normed_one, scale_one = norm_rows(residual_in)
    first_in = (normed_one * attn_gain.astype(jnp.float32)).astype(jnp.bfloat16)
    first_all = gather_pieces(first_in)
    query_raw = jnp.dot(first_all, query_w, preferred_element_type=jnp.float32)
    key_raw = jnp.dot(first_all, key_w, preferred_element_type=jnp.float32)
    value_raw = jnp.dot(first_all, value_w, preferred_element_type=jnp.float32)
    query_sq, key_sq = across_heads(
        (jnp.sum(query_raw * query_raw, axis=-1), jnp.sum(key_raw * key_raw, axis=-1))
    )
    query_scale = lax.rsqrt(query_sq / model_width + EPSILON)[:, None]
    key_scale = lax.rsqrt(key_sq / model_width + EPSILON)[:, None]
    cosine, sine_table = rope_tables(seq_len, HEAD_DIM)
    query_normed = (query_raw * query_scale * local_qgain).reshape(head_shape)
    key_normed = (key_raw * key_scale * local_kgain).reshape(head_shape)
    query_bf = (query_normed * cosine + rotate(query_normed) * sine_table).astype(jnp.bfloat16)
    key_bf = (key_normed * cosine + rotate(key_normed) * sine_table).astype(jnp.bfloat16)
    value_bf = value_raw.astype(jnp.bfloat16).reshape(head_shape)
    block_rows = min(512, seq_len)
    block_count = seq_len // block_rows
    key_pos = jnp.arange(seq_len)

    def block_scores(block_index):
        query_block = lax.dynamic_slice_in_dim(query_bf, block_index * block_rows, block_rows, 0)
        scores = (
            jnp.einsum("qhd,khd->hqk", query_block, key_bf, preferred_element_type=jnp.float32)
            * scale_factor
        )
        query_pos = block_index * block_rows + jnp.arange(block_rows)
        causal = query_pos[:, None] >= key_pos[None, :]
        return (query_block, jnp.where(causal[None], scores, -1e30), causal)

    def attend_block(block_index):
        query_block, scores, causal = block_scores(block_index)
        top_score = jnp.max(scores, axis=-1, keepdims=True)
        exponent = jnp.exp(scores - top_score)
        row_total = jnp.sum(exponent, axis=-1, keepdims=True)
        attn_probs = (exponent / row_total).astype(jnp.bfloat16)
        outcome = jnp.einsum(
            "hqk,khd->qhd", attn_probs, value_bf, preferred_element_type=jnp.float32
        )
        return (outcome, top_score[..., 0] + jnp.log(row_total[..., 0]))

    attn_blocks, log_totals = lax.map(attend_block, jnp.arange(block_count))
    heads_out = attn_blocks.reshape(seq_len, local_width).astype(jnp.bfloat16)
    attn_sum = scatter_partial(jnp.dot(heads_out, out_w, preferred_element_type=jnp.float32))
    hidden_res = residual_in + attn_sum
    normed_two, scale_two = norm_rows(hidden_res)
    second_in = (normed_two * moe_gain.astype(jnp.float32)).astype(jnp.bfloat16)
    second_all = gather_pieces(second_in)
    logits = jnp.dot(second_all, router_w, preferred_element_type=jnp.float32)
    router_probs = jax.nn.softmax(logits, axis=-1)
    gate_values = jnp.take_along_axis(router_probs, routes, axis=1)
    capacity = (seq_len * top_count * 5 // (4 * expert_count) + tp_count - 1) // tp_count * tp_count
    window = capacity // tp_count
    window_start = tp_rank * window
    flat_routes = routes.reshape(-1)
    assign_count = flat_routes.shape[0]
    onehot = (flat_routes[:, None] == jnp.arange(expert_count, dtype=jnp.int32)[None, :]).astype(
        jnp.int32
    )
    slot_rank = jnp.sum(onehot * (jnp.cumsum(onehot, axis=0) - 1), axis=1)
    local_slot = slot_rank - window_start
    owned_slot = (local_slot >= 0) & (local_slot < window)
    slot_total = window * expert_count
    position = jnp.where(owned_slot, local_slot * expert_count + flat_routes, slot_total)
    token_of = (
        jnp.full((slot_total + 1,), seq_len, jnp.int32)
        .at[position]
        .set(jnp.arange(assign_count, dtype=jnp.int32) // top_count)[:slot_total]
    )
    gate_of = (
        jnp.zeros((slot_total + 1,), jnp.float32)
        .at[position]
        .set(gate_values.reshape(-1))[:slot_total]
    )
    expert_of = jnp.arange(slot_total, dtype=jnp.int32) % expert_count
    padded_in = jnp.concatenate([second_all, jnp.zeros((1, model_width), jnp.bfloat16)], axis=0)
    send_rows = padded_in[token_of].reshape(window, expert_count, model_width)
    gate_use, up_use, down_use = (
        lax.all_gather(w_gate, "tp", axis=2, tiled=True),
        lax.all_gather(w_up, "tp", axis=2, tiled=True),
        lax.all_gather(w_down, "tp", axis=1, tiled=True),
    )
    owned_rows = to_owners(send_rows).reshape(window, fsdp_count, local_experts, model_width)
    gate_pre = jnp.einsum(
        "wsed,edh->wseh", owned_rows, gate_use, preferred_element_type=jnp.float32
    )
    up_pre = jnp.einsum("wsed,edh->wseh", owned_rows, up_use, preferred_element_type=jnp.float32)
    activated = jax.nn.silu(gate_pre)
    hidden_bf = (activated * up_pre).astype(jnp.bfloat16)
    expert_out = jnp.einsum(
        "wseh,ehd->wsed", hidden_bf, down_use, preferred_element_type=jnp.float32
    )
    returned = from_owners(expert_out.reshape(window, expert_count, model_width)).reshape(
        slot_total, model_width
    )
    moe_part = jax.ops.segment_sum(returned * gate_of[:, None], token_of, num_segments=seq_len + 1)[
        :seq_len
    ]
    moe_sum = scatter_partial(moe_part)
    output = (hidden_res + moe_sum).astype(jnp.bfloat16)
    grad_out = cotangent.astype(jnp.float32)
    grad_all = gather_pieces(cotangent)
    grad_rows = jnp.concatenate([grad_all, jnp.zeros((1, model_width), jnp.bfloat16)], axis=0)[
        token_of
    ].astype(jnp.float32)
    gate_grad = jnp.sum(returned * grad_rows, axis=-1)
    expert_grad = (
        (grad_rows * gate_of[:, None])
        .astype(jnp.bfloat16)
        .reshape(window, expert_count, model_width)
    )
    sigmoid_gate = jax.nn.sigmoid(gate_pre)
    owned_grad = to_owners(expert_grad).reshape(window, fsdp_count, local_experts, model_width)
    hidden_grad = jnp.einsum(
        "wsed,ehd->wseh", owned_grad, down_use, preferred_element_type=jnp.float32
    )
    down_w_grad = jnp.einsum(
        "wseh,wsed->ehd", hidden_bf, owned_grad, preferred_element_type=jnp.float32
    )
    gate_pre_grad = (
        hidden_grad * up_pre * sigmoid_gate * (1.0 + gate_pre * (1.0 - sigmoid_gate))
    ).astype(jnp.bfloat16)
    up_pre_grad = (hidden_grad * activated).astype(jnp.bfloat16)
    gate_w_grad = jnp.einsum(
        "wsed,wseh->edh", owned_rows, gate_pre_grad, preferred_element_type=jnp.float32
    )
    up_w_grad = jnp.einsum(
        "wsed,wseh->edh", owned_rows, up_pre_grad, preferred_element_type=jnp.float32
    )
    rows_grad = jnp.einsum(
        "wseh,edh->wsed", gate_pre_grad, gate_use, preferred_element_type=jnp.float32
    )
    rows_grad = rows_grad + jnp.einsum(
        "wseh,edh->wsed", up_pre_grad, up_use, preferred_element_type=jnp.float32
    )
    rows_back = from_owners(rows_grad.reshape(window, expert_count, model_width)).reshape(
        slot_total, model_width
    )
    gate_w_grad, up_w_grad, down_w_grad = (
        lax.psum_scatter(
            gate_w_grad.astype(jnp.bfloat16), "tp", scatter_dimension=2, tiled=True
        ).astype(jnp.float32),
        lax.psum_scatter(
            up_w_grad.astype(jnp.bfloat16), "tp", scatter_dimension=2, tiled=True
        ).astype(jnp.float32),
        lax.psum_scatter(
            down_w_grad.astype(jnp.bfloat16), "tp", scatter_dimension=1, tiled=True
        ).astype(jnp.float32),
    )
    prob_grad = (
        jnp.zeros((seq_len + 1, expert_count), jnp.float32)
        .at[token_of, expert_of]
        .add(gate_grad)[:seq_len]
    )
    logit_grad = router_probs * (
        prob_grad - jnp.sum(router_probs * prob_grad, axis=-1, keepdims=True)
    )
    router_grad = jnp.dot(
        second_all.astype(jnp.float32).T, logit_grad, precision=lax.Precision.HIGHEST
    )
    second_part = jax.ops.segment_sum(rows_back, token_of, num_segments=seq_len + 1)[:seq_len]
    second_part = second_part + jnp.dot(
        logit_grad, router_w.astype(jnp.float32).T, precision=lax.Precision.HIGHEST
    )
    second_grad = scatter_partial(second_part)
    moe_gain_grad = jnp.sum(normed_two * second_grad, axis=0)
    residual_grad = grad_out + norm_back(
        normed_two, scale_two, second_grad * moe_gain.astype(jnp.float32)
    )
    residual_all = gather_pieces(residual_grad.astype(jnp.bfloat16))
    out_w_grad = jnp.einsum(
        "tk,td->kd", heads_out, residual_all, preferred_element_type=jnp.float32
    )
    heads_grad = (
        jnp.einsum("td,kd->tk", residual_all, out_w, preferred_element_type=jnp.float32)
        .astype(jnp.bfloat16)
        .reshape(head_shape)
    )

    def back_block(carried, block_index):
        key_acc, value_acc = carried
        query_block, scores, causal = block_scores(block_index)
        log_block = log_totals[block_index]
        probs_full = jnp.where(causal[None], jnp.exp(scores - log_block[..., None]), 0.0)
        probs_bf = probs_full.astype(jnp.bfloat16)
        out_block = lax.dynamic_slice_in_dim(heads_grad, block_index * block_rows, block_rows, 0)
        value_acc = value_acc + jnp.einsum(
            "hqk,qhd->khd", probs_bf, out_block, preferred_element_type=jnp.float32
        )
        prob_block_grad = jnp.einsum(
            "qhd,khd->hqk", out_block, value_bf, preferred_element_type=jnp.float32
        )
        centre = jnp.sum(probs_full * prob_block_grad, axis=-1, keepdims=True)
        score_grad = (probs_full * (prob_block_grad - centre)).astype(jnp.bfloat16)
        query_block_grad = (
            jnp.einsum("hqk,khd->qhd", score_grad, key_bf, preferred_element_type=jnp.float32)
            * scale_factor
        )
        key_acc = (
            key_acc
            + jnp.einsum(
                "hqk,qhd->khd", score_grad, query_block, preferred_element_type=jnp.float32
            )
            * scale_factor
        )
        return ((key_acc, value_acc), query_block_grad)

    zero_heads = jnp.zeros(head_shape, jnp.float32)
    (key_rot_grad, value_grad), query_blocks_grad = lax.scan(
        back_block, (zero_heads, zero_heads), jnp.arange(block_count)
    )
    query_rot_grad = query_blocks_grad.reshape(head_shape)
    query_norm_grad = (query_rot_grad * cosine + rotate_back(query_rot_grad * sine_table)).reshape(
        seq_len, local_width
    )
    key_norm_grad = (key_rot_grad * cosine + rotate_back(key_rot_grad * sine_table)).reshape(
        seq_len, local_width
    )
    qgain_local = jnp.sum(query_raw * query_scale * query_norm_grad, axis=0)
    kgain_local = jnp.sum(key_raw * key_scale * key_norm_grad, axis=0)
    query_inner = query_norm_grad * local_qgain
    key_inner = key_norm_grad * local_kgain
    query_dot, key_dot = across_heads(
        (jnp.sum(query_raw * query_inner, axis=-1), jnp.sum(key_raw * key_inner, axis=-1))
    )
    query_raw_grad = (
        query_scale * query_inner - query_raw * query_scale**3 * query_dot[:, None] / model_width
    ).astype(jnp.bfloat16)
    key_raw_grad = (
        key_scale * key_inner - key_raw * key_scale**3 * key_dot[:, None] / model_width
    ).astype(jnp.bfloat16)
    value_raw_grad = value_grad.reshape(seq_len, local_width).astype(jnp.bfloat16)
    query_w_grad = jnp.einsum(
        "td,tk->dk", first_all, query_raw_grad, preferred_element_type=jnp.float32
    )
    key_w_grad = jnp.einsum(
        "td,tk->dk", first_all, key_raw_grad, preferred_element_type=jnp.float32
    )
    value_w_grad = jnp.einsum(
        "td,tk->dk", first_all, value_raw_grad, preferred_element_type=jnp.float32
    )
    first_part = jnp.einsum(
        "tk,dk->td", query_raw_grad, query_w, preferred_element_type=jnp.float32
    )
    first_part = first_part + jnp.einsum(
        "tk,dk->td", key_raw_grad, key_w, preferred_element_type=jnp.float32
    )
    first_part = first_part + jnp.einsum(
        "tk,dk->td", value_raw_grad, value_w, preferred_element_type=jnp.float32
    )
    first_grad = scatter_partial(first_part)
    attn_gain_grad = jnp.sum(normed_one * first_grad, axis=0)
    input_grad = residual_grad + norm_back(
        normed_one, scale_one, first_grad * attn_gain.astype(jnp.float32)
    )
    qgain_full = lax.dynamic_update_slice_in_dim(
        jnp.zeros((model_width,), jnp.float32), qgain_local, column_start, 0
    )
    kgain_full = lax.dynamic_update_slice_in_dim(
        jnp.zeros((model_width,), jnp.float32), kgain_local, column_start, 0
    )
    attn_gain_grad, moe_gain_grad, qgain_full, kgain_full, router_grad = across_heads(
        (attn_gain_grad, moe_gain_grad, qgain_full, kgain_full, router_grad)
    )
    reduced = (
        lax.psum_scatter(
            query_w_grad.astype(jnp.bfloat16), "fsdp", scatter_dimension=0, tiled=True
        ).astype(jnp.float32),
        lax.psum_scatter(
            key_w_grad.astype(jnp.bfloat16), "fsdp", scatter_dimension=0, tiled=True
        ).astype(jnp.float32),
        lax.psum_scatter(
            value_w_grad.astype(jnp.bfloat16), "fsdp", scatter_dimension=0, tiled=True
        ).astype(jnp.float32),
        lax.psum_scatter(
            out_w_grad.astype(jnp.bfloat16), "fsdp", scatter_dimension=1, tiled=True
        ).astype(jnp.float32),
        lax.psum_scatter(
            router_grad.astype(jnp.bfloat16), "fsdp", scatter_dimension=0, tiled=True
        ).astype(jnp.float32),
        lax.psum_scatter(
            attn_gain_grad.astype(jnp.bfloat16), "fsdp", scatter_dimension=0, tiled=True
        ).astype(jnp.float32),
        lax.psum_scatter(
            moe_gain_grad.astype(jnp.bfloat16), "fsdp", scatter_dimension=0, tiled=True
        ).astype(jnp.float32),
        lax.psum_scatter(
            qgain_full.astype(jnp.bfloat16), "fsdp", scatter_dimension=0, tiled=True
        ).astype(jnp.float32),
        lax.psum_scatter(
            kgain_full.astype(jnp.bfloat16), "fsdp", scatter_dimension=0, tiled=True
        ).astype(jnp.float32),
    )
    return (
        output,
        input_grad,
        reduced[5],
        reduced[0],
        reduced[1],
        reduced[2],
        reduced[7],
        reduced[8],
        reduced[3],
        reduced[6],
        reduced[4],
        gate_w_grad,
        up_w_grad,
        down_w_grad,
    )


def solution(mesh):
    placed = (
        P(("fsdp", "tp"), None),
        P(("fsdp", "tp"), None),
        P("fsdp", None),
        P("fsdp"),
        P("fsdp", "tp"),
        P("fsdp", "tp"),
        P("fsdp", "tp"),
        P("fsdp"),
        P("fsdp"),
        P("tp", "fsdp"),
        P("fsdp"),
        P("fsdp", None),
        P("fsdp", None, "tp"),
        P("fsdp", None, "tp"),
        P("fsdp", "tp", None),
    )
    return jax.shard_map(
        shards,
        mesh=mesh,
        in_specs=placed,
        out_specs=(
            P(("fsdp", "tp"), None),
            P(("fsdp", "tp"), None),
            P("fsdp"),
            P("fsdp", "tp"),
            P("fsdp", "tp"),
            P("fsdp", "tp"),
            P("fsdp"),
            P("fsdp"),
            P("tp", "fsdp"),
            P("fsdp"),
            P("fsdp", None),
            P("fsdp", None, "tp"),
            P("fsdp", None, "tp"),
            P("fsdp", "tp", None),
        ),
        check_vma=False,
    )
```

profile of v0, /device:TPU:0, one launch (start us, length us, event | category | flops | bytes accessed | tf_op | source)
XLA Modules:
  0.0 3368.9 jit_solution(11402865334748897935)
XLA Ops:
  52.0 44.2 %all-gather.16.cloned.1.call-done = bf16[1024,2048]{1,0:T(8,128)(2,1)} async-done(((bf16[256,2048]{1,0:T(8,128)(2,1)}), bf16[1024,2048]{1,0:T(8,128)(2,1)}) %all-gather.16.cloned.1.call-update) | async-done | bytes 4194320 | tf_op jit(solution)/shard_map/all_gather | solution.py:14
  102.7 24.2 all-gather.20.cloned.1.call-done
  210.9 75.3 %reduce-scatter.13.cloned.1.call-done = f32[256,2048]{1,0:T(8,128)} async-done(((f32[1024,2048]{1,0:T(8,128)}), f32[256,2048]{1,0:T(8,128)}) %reduce-scatter.13.cloned.1.call-update) | async-done | bytes 2097168 | tf_op jit(solution)/shard_map/reduce_scatter | solution.py:18
  305.8 30.5 scatter_custom_fusion
  390.8 112.0 %all-gather.28.cloned.1.call-done = bf16[4,2048,1024]{2,1,0:T(8,128)(2,1)} async-done(((bf16[4,2048,256]{2,1,0:T(8,128)(2,1)}), bf16[4,2048,1024]{2,1,0:T(8,128)(2,1)}) %all-gather.28.cloned.1.call-update) | async-done | bytes 16777232 | tf_op jit(solution)/shard_map/all_gather | solution.py:188
  502.8 116.9 %all-to-all-done = bf16[80,32,2048]{2,0,1:T(8,128)(2,1)} async-done(((bf16[80,32,2048]{2,0,1:T(8,128)(2,1)}), bf16[80,32,2048]{2,0,1:T(8,128)(2,1)}, u32[]{:S(2)}, u32[]{:S(2)}) %all-to-all-start) | async-done | bytes 10485792 | tf_op jit(solution)/shard_map/all_to_all | solution.py:26
  619.7 33.4 fusion.35
  662.1 35.6 %fusion.45 = (bf16[80,8,4,1024]{3,1,0,2:T(8,128)(2,1)}, f32[4,80,8,1024]{3,2,1,0:T(8,128)}) fusion(f32[4,80,8,1024]{3,2,1,0:T(8,128)} %fusion.35, bf16[4,2048,1024]{2,1,0:T(8,128)(2,1)} %all-gather.30.cloned.1.call-done, bf16[80,8,4,2048]{3,0,2,1:T(8,128)(2,1)} %bitcast.9), kind=kOutput, calls=%fused_computation.74 | convolution fusion | flops 10753146880 | bytes 53477376 | tf_op jit(solution)/shard_map/wsed,edh->wseh/dot_general | solution.py:196
  697.7 123.7 %all-gather.32.cloned.1.call-done = bf16[4,1024,2048]{2,1,0:T(8,128)(2,1)} async-done(((bf16[4,256,2048]{2,1,0:T(8,128)(2,1)}), bf16[4,1024,2048]{2,1,0:T(8,128)(2,1)}) %all-gather.32.cloned.1.call-update) | async-done | bytes 16777232 | tf_op jit(solution)/shard_map/all_gather | solution.py:190
  872.7 458.5 %all_gather.61 = bf16[2048,32]{0,1:T(8,128)(2,1)S(1)} all-gather(bf16[256,32]{0,1:T(8,128)(2,1)S(1)} %copy-done.66), channel_id=1, replica_groups=mesh['fsdp'=8,'tp'=4] {'fsdp'}, dimensions={0}, use_global_device_ids=true | all-gather | bytes 147456 | tf_op jit(solution)/shard_map/all_gather | solution.py:88
  1412.1 65.7 %gather_fusion.2 = f32[8192]{0:T(1024)S(1)} fusion(f32[1024,32]{0,1:T(8,128)S(1)} %get-tuple-element.297, s32[8192]{0:T(1024)S(1)} %reshape.430), kind=kCustom, calls=%fused_computation.2 | custom fusion | bytes 131072 | tf_op jit(solution)/shard_map/jit(take_along_axis)/gather | solution.py:160
  1478.8 30.6 scatter_custom_fusion.1
  1529.2 233.0 %all_to_all.20 = bf16[80,32,2048]{2,0,1:T(8,128)(2,1)} all-to-all(bf16[80,32,2048]{2,0,1:T(8,128)(2,1)S(1)} %multiply_convert_fusion.1), channel_id=1, replica_groups=mesh['fsdp'=8,'tp'=4] {'fsdp'}, dimensions={1} | all-to-all | bytes 20971520 | tf_op jit(solution)/shard_map/all_to_all | solution.py:26
  1762.3 33.8 %fusion.43 = (bf16[80,8,4,1024]{3,1,0,2:T(8,128)(2,1)}, bf16[80,8,4,1024]{3,1,0,2:T(8,128)(2,1)}) fusion(f32[4,80,8,1024]{3,2,1,0:T(8,128)} %get-tuple-element.333, f32[4,80,8,1024]{3,2,1,0:T(8,128)} %fusion.35, bf16[4,1024,2048]{2,1,0:T(8,128)(2,1)} %all-gather.32.cloned.1.call-done, bf16[80,8,4,2048]{3,0,2,1:T(8,128)(2,1)} %bitcast.269), kind=kOutput, calls=%fused_computation.71 | convolution fusion | flops 10771496960 | bytes 58720256 | tf_op jit(solution)/shard_map/wsed,ehd->wseh/dot_general | solution.py:223
  1815.7 24.4 add_bitcast_fusion
  1858.6 458.6 %all_to_all.21 = f32[80,32,2048]{2,0,1:T(8,128)} all-to-all(f32[80,32,2048]{2,0,1:T(8,128)S(1)} %bitcast.264), channel_id=1, replica_groups=mesh['fsdp'=8,'tp'=4] {'fsdp'}, dimensions={1} | all-to-all | bytes 41943040 | tf_op jit(solution)/shard_map/all_to_all | solution.py:30
  2338.6 37.1 %scatter_custom_fusion.3 = f32[1025,2048]{1,0:T(8,128)} fusion(s32[2560]{0:T(1024)} %get-tuple-element.323, f32[2560,2048]{1,0:T(8,128)} %bitcast.268, f32[]{:T(128)} %constant.88.clone.1), kind=kCustom, calls=%fused_computation.91 | custom fusion | flops 5242880 | bytes 8397312 | tf_op jit(solution)/shard_map/scatter-add | solution.py:270
  2384.0 83.8 %reduce-scatter.17.cloned.1.call-done = f32[256,2048]{1,0:T(8,128)} async-done(((f32[1024,2048]{1,0:T(8,128)}), f32[256,2048]{1,0:T(8,128)}) %reduce-scatter.17.cloned.1.call-update) | async-done | bytes 2097168 | tf_op jit(solution)/shard_map/reduce_scatter | solution.py:18
  2473.0 33.7 %bitcast_convert_fusion = bf16[4,1024,2048]{2,1,0:T(8,128)(2,1)} fusion(bf16[80,8,4,1024]{3,1,0,2:T(8,128)(2,1)} %get-tuple-element.332, bf16[80,8,4,2048]{3,0,2,1:T(8,128)(2,1)} %bitcast.270), kind=kOutput, calls=%fused_computation.48 | convolution fusion | flops 10745806848 | bytes 32505856 | tf_op jit(solution)/shard_map/wseh,wsed->ehd/dot_general | solution.py:226
  2559.0 68.8 %while.31 = (s32[]{:T(128)}, f32[1024,4,128]{0,2,1:T(8,128)S(1)}, f32[1024,4,128]{0,2,1:T(8,128)}, f32[2,512,4,128]{3,1,2,0:T(8,128)}, s32[2]{0:T(128)S(1)}, /*i...) while((s32[]{:T(128)}, f32[1024,4,128]{0,2,1:T(8,128)S(1)}, ...), condition=%wide.region_28.29_spmd.clone.clone, body=%wide.region_26.28_spmd.clone.sunk.clone | while | flops 2708732416 | bytes 183546784 | solution.py:318
  2736.5 37.7 %scatter_custom_fusion.2 = f32[1025,2048]{1,0:T(8,128)} fusion(s32[2560]{0:T(1024)} %get-tuple-element.323, f32[2560,2048]{1,0:T(8,128)} %bitcast_multiply_fusion, f32[]{:T(128)} %constant.88.clone.1), kind=kCustom, calls=%fused_computation.93 | custom fusion | flops 5242880 | bytes 8397312 | tf_op jit(solution)/shard_map/scatter-add | solution.py:205
  2795.3 44.5 %reduce-scatter.31.cloned.1.call-done = bf16[4,2048,256]{2,1,0:T(8,128)(2,1)} async-done(((bf16[4,2048,1024]{2,1,0:T(8,128)(2,1)}), bf16[4,2048,256]{2,1,0:T(8,128)(2,1)}) %reduce-scatter.31.cloned.1.call-update) | async-done | bytes 4194320 | tf_op jit(solution)/shard_map/reduce_scatter | solution.py:249
  2846.1 150.4 %reduce-scatter.33.cloned.1.call-done = bf16[4,2048,256]{2,1,0:T(8,128)(2,1)} async-done(((bf16[4,2048,1024]{2,1,0:T(8,128)(2,1)}), bf16[4,2048,256]{2,1,0:T(8,128)(2,1)}) %reduce-scatter.33.cloned.1.call-update) | async-done | bytes 4194320 | tf_op jit(solution)/shard_map/reduce_scatter | solution.py:252
  3003.4 31.0 reduce-scatter.23.cloned.1.call-done
  3036.2 35.2 %reduce-scatter.21.cloned.1.call-done = bf16[256,512]{1,0:T(8,128)(2,1)} async-done(((bf16[2048,512]{1,0:T(8,128)(2,1)}), bf16[256,512]{1,0:T(8,128)(2,1)}) %reduce-scatter.21.cloned.1.call-update) | async-done | bytes 262160 | tf_op jit(solution)/shard_map/reduce_scatter | solution.py:375
  3073.3 35.0 %reduce-scatter.27.cloned.1.call-done = bf16[512,256]{1,0:T(8,128)(2,1)} async-done(((bf16[512,2048]{1,0:T(8,128)(2,1)}), bf16[512,256]{1,0:T(8,128)(2,1)}) %reduce-scatter.27.cloned.1.call-update) | async-done | bytes 262160 | tf_op jit(solution)/shard_map/reduce_scatter | solution.py:384
  3110.0 34.8 %reduce-scatter.25.cloned.1.call-done = bf16[256,512]{1,0:T(8,128)(2,1)} async-done(((bf16[2048,512]{1,0:T(8,128)(2,1)}), bf16[256,512]{1,0:T(8,128)(2,1)}) %reduce-scatter.25.cloned.1.call-update) | async-done | bytes 262160 | tf_op jit(solution)/shard_map/reduce_scatter | solution.py:381
  3146.6 86.4 %reduce-scatter.19.cloned.1.call-done = f32[256,2048]{1,0:T(8,128)} async-done(((f32[1024,2048]{1,0:T(8,128)}), f32[256,2048]{1,0:T(8,128)}) %reduce-scatter.19.cloned.1.call-update) | async-done | bytes 2097168 | tf_op jit(solution)/shard_map/reduce_scatter | solution.py:18
  3235.2 27.5 all-reduce.11
  3262.8 26.0 all-reduce.9
  3289.5 38.7 %reduce-scatter.15.cloned.1.call-done = f32[256,2048]{1,0:T(8,128)} async-done(((f32[1024,2048]{1,0:T(8,128)}), f32[256,2048]{1,0:T(8,128)}) %reduce-scatter.15.cloned.1.call-update) | async-done | bytes 2097168 | tf_op jit(solution)/shard_map/reduce_scatter | solution.py:18
  3336.1 24.5 reduce-scatter.29.cloned.1.call-done
  (433 shorter events, 737.8 us)
Async XLA Ops:
  7.2 44.8 %all-gather.18.cloned.1.call-start = ((), (), s32[]{:S(2)}) async-start(), calls=%async_computation.17 | async-start | bytes 2359296 | tf_op jit(solution)/shard_map/all_gather | solution.py:84
  7.9 88.3 %all-gather.16.cloned.1.call-start = ((), (), s32[]{:S(2)}) async-start(), calls=%async_computation.16 | async-start | bytes 5242880 | tf_op jit(solution)/shard_map/all_gather | solution.py:14
  26.7 100.2 %all-gather.20.cloned.1.call-start = ((), (), s32[]{:S(2)}) async-start(), calls=%async_computation.18 | async-start | bytes 2359296 | tf_op jit(solution)/shard_map/all_gather | solution.py:85
  27.4 129.6 %all-gather.22.cloned.1.call-start = ((), (), s32[]{:S(2)}) async-start(), calls=%async_computation.19 | async-start | bytes 2359296 | tf_op jit(solution)/shard_map/all_gather | solution.py:86
  28.0 164.3 %all-gather.24.cloned.1.call-start = ((), (), s32[]{:S(2)}) async-start(), calls=%async_computation.20 | async-start | bytes 2359296 | tf_op jit(solution)/shard_map/all_gather | solution.py:87
  28.6 257.5 %reduce-scatter.13.cloned.1.call-start = ((), (), s32[]{:S(2)}) async-start(), calls=%async_computation.21 | async-start | bytes 10485760 | tf_op jit(solution)/shard_map/reduce_scatter | solution.py:18
  200.1 143.4 %all-gather.26.cloned.1.call-start = ((), (), s32[]{:S(2)}) async-start(), calls=%async_computation.22 | async-start | bytes 5242880 | tf_op jit(solution)/shard_map/all_gather | solution.py:14
  290.7 212.1 %all-gather.28.cloned.1.call-start = ((), (), s32[]{:S(2)}) async-start(), calls=%async_computation.23 | async-start | bytes 20971520 | tf_op jit(solution)/shard_map/all_gather | solution.py:188
  291.4 370.7 %all-gather.30.cloned.1.call-start = ((), (), s32[]{:S(2)}) async-start(), calls=%async_computation.24 | async-start | bytes 20971520 | tf_op jit(solution)/shard_map/all_gather | solution.py:189
  292.2 529.2 %all-gather.32.cloned.1.call-start = ((), (), s32[]{:S(2)}) async-start(), calls=%async_computation.25 | async-start | bytes 20971520 | tf_op jit(solution)/shard_map/all_gather | solution.py:190
  385.5 234.2 %all-to-all-start = ((bf16[80,32,2048]{2,0,1:T(8,128)(2,1)}), bf16[80,32,2048]{2,0,1:T(8,128)(2,1)}, u32[]{:S(2)}, u32[]{:S(2)}) async-start(bf16[80,32,2048]{2,0,1:T(8,128)(2,1)} %copy.144), calls=%async_computation.1 | async-start | bytes 20971520 | tf_op jit(solution)/shard_map/all_to_all | solution.py:26
  865.1 466.0 %copy-start.71 = (s32[2]{0:T(128)S(1)}, s32[2]{0:T(128)}, u32[]{:S(2)}) copy-start(s32[2]{0:T(128)} %constant.167) | copy-start | bytes 28
  865.1 466.1 %copy-start.72 = (s32[2]{0:T(128)S(1)}, s32[2]{0:T(128)}, u32[]{:S(2)}) copy-start(s32[2]{0:T(128)} %constant.170) | copy-start | bytes 28
  865.1 511.4 %all-to-all-start.1 = ((f32[80,32,2048]{2,0,1:T(8,128)}), f32[80,32,2048]{2,0,1:T(8,128)}, u32[]{:S(2)}, u32[]{:S(2)}) async-start(f32[80,32,2048]{2,0,1:T(8,128)} %bitcast.263), calls=%async_computation.2 | async-start | bytes 41943040 | tf_op jit(solution)/shard_map/all_to_all | solution.py:30
  871.4 460.0 %all-gather.34.cloned.1.call-start = ((), (), s32[]{:S(2)}) async-start(), calls=%async_computation.27 | async-start | bytes 5242880 | tf_op jit(solution)/shard_map/all_gather | solution.py:14
  872.1 1595.7 %reduce-scatter.17.cloned.1.call-start = ((), (), s32[]{:S(2)}) async-start(), calls=%async_computation.28 | async-start | bytes 10485760 | tf_op jit(solution)/shard_map/reduce_scatter | solution.py:18
  1412.1 963.6 %copy-start = (f32[1024,32]{0,1:T(8,128)}, f32[1024,32]{0,1:T(8,128)S(1)}, u32[]{:S(2)}) copy-start(f32[1024,32]{0,1:T(8,128)S(1)} %get-tuple-element.297) | copy-start | bytes 393220
  2384.0 168.7 %all-gather.36.cloned.1.call-start = ((), (), s32[]{:S(2)}) async-start(), calls=%async_computation.29 | async-start | bytes 5242880 | tf_op jit(solution)/shard_map/all_gather | solution.py:14
  2472.9 315.7 %reduce-scatter.35.cloned.1.call-start = ((), (), s32[]{:S(2)}) async-start(), calls=%async_computation.38 | async-start | bytes 20971520 | tf_op jit(solution)/shard_map/reduce_scatter | solution.py:255
  2506.7 333.0 %reduce-scatter.31.cloned.1.call-start = ((), (), s32[]{:S(2)}) async-start(), calls=%async_computation.36 | async-start | bytes 20971520 | tf_op jit(solution)/shard_map/reduce_scatter | solution.py:249
  2528.8 467.6 %reduce-scatter.33.cloned.1.call-start = ((), (), s32[]{:S(2)}) async-start(), calls=%async_computation.37 | async-start | bytes 20971520 | tf_op jit(solution)/shard_map/reduce_scatter | solution.py:252
  2550.6 483.8 %reduce-scatter.23.cloned.1.call-start = ((), (), s32[]{:S(2)}) async-start(), calls=%async_computation.32 | async-start | bytes 2359296 | tf_op jit(solution)/shard_map/reduce_scatter | solution.py:378
  2675.4 396.1 %reduce-scatter.21.cloned.1.call-start = ((), (), s32[]{:S(2)}) async-start(), calls=%async_computation.31 | async-start | bytes 2359296 | tf_op jit(solution)/shard_map/reduce_scatter | solution.py:375
  2682.5 425.8 %reduce-scatter.27.cloned.1.call-start = ((), (), s32[]{:S(2)}) async-start(), calls=%async_computation.34 | async-start | bytes 2359296 | tf_op jit(solution)/shard_map/reduce_scatter | solution.py:384
  2688.5 456.3 %reduce-scatter.25.cloned.1.call-start = ((), (), s32[]{:S(2)}) async-start(), calls=%async_computation.33 | async-start | bytes 2359296 | tf_op jit(solution)/shard_map/reduce_scatter | solution.py:381
  2696.7 536.3 %reduce-scatter.19.cloned.1.call-start = ((), (), s32[]{:S(2)}) async-start(), calls=%async_computation.30 | async-start | bytes 10485760 | tf_op jit(solution)/shard_map/reduce_scatter | solution.py:18
  2709.1 619.1 %reduce-scatter.15.cloned.1.call-start = ((), (), s32[]{:S(2)}) async-start(), calls=%async_computation.26 | async-start | bytes 10485760 | tf_op jit(solution)/shard_map/reduce_scatter | solution.py:18
  2782.3 578.3 %reduce-scatter.29.cloned.1.call-start = ((), (), s32[]{:S(2)}) async-start(), calls=%async_computation.35 | async-start | bytes 147456 | tf_op jit(solution)/shard_map/reduce_scatter | solution.py:387
  2846.1 386.9 %copy-start.14 = (bf16[256,2048]{1,0:T(8,128)(2,1)S(1)}, bf16[256,2048]{1,0:T(8,128)(2,1)}, u32[]{:S(2)}) copy-start(bf16[256,2048]{1,0:T(8,128)(2,1)} %param.19) | copy-start | bytes 3145732
  2846.1 386.9 %copy-start.44 = (f32[8,1,256]{2,1,0:T(1,128)S(1)}, f32[8,1,256]{2,1,0:T(1,128)}, u32[]{:S(2)}) copy-start(f32[8,1,256]{2,1,0:T(1,128)} %copy-done.43) | copy-start | bytes 24580
  2846.1 386.9 %copy-start.65 = (f32[256]{0:T(256)S(1)}, f32[256]{0:T(256)}, u32[]{:S(2)}) copy-start(f32[256]{0:T(256)} %copy-done.64) | copy-start | bytes 3076
  3002.8 325.4 %copy-start.63 = (f32[256]{0:T(256)S(1)}, f32[256]{0:T(256)}, u32[]{:S(2)}) copy-start(f32[256]{0:T(256)} %copy-done.61) | copy-start | bytes 3076
  (84 other events, 2562.0 us)
Sparse Core Ops, SparseCore 0:
  9.6 31.8 all-gather.17
  44.0 52.1 all-gather.15
  97.8 29.0 all-gather.19
  128.4 28.5 all-gather.21
  158.4 30.3 all-gather.23
  200.2 85.8 reduce-scatter.12
  290.8 52.6 all-gather.25
  345.5 157.2 all-gather.27
  504.8 157.2 all-gather.29
  663.9 157.4 all-gather.31
  874.2 53.0 all-gather.33
  2384.1 83.6 reduce-scatter.16
  2473.0 52.6 all-gather.35
  2528.7 154.2 reduce-scatter.34
  2685.9 153.7 reduce-scatter.30
  2842.7 153.7 reduce-scatter.32
  2998.6 35.7 reduce-scatter.22
  3037.1 34.2 reduce-scatter.20
  3073.8 34.4 reduce-scatter.26
  3110.4 34.3 reduce-scatter.24
  3147.9 85.0 reduce-scatter.18
  3236.3 91.8 reduce-scatter.14
  3330.5 30.1 reduce-scatter.28
where the time goes:
time: 3380 us; the launch traced here: 3370 us
  blocking collectives  1270 us (38%)
  waiting for transfers between devices  1080 us (32%)
  matrix products  386 us (11%)
  local copies, waits for them, and re-layouts  335 us (10%)
  other arithmetic  263 us (8%)
    all_to_all x1, blocking collectives, from_owners(): lax.all_to_all(operand, 'fsdp', split_axis=1, concat_axis=1, tiled=True)  459 us
    all_gather x1, blocking collectives, shards(): lax.all_gather(w_router, 'fsdp', axis=0, tiled=True)  458 us
    reduce_scatter x4, waiting for transfers between devices, scatter_partial(): return lax.psum_scatter(operand, 'tp', scatter_dimension=0, tiled=True)  284 us
    all_to_all x1, blocking collectives, to_owners(): lax.all_to_all(operand, 'fsdp', split_axis=1, concat_axis=1, tiled=True)  233 us
    reduce_scatter x1, waiting for transfers between devices, shards(): lax.psum_scatter(up_w_grad.astype(jnp.bfloat16), 'tp', scatter_dimension=...  150 us
    all_gather x1, waiting for transfers between devices, shards(): lax.all_gather(w_down, 'tp', axis=1, tiled=True)  124 us
    all_to_all x1, waiting for transfers between devices, to_owners(): lax.all_to_all(operand, 'fsdp', split_axis=1, concat_axis=1, tiled=True)  117 us
    all_gather x1, waiting for transfers between devices, shards(): lax.all_gather(w_gate, 'tp', axis=2, tiled=True)  112 us
  transfers between devices with their start and end apart: 25, of which 19 were waited for; matrix products, arithmetic and copies ran while one was open for 18% of the time, Pallas kernels for 0%

commit v1 on v0

v1 whole, which is shorter than its diff:
```python
import functools

import jax
import jax.numpy as jnp
from jax import lax
from jax.experimental import pallas as pl
from jax.experimental.pallas import tpu as pltpu
from jax.sharding import PartitionSpec as P

HEAD_DIM = 128
EPSILON = 1e-05
ROPE_BASE = 10000.0
F32 = jnp.float32
BF16 = jnp.bfloat16


def dot(a, b):
    return jnp.dot(a, b, preferred_element_type=F32)


def dot_nt(a, b):
    return lax.dot_general(a, b, (((1,), (1,)), ((), ())), preferred_element_type=F32)


def dot_tn(a, b):
    return lax.dot_general(a, b, (((0,), (0,)), ((), ())), preferred_element_type=F32)


def swap_core(operand):
    count = lax.axis_size("fsdp")
    return lax.ppermute(operand, "fsdp", [(i, i ^ 1) for i in range(count)])


def shift_node(operand, step):
    count = lax.axis_size("fsdp")
    nodes = count // 2
    if step % nodes == 0:
        return operand
    return lax.ppermute(
        operand, "fsdp", [(i, ((i // 2 + step) % nodes) * 2 + i % 2) for i in range(count)]
    )


def around_nodes(operand):
    count = lax.axis_size("fsdp") // 2
    pieces = []
    for step in range(1, count - 1):
        pieces.append(shift_node(pieces[-1] if pieces else operand, 1))
    if count > 1:
        pieces.append(shift_node(operand, -1))
    return pieces


def swap_tp(operand, mask):
    count = lax.axis_size("tp")
    return lax.ppermute(operand, "tp", [(i, i ^ mask) for i in range(count)])


def after(operand, *earlier):
    return lax.optimization_barrier((operand,) + earlier)[0]


def gather_halves(operand):
    if lax.axis_size("tp") != 4:
        return lax.all_gather(operand, "tp", axis=0, tiled=True)
    rows = operand.shape[0]
    half = rows // 2
    a, b = operand[:half], operand[half:]
    a1 = swap_tp(a, 1)
    b2 = swap_tp(b, 2)
    b1 = swap_tp(b, 1)
    a2 = swap_tp(a, 2)
    a3 = swap_tp(a1, 2)
    b3 = swap_tp(b2, 1)
    rank = lax.axis_index("tp")
    placed = jnp.zeros((4 * rows,) + operand.shape[1:], operand.dtype)
    for mask, part, offset in (
        (0, operand, 0),
        (1, a1, 0),
        (1, b1, half),
        (2, a2, 0),
        (2, b2, half),
        (3, a3, 0),
        (3, b3, half),
    ):
        placed = lax.dynamic_update_slice_in_dim(placed, part, (rank ^ mask) * rows + offset, 0)
    return placed


def plus(mine, other):
    return mine.astype(F32) + other.astype(F32)


def hop_one(operand, other=None):
    rows = operand.shape[0] // 4
    half = rows // 2
    rank = lax.axis_index("tp")

    def part(mask, offset):
        start = (rank ^ mask) * rows + offset
        mine = lax.dynamic_slice_in_dim(operand, start, half, 0)
        if other is None:
            return mine
        return plus(mine, lax.dynamic_slice_in_dim(other, start, half, 0))

    arrived = (
        swap_tp(part(3, 0).astype(BF16), 2),
        swap_tp(part(3, half).astype(BF16), 1),
        swap_tp(part(2, 0).astype(BF16), 2),
        swap_tp(part(1, half).astype(BF16), 1),
    )
    return part, half, arrived


def hop_two(part, half, arrived):
    a3, b3, _, _ = arrived
    return (
        swap_tp(plus(part(1, 0), a3).astype(BF16), 1),
        swap_tp(plus(part(2, half), b3).astype(BF16), 2),
    )


def hop_sum(part, half, arrived, last):
    _, _, a2, b1 = arrived
    ra = plus(plus(part(0, 0), a2), last[0])
    rb = plus(plus(part(0, half), b1), last[1])
    return jnp.concatenate([ra, rb], axis=0)


def scatter_halves(operand):
    if lax.axis_size("tp") != 4:
        return lax.psum_scatter(operand, "tp", scatter_dimension=0, tiled=True).astype(F32)
    first = hop_one(operand)
    return hop_sum(*first, hop_two(*first))


def gather_small(operand):
    count = lax.axis_size("fsdp")
    nodes = count // 2
    rank = lax.axis_index("fsdp")
    node, core = rank // 2, rank % 2
    other = swap_core(operand)
    pair = jnp.where(core == 0, jnp.stack([operand, other]), jnp.stack([other, operand]))
    around = [shift_node(pair, step) for step in range(nodes - 1, 0, -1)] + [pair]
    both = jnp.concatenate(around + around, axis=0)
    placed = lax.dynamic_slice_in_dim(both, 2 * (nodes - 1 - node), count, 0)
    return placed.transpose(1, 0, 2).reshape(operand.shape[0], -1)


def reduce_small(operand):
    count = lax.axis_size("fsdp")
    nodes = count // 2
    rank = lax.axis_index("fsdp")
    node, core = rank // 2, rank % 2
    blocks = operand.reshape(operand.shape[0], nodes, 2, -1).transpose(2, 1, 0, 3)
    mine = lax.dynamic_index_in_dim(blocks, core, 0, keepdims=False)
    mine = mine + swap_core(lax.dynamic_index_in_dim(blocks, 1 - core, 0, keepdims=False))
    total = lax.dynamic_index_in_dim(mine, node, 0, keepdims=False)
    for step in range(1, nodes):
        part = lax.dynamic_index_in_dim(mine, (node + step) % nodes, 0, keepdims=False)
        total = total + shift_node(part, step)
    return sum_tp(total)


def sum_tp(operand):
    if lax.axis_size("tp") != 4:
        return lax.psum(operand, "tp")
    return (operand + swap_tp(operand, 1)) + (swap_tp(operand, 2) + swap_tp(operand, 3))


def rope_tables(positions, columns):
    halfway = columns // 2
    frequency = ROPE_BASE ** (-2.0 * jnp.arange(halfway).astype(F32) / columns)
    angles = positions.astype(F32)[:, None] * frequency[None, :]
    angles = jnp.concatenate([angles, angles], axis=-1)
    return (jnp.cos(angles)[:, None, :], jnp.sin(angles)[:, None, :])


def rotate(tensor):
    halfway = tensor.shape[-1] // 2
    return jnp.concatenate([-tensor[..., halfway:], tensor[..., :halfway]], axis=-1)


def rotate_back(tensor):
    halfway = tensor.shape[-1] // 2
    return jnp.concatenate([tensor[..., halfway:], -tensor[..., :halfway]], axis=-1)


def norm_rows(tensor):
    row_scale = lax.rsqrt(jnp.mean(tensor * tensor, axis=-1, keepdims=True) + EPSILON)
    return (tensor * row_scale, row_scale)


def norm_back(normed, row_scale, grad_normed):
    return row_scale * (
        grad_normed - normed * jnp.mean(normed * grad_normed, axis=-1, keepdims=True)
    )


def expert_kernel(extra, experts, base, *refs):
    x_ref, z_ref, gate_w, up_w, down_w = refs[:5]
    back_ref, out_ref, dots_ref, hidden_ref, gate_grad_ref, up_grad_ref, copy_ref = refs[-7:]
    count, width, size = gate_w.shape
    x = x_ref[:, :width]
    copy_ref[0] = x
    ends = x_ref[:, width:].astype(F32)
    lane = lax.broadcasted_iota(jnp.int32, ends.shape, 1)
    dots = jnp.zeros(ends.shape, F32)
    for e in range(count):
        columns = slice(e * size, (e + 1) * size)
        number = base[0] + e
        gate = jnp.sum(
            jnp.where((lane == number) | (lane == number + experts), ends, 0.0),
            axis=1,
            keepdims=True,
        )
        gate_pre = dot(x, gate_w[e])
        up_pre = dot(x, up_w[e])
        down_grad = z_ref[:, columns].astype(F32)
        sigmoid_gate = 1.0 / (1.0 + jnp.exp(-gate_pre))
        activated = gate_pre * sigmoid_gate
        hidden = activated * up_pre
        hidden_ref[0, :, columns] = (hidden * gate).astype(BF16)
        dots = dots + jnp.where(
            lane == number, jnp.sum(hidden * down_grad, axis=1, keepdims=True), 0.0
        )
        hidden_grad = down_grad * gate
        gate_grad_ref[0, :, columns] = (
            hidden_grad * up_pre * sigmoid_gate * (1.0 + gate_pre * (1.0 - sigmoid_gate))
        ).astype(BF16)
        up_grad_ref[0, :, columns] = (hidden_grad * activated).astype(BF16)
    dots_ref[...] = dots
    tile = min(512, width)
    for start in range(0, width, tile):
        rows = slice(start, start + tile)
        back = jnp.zeros((x.shape[0], tile), F32)
        out = jnp.zeros((x.shape[0], tile), F32)
        for e in range(count):
            columns = slice(e * size, (e + 1) * size)
            back = back + dot_nt(gate_grad_ref[0, :, columns], gate_w[e, rows, :])
            back = back + dot_nt(up_grad_ref[0, :, columns], up_w[e, rows, :])
            out = out + dot(hidden_ref[0, :, columns], down_w[e, :, rows])
        back_ref[:, rows] = back.astype(BF16)
        out_ref[:, rows] = out.astype(BF16)


def expert_products(base, x, z, gate_w, up_w, down_w, slots, slot, kept, experts):
    rows, wide = x.shape
    count, width, size = gate_w.shape
    extra = wide - width
    block = min(512, rows)
    hidden = count * size

    def whole(array):
        return pl.BlockSpec(
            array.shape, lambda i, base: (0, 0, 0), pipeline_mode=pl.Buffered(1)
        )

    def by_rows(columns):
        return pl.BlockSpec((block, columns), lambda i, base: (i, 0))

    def in_slot(columns):
        return pl.BlockSpec((1, block, columns), lambda i, base: (slot, i, 0))

    kept_shapes = [
        jax.ShapeDtypeStruct((slots, rows, columns), BF16)
        for columns in (hidden, hidden, hidden, width)
    ]
    results = pl.pallas_call(
        functools.partial(expert_kernel, extra, experts),
        out_shape=[
            jax.ShapeDtypeStruct((rows, width), BF16),
            jax.ShapeDtypeStruct((rows, width), BF16),
            jax.ShapeDtypeStruct((rows, extra), F32),
        ]
        + kept_shapes,
        grid_spec=pltpu.PrefetchScalarGridSpec(
            num_scalar_prefetch=1,
            grid=(rows // block,),
            in_specs=[by_rows(wide), by_rows(hidden), whole(gate_w), whole(up_w), whole(down_w)]
            + [pl.BlockSpec(memory_space=pl.ANY)] * len(kept),
            out_specs=[by_rows(width), by_rows(width), by_rows(extra)]
            + [in_slot(columns) for columns in (hidden, hidden, hidden, width)],
        ),
        input_output_aliases={6 + i: 3 + i for i in range(len(kept))},
        cost_estimate=pl.CostEstimate(
            flops=10 * rows * width * hidden,
            bytes_accessed=6 * width * hidden + 2 * rows * (4 * width + 4 * hidden),
            transcendentals=rows * hidden,
        ),
        compiler_params=pltpu.CompilerParams(vmem_limit_bytes=60 * 1024 * 1024),
    )(base, x, z, gate_w, up_w, down_w, *kept)
    return results[0], results[1], results[2], tuple(results[3:])


def shards(
    tokens,
    cotangent,
    routes,
    gain_attn,
    w_query,
    w_key,
    w_value,
    gain_query,
    gain_key,
    w_out,
    gain_moe,
    w_router,
    w_gate,
    w_up,
    w_down,
):
    tp_count = lax.axis_size("tp")
    tp_rank = lax.axis_index("tp")
    fsdp_count = lax.axis_size("fsdp")
    fsdp_rank = lax.axis_index("fsdp")
    nodes = fsdp_count // 2
    piece, model_width = tokens.shape
    seq_len = piece * tp_count
    local_width = w_query.shape[1]
    head_count = local_width // HEAD_DIM
    expert_count = w_router.shape[1]
    local_experts, _, hidden_slice = w_gate.shape
    hidden_all = local_experts * hidden_slice
    extra = -(-2 * expert_count // 128) * 128
    scale_factor = HEAD_DIM ** (-0.5)
    head_shape = (seq_len, head_count, HEAD_DIM)
    column_start = tp_rank * local_width

    small = gather_small(
        jnp.concatenate(
            [gain_attn[None], gain_moe[None], gain_query[None], gain_key[None], w_router.T], axis=0
        )
    )
    attn_gain, moe_gain = small[0].astype(F32), small[1].astype(F32)
    local_gains = lax.dynamic_slice_in_dim(small[2:4], column_start, local_width, 1).astype(F32)
    local_qgain, local_kgain = local_gains[0], local_gains[1]
    router_w = small[4:]
    qkv_w = lax.all_gather(
        jnp.concatenate([w_query, w_key, w_value], axis=1), "fsdp", axis=0, tiled=True
    )

    down_w = w_down.reshape(hidden_all, model_width)

    residual_in = tokens.astype(F32)
    normed_one, scale_one = norm_rows(residual_in)
    first_in = (normed_one * attn_gain).astype(BF16)
    first_all = gather_halves(first_in)

    early = after(cotangent, qkv_w, first_all)
    grad_own = lax.all_gather(early, "tp", axis=0, tiled=True)
    out_w = lax.all_gather(after(w_out, first_all), "fsdp", axis=1, tiled=True)
    around = around_nodes(early)
    near, far = around[:1] + around[2:], around[1:2]

    qkv_raw = dot(first_all, qkv_w)
    query_raw = qkv_raw[:, :local_width]
    key_raw = qkv_raw[:, local_width : 2 * local_width]
    value_raw = qkv_raw[:, 2 * local_width :]
    squares = sum_tp(
        jnp.stack([jnp.sum(query_raw * query_raw, axis=-1), jnp.sum(key_raw * key_raw, axis=-1)])
    )
    query_scale = lax.rsqrt(squares[0] / model_width + EPSILON)[:, None]
    key_scale = lax.rsqrt(squares[1] / model_width + EPSILON)[:, None]
    positions = jnp.arange(seq_len, dtype=jnp.int32)
    cosine, sine_table = rope_tables(positions, HEAD_DIM)
    query_normed = (query_raw * query_scale * local_qgain).reshape(head_shape)
    key_normed = (key_raw * key_scale * local_kgain).reshape(head_shape)
    query_bf = (query_normed * cosine + rotate(query_normed) * sine_table).astype(BF16)
    key_bf = (key_normed * cosine + rotate(key_normed) * sine_table).astype(BF16)
    value_bf = value_raw.astype(BF16).reshape(head_shape)
    block_rows = min(512, seq_len)
    block_count = seq_len // block_rows

    def block_of(array, block_index):
        return array[block_index * block_rows : (block_index + 1) * block_rows]

    def block_scores(block_index):
        query_block = block_of(query_bf, block_index)
        scores = (
            jnp.einsum("qhd,khd->hqk", query_block, key_bf, preferred_element_type=F32)
            * scale_factor
        )
        causal = block_of(positions, block_index)[:, None] >= positions[None, :]
        return (query_block, jnp.where(causal[None], scores, -1e30), causal)

    attn_blocks, log_totals = [], []
    for block_index in range(block_count):
        query_block, scores, causal = block_scores(block_index)
        if block_index > 0:
            scores = after(scores, near[0])
        top_score = jnp.max(scores, axis=-1, keepdims=True)
        exponent = jnp.exp(scores - top_score)
        row_total = jnp.sum(exponent, axis=-1, keepdims=True)
        attn_probs = (exponent / row_total).astype(BF16)
        attn_blocks.append(
            jnp.einsum("hqk,khd->qhd", attn_probs, value_bf, preferred_element_type=F32)
        )
        log_totals.append(top_score[..., 0] + jnp.log(row_total[..., 0]))
    heads_out = jnp.concatenate(attn_blocks, axis=0).reshape(seq_len, local_width).astype(BF16)
    heads_out = after(heads_out, *near)
    attn_sum = scatter_halves(dot(heads_out, out_w).astype(BF16))
    hidden_res = residual_in + after(attn_sum, *far)
    normed_two, scale_two = norm_rows(hidden_res)
    second_in = (normed_two * moe_gain).astype(BF16)

    router_probs = jax.nn.softmax(dot_nt(second_in, router_w), axis=-1)
    own_routes = lax.dynamic_slice_in_dim(routes, tp_rank * piece, piece, 0)
    routed = jnp.any(
        own_routes[:, :, None] == jnp.arange(expert_count, dtype=jnp.int32)[None, None, :], axis=1
    ).astype(F32)
    gates = router_probs * routed
    gates_high = gates.astype(BF16)
    gates_low = (gates - gates_high.astype(F32)).astype(BF16)
    sent = jnp.concatenate(
        [
            second_in,
            gates_high,
            gates_low,
            jnp.zeros((piece, extra - 2 * expert_count), BF16),
        ],
        axis=1,
    )

    grad_around = lax.all_gather(jnp.stack(around), "tp", axis=1, tiled=True)
    grad_sets = [grad_own, grad_around, swap_core(grad_own), swap_core(grad_around)]
    down_grads = [
        dot_nt(one.reshape(-1, model_width), down_w).astype(BF16).reshape(-1, seq_len, hidden_all)
        for one in grad_sets
    ]
    sources = around_nodes(sent)
    owns = [gather_halves(sent)]
    for source in sources:
        owns.append(lax.all_gather(source, "tp", axis=0, tiled=True))
    defer = nodes <= 4
    by_hops = tp_count == 4
    kept, gate_dots, backs, swaps, hops, lasts, returns = (), [], [], [], [], [], []
    outs, outs_back = [], []
    base = jnp.reshape(fsdp_rank * local_experts, (1,)).astype(jnp.int32)

    def one_sequence(step, other, rows):
        nonlocal kept
        grads = down_grads[(1 if step > 0 else 0) + (2 if other else 0)]
        back, out, dots, kept = expert_products(
            base,
            rows,
            grads[max(step - 1, 0)],
            w_gate,
            w_up,
            w_down,
            2 * nodes,
            step + (nodes if other else 0),
            kept,
            expert_count,
        )
        return back, out, dots[:, :expert_count]

    def outputs_home(outs, steps):
        outs = jnp.stack([plus(own, swap_core(other)).astype(BF16) for own, other in outs])
        outs = lax.psum_scatter(outs, "tp", scatter_dimension=1, tiled=True)
        return [shift_node(outs[i], -step) for i, step in enumerate(steps)]

    for step in range(nodes):
        own = owns[step]
        other = swap_core(own)
        if by_hops and step > 1:
            own = after(own, *hops[step - 2][2])
            other = after(other, *lasts[step - 2])
        if step == 0:
            first = one_sequence(step, False, after(own, *sources))
            second = one_sequence(step, True, after(other, grad_around))
            mine, others = first, second
        else:
            if by_hops:
                own = after(own, *hops[step - 1][2])
            first = one_sequence(step, True, other)
            second = one_sequence(step, False, own)
            mine, others = second, first
        if step + 1 < nodes:
            owns[step + 1] = after(owns[step + 1], first[0])
        gate_dots.append((mine[2], others[2]))
        backs.append(mine[0])
        swaps.append(swap_core(others[0]))
        outs.append((mine[1], others[1]))
        if by_hops:
            hops.append(hop_one(mine[0], swaps[-1]))
            lasts.append(hop_two(*hops[-1]))
            returns.append(shift_node(hop_sum(*hops[-1], lasts[-1]).astype(BF16), -step))
        else:
            back_own = plus(mine[0], swaps[-1]).astype(BF16)
            total = lax.psum_scatter(back_own, "tp", scatter_dimension=0, tiled=True)
            returns.append(shift_node(total, -step))
        if not defer:
            outs_back += outputs_home(outs, [step])
            outs = []
            kept = after(kept, outs_back[-1], returns[-1])
    if defer:
        late = owns[-1]
        for steps in ([1, 2], [0, 3]) if nodes == 4 else [list(range(nodes))]:
            outs_back += outputs_home([after(outs[step], late) for step in steps], steps)
    hidden_kept, gate_kept, up_kept, rows_kept = kept

    def down_product(index, *earlier):
        grads = grad_sets[index].reshape(-1, model_width)
        start = (0, 1, nodes, nodes + 1)[index]
        count = grads.shape[0] // seq_len
        hidden = hidden_kept[start : start + count].reshape(-1, hidden_all)
        return dot_tn(after(hidden, *earlier), grads)

    down_w_grad = down_product(0) + down_product(1)
    pins = hops[-1][2] if by_hops else ()
    down_w_grad = down_w_grad + (down_product(2, *pins) + down_product(3, *pins))
    if by_hops and nodes > 1:
        returns[-1] = after(returns[-1], down_w_grad)

    def wide_product(grads, *earlier):
        rows = rows_kept.reshape(-1, model_width)
        grads = after(grads, *earlier).reshape(-1, hidden_all)
        return dot_tn(rows, grads).reshape(
            model_width, local_experts, hidden_slice
        ).transpose(1, 0, 2)

    back_sum = sum(one.astype(F32) for one in returns)
    output = (hidden_res + sum(one.astype(F32) for one in outs_back)).astype(BF16)

    node, core = fsdp_rank // 2, fsdp_rank % 2
    blocks = []
    for mine, others in gate_dots:
        blocks.append(
            jnp.where(core == 0, jnp.stack([mine.T, others.T], 1), jnp.stack([others.T, mine.T], 1))
        )
    blocks = jnp.stack(blocks[::-1] + blocks[::-1], axis=1)
    blocks = lax.dynamic_slice_in_dim(blocks, nodes - 1 - node, nodes, 1)
    prob_grad = lax.psum_scatter(
        blocks.reshape(expert_count, fsdp_count * seq_len),
        ("fsdp", "tp"),
        scatter_dimension=1,
        tiled=True,
    ).T

    grad_out = cotangent.astype(F32)
    prob_grad = prob_grad * routed
    logit_grad = router_probs * (
        prob_grad - jnp.sum(router_probs * prob_grad, axis=-1, keepdims=True)
    )
    router_grad = lax.dot_general(
        logit_grad,
        second_in.astype(F32),
        (((0,), (0,)), ((), ())),
        precision=lax.Precision.HIGHEST,
    )
    second_grad = back_sum + jnp.dot(
        logit_grad, router_w.astype(F32), precision=lax.Precision.HIGHEST
    )
    moe_gain_grad = jnp.sum(normed_two * second_grad, axis=0)
    residual_grad = grad_out + norm_back(normed_two, scale_two, second_grad * moe_gain)

    residual_all = gather_halves(residual_grad.astype(BF16))

    gate_w_grad = wide_product(gate_kept, *returns[1:])
    residual_all = after(residual_all, gate_w_grad)

    out_w_grad = dot_tn(heads_out, residual_all)
    heads_grad = dot_nt(residual_all, out_w).astype(BF16).reshape(head_shape)
    key_rot_grad = jnp.zeros(head_shape, F32)
    value_grad = jnp.zeros(head_shape, F32)
    query_blocks_grad = []
    for block_index in range(block_count):
        query_block, scores, causal = block_scores(block_index)
        log_block = log_totals[block_index]
        probs_full = jnp.where(causal[None], jnp.exp(scores - log_block[..., None]), 0.0)
        probs_bf = probs_full.astype(BF16)
        out_block = block_of(heads_grad, block_index)
        value_grad = value_grad + jnp.einsum(
            "hqk,qhd->khd", probs_bf, out_block, preferred_element_type=F32
        )
        prob_block_grad = jnp.einsum(
            "qhd,khd->hqk", out_block, value_bf, preferred_element_type=F32
        )
        centre = jnp.sum(probs_full * prob_block_grad, axis=-1, keepdims=True)
        score_grad = (probs_full * (prob_block_grad - centre)).astype(BF16)
        query_blocks_grad.append(
            jnp.einsum("hqk,khd->qhd", score_grad, key_bf, preferred_element_type=F32)
            * scale_factor
        )
        key_rot_grad = (
            key_rot_grad
            + jnp.einsum("hqk,qhd->khd", score_grad, query_block, preferred_element_type=F32)
            * scale_factor
        )
    query_rot_grad = jnp.concatenate(query_blocks_grad, axis=0)
    query_norm_grad = (query_rot_grad * cosine + rotate_back(query_rot_grad * sine_table)).reshape(
        seq_len, local_width
    )
    key_norm_grad = (key_rot_grad * cosine + rotate_back(key_rot_grad * sine_table)).reshape(
        seq_len, local_width
    )
    qgain_local = jnp.sum(query_raw * query_scale * query_norm_grad, axis=0)
    kgain_local = jnp.sum(key_raw * key_scale * key_norm_grad, axis=0)
    query_inner = query_norm_grad * local_qgain
    key_inner = key_norm_grad * local_kgain
    dots = sum_tp(
        jnp.stack(
            [jnp.sum(query_raw * query_inner, axis=-1), jnp.sum(key_raw * key_inner, axis=-1)]
        )
    )
    query_raw_grad = (
        query_scale * query_inner - query_raw * query_scale**3 * dots[0][:, None] / model_width
    ).astype(BF16)
    key_raw_grad = (
        key_scale * key_inner - key_raw * key_scale**3 * dots[1][:, None] / model_width
    ).astype(BF16)
    value_raw_grad = value_grad.reshape(seq_len, local_width).astype(BF16)
    qkv_grad = jnp.concatenate([query_raw_grad, key_raw_grad, value_raw_grad], axis=1)
    first_part = dot_nt(qkv_grad, qkv_w).astype(BF16)
    first_grad = scatter_halves(first_part)
    qkv_w_grad = dot_tn(first_all, qkv_grad).astype(BF16)
    up_w_grad = wide_product(up_kept, first_part, qkv_w_grad)
    down_w_grad = down_w_grad.reshape(local_experts, hidden_slice, model_width)

    attn_gain_grad = jnp.sum(normed_one * first_grad, axis=0)
    input_grad = residual_grad + norm_back(normed_one, scale_one, first_grad * attn_gain)

    def scatter_fsdp(grad, dimension):
        return lax.psum_scatter(
            grad.astype(BF16), "fsdp", scatter_dimension=dimension, tiled=True
        ).astype(F32)

    qkv_out = scatter_fsdp(qkv_w_grad, 0)
    out_w_out = scatter_fsdp(out_w_grad, 1)

    def widen(grad):
        return lax.dynamic_update_slice_in_dim(
            jnp.zeros((1, model_width), F32), grad[None], column_start, 1
        )

    early_out = reduce_small(jnp.concatenate([moe_gain_grad[None], router_grad], axis=0))
    late_out = reduce_small(
        jnp.concatenate(
            [attn_gain_grad[None], widen(qgain_local), widen(kgain_local)], axis=0
        )
    )
    return (
        output,
        input_grad,
        late_out[0],
        qkv_out[:, :local_width],
        qkv_out[:, local_width : 2 * local_width],
        qkv_out[:, 2 * local_width :],
        late_out[1],
        late_out[2],
        out_w_out,
        early_out[0],
        early_out[1:].T,
        gate_w_grad,
        up_w_grad,
        down_w_grad,
    )


def solution(mesh):
    placed = (
        P(("fsdp", "tp"), None),
        P(("fsdp", "tp"), None),
        P("fsdp", None),
        P("fsdp"),
        P("fsdp", "tp"),
        P("fsdp", "tp"),
        P("fsdp", "tp"),
        P("fsdp"),
        P("fsdp"),
        P("tp", "fsdp"),
        P("fsdp"),
        P("fsdp", None),
        P("fsdp", None, "tp"),
        P("fsdp", None, "tp"),
        P("fsdp", "tp", None),
    )
    return jax.shard_map(
        shards,
        mesh=mesh,
        in_specs=placed,
        out_specs=(
            P(("fsdp", "tp"), None),
            P(("fsdp", "tp"), None),
            P("fsdp"),
            P("fsdp", "tp"),
            P("fsdp", "tp"),
            P("fsdp", "tp"),
            P("fsdp"),
            P("fsdp"),
            P("tp", "fsdp"),
            P("fsdp"),
            P("fsdp", None),
            P("fsdp", None, "tp"),
            P("fsdp", None, "tp"),
            P("fsdp", "tp", None),
        ),
        check_vma=False,
    )
```

time: 3380 us -> 1510 us (0.45)
  blocking collectives: 1270 us -> 0 us
  waiting for transfers between devices: 1080 us -> 515 us
  Pallas kernels: 0 us -> 260 us
  local copies, waits for them, and re-layouts: 335 us -> 140 us
  starting transfers between devices: 12.9 us -> 117 us
  other arithmetic: 263 us -> 161 us
  matrix products: 386 us -> 297 us
    all_to_all x2 -> x0, blocking collectives: 692 us -> none  [the longest x1 459 us: from_owners(): lax.all_to_all(operand, 'fsdp', split_axis=1, concat_axis=1, tiled=True)]
    reduce_scatter x12 -> x5, waiting for transfers between devices: 640 us -> 75.1 us  [the longest x1 52.9 us: shards(): lax.psum_scatter(blocks.reshape(expert_count, fsdp_count * seq_len), ('fs...]
    all_gather x5 -> x0, blocking collectives: 501 us -> none  [the longest x1 458 us: shards(): lax.all_gather(w_router, 'fsdp', axis=0, tiled=True)]
    ppermute x0 -> x104, waiting for transfers between devices: none -> 428 us  [the longest x66 253 us: swap_tp(): return lax.ppermute(operand, 'tp', [(i, i ^ mask) for i in range(count)])]
    all_gather x11 -> x7, waiting for transfers between devices: 321 us -> 11.7 us  [the longest x1 11.6 us: shards(): lax.all_gather(jnp.concatenate([w_query, w_key, w_value], axis=1), 'fsdp'...]
    pallas_call x0 -> x8, Pallas kernels: none -> 260 us  [expert_products(): pl.pallas_call(functools.partial(expert_kernel, extra, experts), out_shap...]
    all_to_all x2 -> x0, waiting for transfers between devices: 117 us -> none  [the longest x1 117 us: to_owners(): lax.all_to_all(operand, 'fsdp', split_axis=1, concat_axis=1, tiled=True)]
    ppermute x0 -> x104, starting transfers between devices: none -> 116 us  [the longest x66 77.7 us: swap_tp(): return lax.ppermute(operand, 'tp', [(i, i ^ mask) for i in range(count)])]
  transfers between devices with their start and end apart: 25 -> 116, of which waited for: 19 -> 47; matrix products, arithmetic and copies ran while one was open for 18% -> 38% of each run, Pallas kernels for 0% -> 17%
where the time goes in v1:
time: 1510 us
  waiting for transfers between devices  515 us (34%)
  matrix products  297 us (20%)
  Pallas kernels  260 us (17%)
  other arithmetic  161 us (11%)
  local copies, waits for them, and re-layouts  140 us (9%)
  starting transfers between devices  117 us (8%)
  between operations  17.3 us (1%)
    pallas_call x8, Pallas kernels, expert_products(): pl.pallas_call(functools.partial(expert_kernel, extra, experts), out_shap...  260 us
    ppermute x66, waiting for transfers between devices, swap_tp(): return lax.ppermute(operand, 'tp', [(i, i ^ mask) for i in range(count)])  253 us
    ppermute x21, waiting for transfers between devices, shift_node(): lax.ppermute(operand, 'fsdp', [(i, (i // 2 + step) % nodes * 2 + i % 2) f...  165 us
    dot_general x8, matrix products, dot_tn(): lax.dot_general(a, b, (((0,), (0,)), ((), ())), preferred_element_type=F32)  160 us
    ppermute x66, starting transfers between devices, swap_tp(): return lax.ppermute(operand, 'tp', [(i, i ^ mask) for i in range(count)])  77.7 us
    dot_general x7, matrix products, dot_nt(): lax.dot_general(a, b, (((1,), (1,)), ((), ())), preferred_element_type=F32)  67.2 us
    reduce_scatter x1, waiting for transfers between devices, shards(): lax.psum_scatter(blocks.reshape(expert_count, fsdp_count * seq_len), ('fs...  52.9 us
    dot_general x2, local copies, waits for them, and re-layouts, dot_tn(): lax.dot_general(a, b, (((0,), (0,)), ((), ())), preferred_element_type=F32)  42.3 us
  transfers between devices with their start and end apart: 116, of which 47 were waited for; matrix products, arithmetic and copies ran while one was open for 38% of the time, Pallas kernels for 17%

profile of v1, /device:TPU:0, one launch (start us, length us, event | category | flops | bytes accessed | tf_op | source)
XLA Modules:
  0.0 1507.3 jit_solution(11179938289192013021)
XLA Ops:
  83.0 39.1 %collective-permute-done.13 = bf16[256,2048]{1,0:T(8,128)(2,1)S(1)} collective-permute-done((bf16[256,2048]{1,0:T(8,128)(2,1)S(1)}, bf16[256,2048]{1,0:T(8,128)(2,1)S(1)}, u32[]{:S(2)}, u32[]{:S(2)}) %collective-permute-start.13) | collective-permute-done | bytes 1048608 | tf_op jit(solution)/shard_map/ppermute | solution.py:39
  126.0 17.9 %collective-permute-done.14 = bf16[256,2048]{1,0:T(8,128)(2,1)S(1)} collective-permute-done((bf16[256,2048]{1,0:T(8,128)(2,1)S(1)}, bf16[256,2048]{1,0:T(8,128)(2,1)S(1)}, u32[]{:S(2)}, u32[]{:S(2)}) %collective-permute-start.14) | collective-permute-done | bytes 1048608 | tf_op jit(solution)/shard_map/ppermute | solution.py:39
  143.9 24.2 %collective-permute-done.21 = bf16[256,2048]{1,0:T(8,128)(2,1)S(1)} collective-permute-done((bf16[256,2048]{1,0:T(8,128)(2,1)S(1)}, bf16[256,2048]{1,0:T(8,128)(2,1)S(1)}, u32[]{:S(2)}, u32[]{:S(2)}) %collective-permute-start.21) | collective-permute-done | bytes 1048608 | tf_op jit(solution)/shard_map/ppermute | solution.py:39
  238.3 22.5 %collective-permute-done.16 = bf16[128,2048]{1,0:T(8,128)(2,1)S(1)} collective-permute-done((bf16[128,2048]{1,0:T(8,128)(2,1)S(1)}, bf16[128,2048]{1,0:T(8,128)(2,1)S(1)}, u32[]{:S(2)}, u32[]{:S(2)}) %collective-permute-start.16) | collective-permute-done | bytes 524320 | tf_op jit(solution)/shard_map/ppermute | solution.py:56
  278.3 14.8 collective-permute-done.18
  307.3 21.2 %collective-permute-done.22 = bf16[256,2176]{1,0:T(8,128)(2,1)} collective-permute-done((bf16[256,2176]{1,0:T(8,128)(2,1)S(1)}, bf16[256,2176]{1,0:T(8,128)(2,1)}, u32[]{:S(2)}, u32[]{:S(2)}) %collective-permute-start.22) | collective-permute-done | bytes 1114144 | tf_op jit(solution)/shard_map/ppermute | solution.py:39
  338.1 18.2 %collective-permute-done.26 = bf16[128,2176]{1,0:T(8,128)(2,1)} collective-permute-done((bf16[128,2176]{1,0:T(8,128)(2,1)S(1)}, bf16[128,2176]{1,0:T(8,128)(2,1)}, u32[]{:S(2)}, u32[]{:S(2)}) %collective-permute-start.26) | collective-permute-done | bytes 557088 | tf_op jit(solution)/shard_map/ppermute | solution.py:56
  360.4 19.0 %collective-permute-done.24 = bf16[128,2176]{1,0:T(8,128)(2,1)S(1)} collective-permute-done((bf16[128,2176]{1,0:T(8,128)(2,1)S(1)}, bf16[128,2176]{1,0:T(8,128)(2,1)S(1)}, u32[]{:S(2)}, u32[]{:S(2)}) %collective-permute-start.24) | collective-permute-done | bytes 557088 | tf_op jit(solution)/shard_map/ppermute | solution.py:56
  410.7 32.4 %shard_map.254 = (bf16[1024,2048]{1,0:T(8,128)(2,1)}, bf16[1024,2048]{1,0:T(8,128)(2,1)}, f32[1024,128]{1,0:T(8,128)}, bf16[8,1024,1024]{2,1,0:T(8,128)(2,1)}, b...) custom-call(s32[1]{0:T(128)} %bitcast.15.base, ...), custom_call_target="tpu_custom_call" | custom-call | flops 21474836480 | bytes 37748736 | tf_op jit(solution)/shard_map/pallas_call | solution.py:269
  452.4 33.2 %shard_map.255 = (bf16[1024,2048]{1,0:T(8,128)(2,1)}, bf16[1024,2048]{1,0:T(8,128)(2,1)}, f32[1024,128]{1,0:T(8,128)}, bf16[8,1024,1024]{2,1,0:T(8,128)(2,1)}, b...) custom-call(s32[1]{0:T(128)} %bitcast.15.base, ...), custom_call_target="tpu_custom_call", output_to_operand_aliasing={{3}: (6, {}), {4}: (7, {}), {5}: (8, {}), {6}: (9, {})} | custom-call | flops 21474836480 | bytes 37748736 | tf_op jit(solution)/shard_map/pallas_call | solution.py:269
  500.0 12.3 collective-permute-done.35
  518.6 16.0 %convolution_convert_fusion.1 = bf16[3072,1024]{1,0:T(8,128)(2,1)S(1)} fusion(bf16[3072,2048]{1,0:T(8,128)(2,1)} %bitcast.22, bf16[1024,2048]{1,0:T(8,128)(2,1)S(1)} %bitcast.321), kind=kOutput, calls=%fused_computation.22 | convolution fusion | flops 12888047616 | bytes 23068672 | tf_op jit(solution)/shard_map/dot_general | solution.py:22
  537.5 32.2 %shard_map.256 = (bf16[1024,2048]{1,0:T(8,128)(2,1)}, bf16[1024,2048]{1,0:T(8,128)(2,1)}, f32[1024,128]{1,0:T(8,128)}, bf16[8,1024,1024]{2,1,0:T(8,128)(2,1)}, b...) custom-call(s32[1]{0:T(128)} %bitcast.15.base, ...), custom_call_target="tpu_custom_call", output_to_operand_aliasing={{3}: (6, {}), {4}: (7, {}), {5}: (8, {}), {6}: (9, {})} | custom-call | flops 21474836480 | bytes 37748736 | tf_op jit(solution)/shard_map/pallas_call | solution.py:269
  569.8 17.5 %convolution_convert_fusion.2 = bf16[3072,1024]{1,0:T(8,128)(2,1)S(1)} fusion(bf16[3072,2048]{1,0:T(8,128)(2,1)} %bitcast.401, bf16[1024,2048]{1,0:T(8,128)(2,1)} %bitcast.320), kind=kOutput, calls=%fused_computation.23 | convolution fusion | flops 12888047616 | bytes 23068672 | tf_op jit(solution)/shard_map/dot_general | solution.py:22
  592.8 32.5 %shard_map.257 = (bf16[1024,2048]{1,0:T(8,128)(2,1)}, bf16[1024,2048]{1,0:T(8,128)(2,1)}, f32[1024,128]{1,0:T(8,128)}, bf16[8,1024,1024]{2,1,0:T(8,128)(2,1)}, b...) custom-call(s32[1]{0:T(128)} %bitcast.15.base, ...), custom_call_target="tpu_custom_call", output_to_operand_aliasing={{3}: (6, {}), {4}: (7, {}), {5}: (8, {}), {6}: (9, {})} | custom-call | flops 21474836480 | bytes 37748736 | tf_op jit(solution)/shard_map/pallas_call | solution.py:269
  625.4 32.5 %shard_map.258 = (bf16[1024,2048]{1,0:T(8,128)(2,1)}, bf16[1024,2048]{1,0:T(8,128)(2,1)}, f32[1024,128]{1,0:T(8,128)}, bf16[8,1024,1024]{2,1,0:T(8,128)(2,1)}, b...) custom-call(s32[1]{0:T(128)} %bitcast.15.base, ...), custom_call_target="tpu_custom_call", output_to_operand_aliasing={{3}: (6, {}), {4}: (7, {}), {5}: (8, {}), {6}: (9, {})} | custom-call | flops 21474836480 | bytes 37748736 | tf_op jit(solution)/shard_map/pallas_call | solution.py:269
  661.7 12.5 collective-permute-done.46
  692.7 32.7 %shard_map.259 = (bf16[1024,2048]{1,0:T(8,128)(2,1)}, bf16[1024,2048]{1,0:T(8,128)(2,1)}, f32[1024,128]{1,0:T(8,128)}, bf16[8,1024,1024]{2,1,0:T(8,128)(2,1)}, b...) custom-call(s32[1]{0:T(128)} %bitcast.15.base, ...), custom_call_target="tpu_custom_call", output_to_operand_aliasing={{3}: (6, {}), {4}: (7, {}), {5}: (8, {}), {6}: (9, {})} | custom-call | flops 21474836480 | bytes 37748736 | tf_op jit(solution)/shard_map/pallas_call | solution.py:269
  770.5 32.6 %shard_map.260 = (bf16[1024,2048]{1,0:T(8,128)(2,1)}, bf16[1024,2048]{1,0:T(8,128)(2,1)}, f32[1024,128]{1,0:T(8,128)}, bf16[8,1024,1024]{2,1,0:T(8,128)(2,1)}, b...) custom-call(s32[1]{0:T(128)} %bitcast.15.base, ...), custom_call_target="tpu_custom_call", output_to_operand_aliasing={{3}: (6, {}), {4}: (7, {}), {5}: (8, {}), {6}: (9, {})} | custom-call | flops 21474836480 | bytes 37748736 | tf_op jit(solution)/shard_map/pallas_call | solution.py:269
  804.4 32.5 %shard_map.261 = (bf16[1024,2048]{1,0:T(8,128)(2,1)}, bf16[1024,2048]{1,0:T(8,128)(2,1)}, f32[1024,128]{1,0:T(8,128)}, bf16[8,1024,1024]{2,1,0:T(8,128)(2,1)}, b...) custom-call(s32[1]{0:T(128)} %bitcast.15.base, ...), custom_call_target="tpu_custom_call", output_to_operand_aliasing={{3}: (6, {}), {4}: (7, {}), {5}: (8, {}), {6}: (9, {})} | custom-call | flops 21474836480 | bytes 37748736 | tf_op jit(solution)/shard_map/pallas_call | solution.py:269
  910.7 16.2 %fusion.110 = f32[1024,2048]{1,0:T(8,128)} fusion(bf16[3072,1024]{1,0:T(8,128)(2,1)S(1)} %bitcast.333, bf16[3072,2048]{1,0:T(8,128)(2,1)S(1)} %bitcast.404), kind=kOutput, calls=%fused_computation.347 | convolution fusion | flops 12884901888 | bytes 27262976 | tf_op jit(solution)/shard_map/dot_general | solution.py:26
  942.0 52.9 %reduce-scatter.10.cloned.1.call-done = f32[32,256]{0,1:T(8,128)} async-done(((f32[32,8192]{0,1:T(8,128)}), f32[32,256]{0,1:T(8,128)}) %reduce-scatter.10.cloned.1.call-update) | async-done | bytes 32784 | tf_op jit(solution)/shard_map/reduce_scatter | solution.py:534
  1031.7 17.6 %collective-permute-done.71 = bf16[128,2048]{1,0:T(8,128)(2,1)} collective-permute-done((bf16[128,2048]{1,0:T(8,128)(2,1)S(1)}, bf16[128,2048]{1,0:T(8,128)(2,1)}, u32[]{:S(2)}, u32[]{:S(2)}) %collective-permute-start.71) | collective-permute-done | bytes 524320 | tf_op jit(solution)/shard_map/ppermute | solution.py:56
  1049.4 19.1 %fusion.111 = f32[1024,2048]{1,0:T(8,128)} fusion(bf16[3072,1024]{1,0:T(8,128)(2,1)} %bitcast.332, bf16[3072,2048]{1,0:T(8,128)(2,1)} %bitcast.22), kind=kOutput, calls=%fused_computation.348 | convolution fusion | flops 12884901888 | bytes 27262976 | tf_op jit(solution)/shard_map/dot_general | solution.py:26
  1070.6 15.3 %add_add_fusion = f32[1024,2048]{1,0:T(8,128)} fusion(f32[1024,2048]{1,0:T(8,128)} %fusion.111, f32[1024,2048]{1,0:T(8,128)} %fusion.109, f32[1024,2048]{1,0:T(8,128)} %fusion.110, bf16[1024,1024]{1,0:T(8,128)(2,1)S(1)} %copy-done.49, bf16[1024,2048]{1,0:T(8,128)(2,1)} %collective-permute-done.32), kind=kOutput, calls=%fused_computation.8 | convolution fusion | flops 4301258752 | bytes 39845888 | tf_op jit(solution)/shard_map/dot_general | solution.py:26
  1104.8 21.5 %copy.284 = bf16[1024,8192]{1,0:T(8,128)(2,1)} copy(bf16[1024,8192]{0,1:T(8,128)(2,1)} %bitcast.314) | data formatting | bytes 33554432 | tf_op jit(solution)/shard_map/dot_general | solution.py:26
  1126.3 44.3 %convolution_bitcast_fusion.1 = f32[4,2048,256]{2,1,0:T(8,128)} fusion(bf16[8192,2048,1]{1,0,2:T(8,128)(2,1)} %bitcast.312, bf16[4,256,8192]{2,1,0:T(8,128)(2,1)} %bitcast.330), kind=kOutput, calls=%fused_computation.27 | convolution fusion | flops 34359738368 | bytes 58720256 | tf_op jit(solution)/shard_map/dot_general | solution.py:26
  1177.5 13.7 collective-permute-done.79
  1345.0 20.8 %copy.306 = bf16[1024,8192]{1,0:T(8,128)(2,1)} copy(bf16[1024,8192]{0,1:T(8,128)(2,1)} %bitcast.315) | data formatting | bytes 33554432 | tf_op jit(solution)/shard_map/dot_general | solution.py:26
  1376.0 44.2 %convolution_bitcast_fusion = f32[4,2048,256]{2,1,0:T(8,128)} fusion(bf16[8192,2048,1]{1,0,2:T(8,128)(2,1)} %bitcast.313, bf16[4,256,8192]{2,1,0:T(8,128)(2,1)} %bitcast.329), kind=kOutput, calls=%fused_computation.26 | convolution fusion | flops 34359738368 | bytes 58720256 | tf_op jit(solution)/shard_map/dot_general | solution.py:26
  1427.7 22.1 %reduce-scatter.12.cloned.1.call-done = bf16[256,1536]{1,0:T(8,128)(2,1)} async-done(((bf16[2048,1536]{1,0:T(8,128)(2,1)}), bf16[256,1536]{1,0:T(8,128)(2,1)}) %reduce-scatter.12.cloned.1.call-update) | async-done | bytes 786448 | tf_op jit(solution)/shard_map/reduce_scatter | solution.py:625
  1452.2 42.2 %collective-permute-done.51 = bf16[256,2048]{1,0:T(8,128)(2,1)} collective-permute-done((bf16[256,2048]{1,0:T(8,128)(2,1)}, bf16[256,2048]{1,0:T(8,128)(2,1)}, u32[]{:S(2)}, u32[]{:S(2)}) %collective-permute-start.51) | collective-permute-done | bytes 1048608 | tf_op jit(solution)/shard_map/ppermute | solution.py:39
  (745 shorter events, 664.4 us)
Async XLA Ops:
  7.2 71.9 %all-gather.8.cloned.1.call-start = ((), (), s32[]{:S(2)}) async-start(), calls=%async_computation.5 | async-start | bytes 7077888 | tf_op jit(solution)/shard_map/all_gather | solution.py:339
  9.4 219.8 %all-gather.10.cloned.1.call-start = ((), (), s32[]{:S(2)}) async-start(), calls=%async_computation.6 | async-start | bytes 2359296 | tf_op jit(solution)/shard_map/all_gather | solution.py:352
  67.4 313.7 %all-gather.14.cloned.1.call-start = ((), (), s32[]{:S(2)}) async-start(), calls=%async_computation.8 | async-start | bytes 5242880 | tf_op jit(solution)/shard_map/all_gather | solution.py:351
  79.1 313.1 %all-gather.16.cloned.1.call-start = ((), (), s32[]{:S(2)}) async-start(), calls=%async_computation.9 | async-start | bytes 15728640 | tf_op jit(solution)/shard_map/all_gather | solution.py:425
  170.2 329.7 %all-gather.12.cloned.1.call-start = ((), (), s32[]{:S(2)}) async-start(), calls=%async_computation.7 | async-start | bytes 5570560 | tf_op jit(solution)/shard_map/all_gather | solution.py:434
  328.6 241.2 %all-gather.20.cloned.1.call-start = ((), (), s32[]{:S(2)}) async-start(), calls=%async_computation.11 | async-start | bytes 5570560 | tf_op jit(solution)/shard_map/all_gather | solution.py:434
  392.2 126.5 %collective-permute-start.39 = (bf16[3,1024,2048]{2,1,0:T(8,128)(2,1)}, bf16[3,1024,2048]{2,1,0:T(8,128)(2,1)}, u32[]{:S(2)}, u32[]{:S(2)}) collective-permute-start(bf16[3,1024,2048]{2,1,0:T(8,128)(2,1)} %all-gather.16.cloned.1.call-done), channel_id=1, source_target_pairs={{0,4},{4,0},{8,12},{12,8},{16,20},{20,16},{24,28},{28,24},{1,5},{5... | collective-permute-start | bytes 37748744 | tf_op jit(solution)/shard_map/ppermute | solution.py:31
  401.1 280.2 %all-gather.18.cloned.1.call-start = ((), (), s32[]{:S(2)}) async-start(), calls=%async_computation.10 | async-start | bytes 5570560 | tf_op jit(solution)/shard_map/all_gather | solution.py:434
  499.9 494.9 %reduce-scatter.10.cloned.1.call-start = ((), (), s32[]{:S(2)}) async-start(), calls=%async_computation.14 | async-start | bytes 4325376 | tf_op jit(solution)/shard_map/reduce_scatter | solution.py:534
  517.0 75.7 %collective-permute-start.37 = (bf16[128,2048]{1,0:T(8,128)(2,1)}, bf16[128,2048]{1,0:T(8,128)(2,1)S(1)}, u32[]{:S(2)}, u32[]{:S(2)}) collective-permute-start(bf16[128,2048]{1,0:T(8,128)(2,1)} %get-tuple-element.232), channel_id=1, source_target_pairs={{0,1},{1,0},{2,3},{3,2},{4,5},{5,4},{6,7},{7,6},{8,9},{9,8},{10,11... | collective-permute-start | bytes 1572872 | tf_op jit(solution)/shard_map/ppermute | solution.py:56
  518.5 74.3 %collective-permute-start.36 = (bf16[128,2048]{1,0:T(8,128)(2,1)S(1)}, bf16[128,2048]{1,0:T(8,128)(2,1)S(1)}, u32[]{:S(2)}, u32[]{:S(2)}) collective-permute-start(bf16[128,2048]{1,0:T(8,128)(2,1)S(1)} %get-tuple-element.235), channel_id=1, source_target_pairs={{0,2},{1,3},{2,0},{3,1},{4,6},{5,7},{6,4},{7,5},{8,10},{9,11},{10,... | collective-permute-start | bytes 1572872 | tf_op jit(solution)/shard_map/ppermute | solution.py:56
  592.7 65.4 %collective-permute-start.44 = (bf16[1024,2048]{1,0:T(8,128)(2,1)}, bf16[1024,2048]{1,0:T(8,128)(2,1)}, u32[]{:S(2)}, u32[]{:S(2)}) collective-permute-start(bf16[1024,2048]{1,0:T(8,128)(2,1)} %get-tuple-element.126), channel_id=1, source_target_pairs={{0,4},{4,0},{8,12},{12,8},{16,20},{20,16},{24,28},{28,24},{1,5},{5... | collective-permute-start | bytes 12582920 | tf_op jit(solution)/shard_map/ppermute | solution.py:31
  657.8 67.6 %collective-permute-start.53 = (bf16[1024,2048]{1,0:T(8,128)(2,1)}, bf16[1024,2048]{1,0:T(8,128)(2,1)}, u32[]{:S(2)}, u32[]{:S(2)}) collective-permute-start(bf16[1024,2048]{1,0:T(8,128)(2,1)} %get-tuple-element.133), channel_id=1, source_target_pairs={{0,4},{4,0},{8,12},{12,8},{16,20},{20,16},{24,28},{28,24},{1,5},{5... | collective-permute-start | bytes 12582920 | tf_op jit(solution)/shard_map/ppermute | solution.py:31
  681.3 76.4 %collective-permute-start.58 = (bf16[1024,2176]{1,0:T(8,128)(2,1)}, bf16[1024,2176]{1,0:T(8,128)(2,1)}, u32[]{:S(2)}, u32[]{:S(2)}) collective-permute-start(bf16[1024,2176]{1,0:T(8,128)(2,1)} %all-gather.18.cloned.1.call-done.refs_0_), channel_id=1, source_target_pairs={{0,4},{4,0},{8,12},{12,8},{16,20},{20,16},{24,28},{28,24},{1,5},{5... | collective-permute-start | bytes 13369352 | tf_op jit(solution)/shard_map/ppermute | solution.py:31
  757.6 87.5 %collective-permute-start.43 = (bf16[1024,2048]{1,0:T(8,128)(2,1)}, bf16[1024,2048]{1,0:T(8,128)(2,1)}, u32[]{:S(2)}, u32[]{:S(2)}) collective-permute-start(bf16[1024,2048]{1,0:T(8,128)(2,1)} %get-tuple-element.136), channel_id=1, source_target_pairs={{0,4},{4,0},{8,12},{12,8},{16,20},{20,16},{24,28},{28,24},{1,5},{5... | collective-permute-start | bytes 12582920 | tf_op jit(solution)/shard_map/ppermute | solution.py:31
  757.7 92.9 %collective-permute-start.49 = (bf16[1024,2048]{1,0:T(8,128)(2,1)}, bf16[1024,2048]{1,0:T(8,128)(2,1)}, u32[]{:S(2)}, u32[]{:S(2)}) collective-permute-start(bf16[1024,2048]{1,0:T(8,128)(2,1)} %get-tuple-element.147), channel_id=1, source_target_pairs={{0,4},{4,0},{8,12},{12,8},{16,20},{20,16},{24,28},{28,24},{1,5},{5... | collective-permute-start | bytes 12582920 | tf_op jit(solution)/shard_map/ppermute | solution.py:31
  844.8 523.4 %reduce-scatter.6.cloned.1.call-start = ((), (), s32[]{:S(2)}) async-start(), calls=%async_computation.12 | async-start | bytes 10485760 | tf_op jit(solution)/shard_map/reduce_scatter | solution.py:460
  863.1 510.6 %reduce-scatter.8.cloned.1.call-start = ((), (), s32[]{:S(2)}) async-start(), calls=%async_computation.13 | async-start | bytes 10485760 | tf_op jit(solution)/shard_map/reduce_scatter | solution.py:460
  871.9 218.7 %collective-permute-start.63 = (bf16[256,2048]{1,0:T(8,128)(2,1)}, bf16[256,2048]{1,0:T(8,128)(2,1)}, u32[]{:S(2)}, u32[]{:S(2)}) collective-permute-start(bf16[256,2048]{1,0:T(8,128)(2,1)} %pad_maximum_fusion.9), channel_id=1, source_target_pairs={{0,24},{4,28},{8,0},{12,4},{16,8},{20,12},{24,16},{28,20},{1,25},{... | collective-permute-start | bytes 3145736 | tf_op jit(solution)/shard_map/ppermute | solution.py:39
  896.4 194.1 %collective-permute-start.66 = (bf16[256,2048]{1,0:T(8,128)(2,1)}, bf16[256,2048]{1,0:T(8,128)(2,1)}, u32[]{:S(2)}, u32[]{:S(2)}) collective-permute-start(bf16[256,2048]{1,0:T(8,128)(2,1)} %pad_maximum_fusion.10), channel_id=1, source_target_pairs={{0,16},{4,20},{8,24},{12,28},{16,0},{20,4},{24,8},{28,12},{1,17},{... | collective-permute-start | bytes 3145736 | tf_op jit(solution)/shard_map/ppermute | solution.py:39
  906.8 99.0 %collective-permute-start.61 = (bf16[1024,2048]{1,0:T(8,128)(2,1)}, bf16[1024,2048]{1,0:T(8,128)(2,1)}, u32[]{:S(2)}, u32[]{:S(2)}) collective-permute-start(bf16[1024,2048]{1,0:T(8,128)(2,1)} %get-tuple-element.167), channel_id=1, source_target_pairs={{0,4},{4,0},{8,12},{12,8},{16,20},{20,16},{24,28},{28,24},{1,5},{5... | collective-permute-start | bytes 12582920 | tf_op jit(solution)/shard_map/ppermute | solution.py:31
  931.1 67.6 %collective-permute-start.68 = (bf16[128,2048]{1,0:T(8,128)(2,1)}, bf16[128,2048]{1,0:T(8,128)(2,1)S(1)}, u32[]{:S(2)}, u32[]{:S(2)}) collective-permute-start(bf16[128,2048]{1,0:T(8,128)(2,1)} %get-tuple-element.224), channel_id=1, source_target_pairs={{0,2},{1,3},{2,0},{3,1},{4,6},{5,7},{6,4},{7,5},{8,10},{9,11},{10,... | collective-permute-start | bytes 1572872 | tf_op jit(solution)/shard_map/ppermute | solution.py:56
  934.2 65.3 %collective-permute-start.70 = (bf16[128,2048]{1,0:T(8,128)(2,1)}, bf16[128,2048]{1,0:T(8,128)(2,1)}, u32[]{:S(2)}, u32[]{:S(2)}) collective-permute-start(bf16[128,2048]{1,0:T(8,128)(2,1)} %add_convert_fusion.12), channel_id=1, source_target_pairs={{0,1},{1,0},{2,3},{3,2},{4,5},{5,4},{6,7},{7,6},{8,9},{9,8},{10,11... | collective-permute-start | bytes 1572872 | tf_op jit(solution)/shard_map/ppermute | solution.py:56
  1018.1 407.8 %reduce-scatter.14.cloned.1.call-start = ((), (), s32[]{:S(2)}) async-start(), calls=%async_computation.16 | async-start | bytes 2359296 | tf_op jit(solution)/shard_map/reduce_scatter | solution.py:625
  1098.7 71.9 %collective-permute-start.78 = (bf16[128,2048]{1,0:T(8,128)(2,1)S(1)}, bf16[128,2048]{1,0:T(8,128)(2,1)S(1)}, u32[]{:S(2)}, u32[]{:S(2)}) collective-permute-start(bf16[128,2048]{1,0:T(8,128)(2,1)S(1)} %get-tuple-element.276), channel_id=1, source_target_pairs={{0,2},{1,3},{2,0},{3,1},{4,6},{5,7},{6,4},{7,5},{8,10},{9,11},{10,... | collective-permute-start | bytes 1572872 | tf_op jit(solution)/shard_map/ppermute | solution.py:56
  1102.8 72.3 %collective-permute-start.76 = (bf16[128,2048]{1,0:T(8,128)(2,1)S(1)}, bf16[128,2048]{1,0:T(8,128)(2,1)S(1)}, u32[]{:S(2)}, u32[]{:S(2)}) collective-permute-start(bf16[128,2048]{1,0:T(8,128)(2,1)S(1)} %get-tuple-element.276), channel_id=1, source_target_pairs={{0,1},{1,0},{2,3},{3,2},{4,5},{5,4},{6,7},{7,6},{8,9},{9,8},{10,11... | collective-permute-start | bytes 1572872 | tf_op jit(solution)/shard_map/ppermute | solution.py:56
  1104.4 71.5 %collective-permute-start.77 = (bf16[128,2048]{1,0:T(8,128)(2,1)S(1)}, bf16[128,2048]{1,0:T(8,128)(2,1)S(1)}, u32[]{:S(2)}, u32[]{:S(2)}) collective-permute-start(bf16[128,2048]{1,0:T(8,128)(2,1)S(1)} %get-tuple-element.277), channel_id=1, source_target_pairs={{0,2},{1,3},{2,0},{3,1},{4,6},{5,7},{6,4},{7,5},{8,10},{9,11},{10,... | collective-permute-start | bytes 1572872 | tf_op jit(solution)/shard_map/ppermute | solution.py:56
  1104.4 67.9 %collective-permute-start.75 = (bf16[128,2048]{1,0:T(8,128)(2,1)S(1)}, bf16[128,2048]{1,0:T(8,128)(2,1)S(1)}, u32[]{:S(2)}, u32[]{:S(2)}) collective-permute-start(bf16[128,2048]{1,0:T(8,128)(2,1)S(1)} %get-tuple-element.277), channel_id=1, source_target_pairs={{0,1},{1,0},{2,3},{3,2},{4,5},{5,4},{6,7},{7,6},{8,9},{9,8},{10,11... | collective-permute-start | bytes 1572872 | tf_op jit(solution)/shard_map/ppermute | solution.py:56
  1269.4 180.5 %reduce-scatter.12.cloned.1.call-start = ((), (), s32[]{:S(2)}) async-start(), calls=%async_computation.15 | async-start | bytes 7077888 | tf_op jit(solution)/shard_map/reduce_scatter | solution.py:625
  1371.3 80.9 %collective-permute-start.50 = (bf16[256,2048]{1,0:T(8,128)(2,1)}, bf16[256,2048]{1,0:T(8,128)(2,1)}, u32[]{:S(2)}, u32[]{:S(2)}) collective-permute-start(bf16[256,2048]{1,0:T(8,128)(2,1)} %get-tuple-element.266), channel_id=1, source_target_pairs={{0,24},{4,28},{8,0},{12,4},{16,8},{20,12},{24,16},{28,20},{1,25},{... | collective-permute-start | bytes 3145736 | tf_op jit(solution)/shard_map/ppermute | solution.py:39
  1371.8 122.5 %collective-permute-start.51 = (bf16[256,2048]{1,0:T(8,128)(2,1)}, bf16[256,2048]{1,0:T(8,128)(2,1)}, u32[]{:S(2)}, u32[]{:S(2)}) collective-permute-start(bf16[256,2048]{1,0:T(8,128)(2,1)} %get-tuple-element.267), channel_id=1, source_target_pairs={{0,16},{4,20},{8,24},{12,28},{16,0},{20,4},{24,8},{28,12},{1,17},{... | collective-permute-start | bytes 3145736 | tf_op jit(solution)/shard_map/ppermute | solution.py:39
  1376.0 118.3 %collective-permute-start.62 = (bf16[256,2048]{1,0:T(8,128)(2,1)}, bf16[256,2048]{1,0:T(8,128)(2,1)}, u32[]{:S(2)}, u32[]{:S(2)}) collective-permute-start(bf16[256,2048]{1,0:T(8,128)(2,1)} %slice_bitcast_fusion.2), channel_id=1, source_target_pairs={{0,8},{4,12},{8,16},{12,20},{16,24},{20,28},{24,0},{28,4},{1,9},{5... | collective-permute-start | bytes 3145736 | tf_op jit(solution)/shard_map/ppermute | solution.py:39
  (221 other events, 4754.1 us)
Sparse Core Ops, SparseCore 0:
  10.3 68.7 all-gather.7
  80.7 57.3 all-gather.9
  139.9 63.0 all-gather.13
  205.3 180.7 all-gather.15
  387.8 56.9 all-gather.11
  446.4 56.4 all-gather.19
  504.8 66.7 all-gather.17
  844.9 149.9 reduce-scatter.9
  998.0 105.1 reduce-scatter.5
  1106.3 101.5 reduce-scatter.7
  1269.5 37.1 reduce-scatter.13
  1336.2 113.6 reduce-scatter.11

commit v2 on v1

--- a/solution.py
+++ b/solution.py
@@ -41,11 +41,11 @@
     )
 
 
-def around_nodes(operand):
+def around_nodes(operand, *between):
     count = lax.axis_size("fsdp") // 2
     pieces = []
     for step in range(1, count - 1):
-        pieces.append(shift_node(pieces[-1] if pieces else operand, 1))
+        pieces.append(shift_node(after(pieces[-1], *between) if pieces else operand, 1))
     if count > 1:
         pieces.append(shift_node(operand, -1))
     return pieces
@@ -134,6 +134,19 @@
     return hop_sum(*first, hop_two(*first))
 
 
+def scatter_dots(operand):
+    if lax.axis_size("tp") != 4:
+        return lax.psum_scatter(operand, "tp", scatter_dimension=2, tiled=True)
+    rank = lax.axis_index("tp")
+    size = operand.shape[2] // 4
+    total = lax.dynamic_slice_in_dim(operand, rank * size, size, 2)
+    for mask in (1, 2, 3):
+        total = total + swap_tp(
+            lax.dynamic_slice_in_dim(operand, (rank ^ mask) * size, size, 2), mask
+        )
+    return total
+
+
 def gather_small(operand):
     count = lax.axis_size("fsdp")
     nodes = count // 2
@@ -199,10 +212,11 @@
 
 def expert_kernel(extra, experts, base, *refs):
     x_ref, z_ref, gate_w, up_w, down_w = refs[:5]
-    back_ref, out_ref, dots_ref, hidden_ref, gate_grad_ref, up_grad_ref, copy_ref = refs[-7:]
+    back_ref, out_ref, dots_ref, hidden_ref, gate_grad_ref, up_grad_ref, copy_ref = refs[-8:-1]
+    gated_ref = refs[-1]
     count, width, size = gate_w.shape
     x = x_ref[:, :width]
-    copy_ref[0] = x
+    copy_ref[0] = x.T
     ends = x_ref[:, width:].astype(F32)
     lane = lax.broadcasted_iota(jnp.int32, ends.shape, 1)
     dots = jnp.zeros(ends.shape, F32)
@@ -220,9 +234,11 @@
         sigmoid_gate = 1.0 / (1.0 + jnp.exp(-gate_pre))
         activated = gate_pre * sigmoid_gate
         hidden = activated * up_pre
-        hidden_ref[0, :, columns] = (hidden * gate).astype(BF16)
+        gated = (hidden * gate).astype(BF16)
+        gated_ref[:, columns] = gated
+        hidden_ref[0, columns, :] = gated.T
         dots = dots + jnp.where(
-            lane == number, jnp.sum(hidden * down_grad, axis=1, keepdims=True), 0.0
+            lane == e, jnp.sum(hidden * down_grad, axis=1, keepdims=True), 0.0
         )
         hidden_grad = down_grad * gate
         gate_grad_ref[0, :, columns] = (
@@ -239,7 +255,7 @@
             columns = slice(e * size, (e + 1) * size)
             back = back + dot_nt(gate_grad_ref[0, :, columns], gate_w[e, rows, :])
             back = back + dot_nt(up_grad_ref[0, :, columns], up_w[e, rows, :])
-            out = out + dot(hidden_ref[0, :, columns], down_w[e, :, rows])
+            out = out + dot(gated_ref[:, columns], down_w[e, :, rows])
         back_ref[:, rows] = back.astype(BF16)
         out_ref[:, rows] = out.astype(BF16)
 
@@ -248,7 +264,7 @@
     rows, wide = x.shape
     count, width, size = gate_w.shape
     extra = wide - width
-    block = min(512, rows)
+    block = min(256, rows)
     hidden = count * size
 
     def whole(array):
@@ -262,9 +278,14 @@
     def in_slot(columns):
         return pl.BlockSpec((1, block, columns), lambda i, base: (slot, i, 0))
 
+    def turned_in_slot(columns):
+        return pl.BlockSpec((1, columns, block), lambda i, base: (slot, 0, i))
+
     kept_shapes = [
-        jax.ShapeDtypeStruct((slots, rows, columns), BF16)
-        for columns in (hidden, hidden, hidden, width)
+        jax.ShapeDtypeStruct((slots, hidden, rows), BF16),
+        jax.ShapeDtypeStruct((slots, rows, hidden), BF16),
+        jax.ShapeDtypeStruct((slots, rows, hidden), BF16),
+        jax.ShapeDtypeStruct((slots, width, rows), BF16),
     ]
     results = pl.pallas_call(
         functools.partial(expert_kernel, extra, experts),
@@ -280,7 +301,8 @@
             in_specs=[by_rows(wide), by_rows(hidden), whole(gate_w), whole(up_w), whole(down_w)]
             + [pl.BlockSpec(memory_space=pl.ANY)] * len(kept),
             out_specs=[by_rows(width), by_rows(width), by_rows(extra)]
-            + [in_slot(columns) for columns in (hidden, hidden, hidden, width)],
+            + [turned_in_slot(hidden), in_slot(hidden), in_slot(hidden), turned_in_slot(width)],
+            scratch_shapes=[pltpu.VMEM((block, hidden), BF16)],
         ),
         input_output_aliases={6 + i: 3 + i for i in range(len(kept))},
         cost_estimate=pl.CostEstimate(
@@ -291,6 +313,122 @@
         compiler_params=pltpu.CompilerParams(vmem_limit_bytes=60 * 1024 * 1024),
     )(base, x, z, gate_w, up_w, down_w, *kept)
     return results[0], results[1], results[2], tuple(results[3:])
+
+
+def wide_kernel(left, right, out_ref):
+    count, width, size = out_ref.shape
+    tile = min(512, width)
+    for start in range(0, width, tile):
+        rows = slice(start, start + tile)
+        part = dot(left[0, rows, :], right[0])
+
+        @pl.when(pl.program_id(0) == 0)
+        def _():
+            for e in range(count):
+                out_ref[e, rows, :] = part[:, e * size : (e + 1) * size]
+
+        @pl.when(pl.program_id(0) > 0)
+        def _():
+            for e in range(count):
+                out_ref[e, rows, :] += part[:, e * size : (e + 1) * size]
+
+
+def wide_products(turned, grads, count):
+    slots, width, rows = turned.shape
+    hidden = grads.shape[2]
+    size = hidden // count
+    return pl.pallas_call(
+        wide_kernel,
+        out_shape=jax.ShapeDtypeStruct((count, width, size), F32),
+        grid=(slots,),
+        in_specs=[
+            pl.BlockSpec((1, width, rows), lambda k: (k, 0, 0)),
+            pl.BlockSpec((1, rows, hidden), lambda k: (k, 0, 0)),
+        ],
+        out_specs=pl.BlockSpec((count, width, size), lambda k: (0, 0, 0)),
+        cost_estimate=pl.CostEstimate(
+            flops=2 * slots * rows * width * hidden,
+            bytes_accessed=2 * slots * rows * (width + hidden) + 4 * width * hidden,
+            transcendentals=0,
+        ),
+        compiler_params=pltpu.CompilerParams(vmem_limit_bytes=60 * 1024 * 1024),
+    )(turned, grads)
+
+
+def down_kernel(has_first, left, near, far, *refs):
+    out_ref = refs[-1]
+    step = pl.program_id(0)
+    height, width = out_ref.shape
+    tile = min(512, width)
+
+    @pl.when(step == 0)
+    def _():
+        for start in range(0, width, tile):
+            columns = slice(start, start + tile)
+            part = dot(left[0], near[0, :, columns])
+            if has_first:
+                part = part + refs[0][:, columns]
+            out_ref[:, columns] = part
+
+    @pl.when(step > 0)
+    def _():
+        for start in range(0, width, tile):
+            columns = slice(start, start + tile)
+            out_ref[:, columns] += dot(left[0], far[0, :, columns])
+
+
+def down_products(turned, slot, near, far, first=None):
+    _, hidden, rows = turned.shape
+    width = near.shape[1]
+    count = far.shape[0]
+    constant = pl.BlockSpec(
+        (hidden, width), lambda k: (0, 0), pipeline_mode=pl.Buffered(1)
+    )
+    return pl.pallas_call(
+        functools.partial(down_kernel, first is not None),
+        out_shape=jax.ShapeDtypeStruct((hidden, width), F32),
+        grid=(count + 1,),
+        in_specs=[
+            pl.BlockSpec((1, hidden, rows), lambda k: (slot + k, 0, 0)),
+            pl.BlockSpec((1, rows, width), lambda k: (0, 0, 0), pipeline_mode=pl.Buffered(1)),
+            pl.BlockSpec((1, rows, width), lambda k: (jnp.maximum(k - 1, 0), 0, 0)),
+        ]
+        + ([constant] if first is not None else []),
+        out_specs=pl.BlockSpec((hidden, width), lambda k: (0, 0)),
+        cost_estimate=pl.CostEstimate(
+            flops=2 * (count + 1) * rows * width * hidden,
+            bytes_accessed=2 * (count + 1) * rows * (width + hidden) + 4 * width * hidden,
+            transcendentals=0,
+        ),
+        compiler_params=pltpu.CompilerParams(vmem_limit_bytes=60 * 1024 * 1024),
+    )(turned, near[None], far, *(() if first is None else (first,)))
+
+
+def swap_rows(grad):
+    count = lax.axis_size("fsdp")
+    core = lax.axis_index("fsdp") % 2
+    blocks = grad.reshape(count // 2, 2, grad.shape[0] // count, grad.shape[1])
+    return (
+        lax.dynamic_index_in_dim(blocks, core, 1, keepdims=False),
+        swap_core(lax.dynamic_index_in_dim(blocks, 1 - core, 1, keepdims=False)),
+    )
+
+
+def sum_rows(mine, arrived):
+    nodes = mine.shape[0]
+    node = lax.axis_index("fsdp") // 2
+
+    def part(step):
+        place = (node + step) % nodes
+        return plus(
+            lax.dynamic_index_in_dim(mine, place, 0, keepdims=False),
+            lax.dynamic_index_in_dim(arrived, place, 0, keepdims=False),
+        )
+
+    total = part(0)
+    for step in range(1, nodes):
+        total = total + shift_node(part(step).astype(BF16), step).astype(F32)
+    return total
 
 
 def shards(
@@ -339,6 +477,7 @@
     qkv_w = lax.all_gather(
         jnp.concatenate([w_query, w_key, w_value], axis=1), "fsdp", axis=0, tiled=True
     )
+    out_w = lax.all_gather(w_out, "fsdp", axis=1, tiled=True)
 
     down_w = w_down.reshape(hidden_all, model_width)
 
@@ -349,11 +488,8 @@
 
     early = after(cotangent, qkv_w, first_all)
     grad_own = lax.all_gather(early, "tp", axis=0, tiled=True)
-    out_w = lax.all_gather(after(w_out, first_all), "fsdp", axis=1, tiled=True)
-    around = around_nodes(early)
-    near, far = around[:1] + around[2:], around[1:2]
-
     qkv_raw = dot(first_all, qkv_w)
+    around = around_nodes(early, qkv_raw)
     query_raw = qkv_raw[:, :local_width]
     key_raw = qkv_raw[:, local_width : 2 * local_width]
     value_raw = qkv_raw[:, 2 * local_width :]
@@ -387,8 +523,6 @@
     attn_blocks, log_totals = [], []
     for block_index in range(block_count):
         query_block, scores, causal = block_scores(block_index)
-        if block_index > 0:
-            scores = after(scores, near[0])
         top_score = jnp.max(scores, axis=-1, keepdims=True)
         exponent = jnp.exp(scores - top_score)
         row_total = jnp.sum(exponent, axis=-1, keepdims=True)
@@ -398,9 +532,9 @@
         )
         log_totals.append(top_score[..., 0] + jnp.log(row_total[..., 0]))
     heads_out = jnp.concatenate(attn_blocks, axis=0).reshape(seq_len, local_width).astype(BF16)
-    heads_out = after(heads_out, *near)
+    heads_out = after(heads_out, grad_own)
     attn_sum = scatter_halves(dot(heads_out, out_w).astype(BF16))
-    hidden_res = residual_in + after(attn_sum, *far)
+    hidden_res = residual_in + attn_sum
     normed_two, scale_two = norm_rows(hidden_res)
     second_in = (normed_two * moe_gain).astype(BF16)
 
@@ -422,7 +556,9 @@
         axis=1,
     )
 
-    grad_around = lax.all_gather(jnp.stack(around), "tp", axis=1, tiled=True)
+    grad_around = lax.all_gather(
+        after(jnp.stack(around), attn_blocks[0]), "tp", axis=1, tiled=True
+    )
     grad_sets = [grad_own, grad_around, swap_core(grad_own), swap_core(grad_around)]
     down_grads = [
         dot_nt(one.reshape(-1, model_width), down_w).astype(BF16).reshape(-1, seq_len, hidden_all)
@@ -435,7 +571,7 @@
     defer = nodes <= 4
     by_hops = tp_count == 4
     kept, gate_dots, backs, swaps, hops, lasts, returns = (), [], [], [], [], [], []
-    outs, outs_back = [], []
+    outs, outs_back, wholes = [], [], []
     base = jnp.reshape(fsdp_rank * local_experts, (1,)).astype(jnp.int32)
 
     def one_sequence(step, other, rows):
@@ -453,12 +589,12 @@
             kept,
             expert_count,
         )
-        return back, out, dots[:, :expert_count]
-
-    def outputs_home(outs, steps):
-        outs = jnp.stack([plus(own, swap_core(other)).astype(BF16) for own, other in outs])
-        outs = lax.psum_scatter(outs, "tp", scatter_dimension=1, tiled=True)
-        return [shift_node(outs[i], -step) for i, step in enumerate(steps)]
+        return back, out, dots[:, :local_experts].T
+
+    def outputs_home(out, step):
+        whole = plus(out[0], swap_core(out[1])).astype(BF16)
+        wholes.append(whole)
+        return [lax.psum_scatter(whole, "tp", scatter_dimension=0, tiled=True)]
 
     for step in range(nodes):
         own = owns[step]
@@ -491,52 +627,40 @@
             total = lax.psum_scatter(back_own, "tp", scatter_dimension=0, tiled=True)
             returns.append(shift_node(total, -step))
         if not defer:
-            outs_back += outputs_home(outs, [step])
-            outs = []
+            outs_back += [shift_node(outputs_home(outs[step], step)[0], -step)]
             kept = after(kept, outs_back[-1], returns[-1])
     if defer:
         late = owns[-1]
-        for steps in ([1, 2], [0, 3]) if nodes == 4 else [list(range(nodes))]:
-            outs_back += outputs_home([after(outs[step], late) for step in steps], steps)
+        for step in range(nodes):
+            outs_back += outputs_home(after(outs[step], late), step)
     hidden_kept, gate_kept, up_kept, rows_kept = kept
 
-    def down_product(index, *earlier):
-        grads = grad_sets[index].reshape(-1, model_width)
-        start = (0, 1, nodes, nodes + 1)[index]
-        count = grads.shape[0] // seq_len
-        hidden = hidden_kept[start : start + count].reshape(-1, hidden_all)
-        return dot_tn(after(hidden, *earlier), grads)
-
-    down_w_grad = down_product(0) + down_product(1)
+    down_w_grad = down_products(hidden_kept, 0, grad_own, grad_around)
     pins = hops[-1][2] if by_hops else ()
-    down_w_grad = down_w_grad + (down_product(2, *pins) + down_product(3, *pins))
+    down_w_grad = down_products(
+        after(hidden_kept, *pins), nodes, grad_sets[2], grad_sets[3], down_w_grad
+    )
     if by_hops and nodes > 1:
         returns[-1] = after(returns[-1], down_w_grad)
 
-    def wide_product(grads, *earlier):
-        rows = rows_kept.reshape(-1, model_width)
-        grads = after(grads, *earlier).reshape(-1, hidden_all)
-        return dot_tn(rows, grads).reshape(
-            model_width, local_experts, hidden_slice
-        ).transpose(1, 0, 2)
-
     back_sum = sum(one.astype(F32) for one in returns)
-    output = (hidden_res + sum(one.astype(F32) for one in outs_back)).astype(BF16)
+
+    def home(step, *earlier):
+        if defer:
+            outs_back[step] = shift_node(after(outs_back[step], *earlier), -step)
 
     node, core = fsdp_rank // 2, fsdp_rank % 2
-    blocks = []
-    for mine, others in gate_dots:
-        blocks.append(
-            jnp.where(core == 0, jnp.stack([mine.T, others.T], 1), jnp.stack([others.T, mine.T], 1))
-        )
-    blocks = jnp.stack(blocks[::-1] + blocks[::-1], axis=1)
-    blocks = lax.dynamic_slice_in_dim(blocks, nodes - 1 - node, nodes, 1)
-    prob_grad = lax.psum_scatter(
-        blocks.reshape(expert_count, fsdp_count * seq_len),
-        ("fsdp", "tp"),
-        scatter_dimension=1,
-        tiled=True,
-    ).T
+    dots = jnp.stack([one[0] for one in gate_dots] + [one[1] for one in gate_dots], axis=1)
+    dots = scatter_dots(dots)
+    mine, others = dots[:, :nodes], swap_core(dots[:, nodes:])
+    pair = jnp.where(core == 0, jnp.stack([mine, others]), jnp.stack([others, mine]))
+    placed = jnp.stack(
+        [pair[:, :, 0]] + [shift_node(pair[:, :, step], -step) for step in range(1, nodes)]
+    )
+    placed = lax.dynamic_slice_in_dim(
+        jnp.concatenate([placed, placed], axis=0), nodes - node, nodes, 0
+    )
+    prob_grad = placed.reshape(expert_count, piece).T
 
     grad_out = cotangent.astype(F32)
     prob_grad = prob_grad * routed
@@ -557,11 +681,15 @@
 
     residual_all = gather_halves(residual_grad.astype(BF16))
 
-    gate_w_grad = wide_product(gate_kept, *returns[1:])
+    gate_w_grad = wide_products(rows_kept, after(gate_kept, *returns[1:], *wholes), local_experts)
     residual_all = after(residual_all, gate_w_grad)
 
-    out_w_grad = dot_tn(heads_out, residual_all)
+    out_w_swapped = swap_rows(dot_tn(residual_all, heads_out).astype(BF16))
+    out_w_out = sum_rows(*out_w_swapped).T
+    early_out = reduce_small(jnp.concatenate([moe_gain_grad[None], router_grad], axis=0))
     heads_grad = dot_nt(residual_all, out_w).astype(BF16).reshape(head_shape)
+    if nodes > 1:
+        home(1, heads_grad)
     key_rot_grad = jnp.zeros(head_shape, F32)
     value_grad = jnp.zeros(head_shape, F32)
     query_blocks_grad = []
@@ -571,6 +699,10 @@
         probs_full = jnp.where(causal[None], jnp.exp(scores - log_block[..., None]), 0.0)
         probs_bf = probs_full.astype(BF16)
         out_block = block_of(heads_grad, block_index)
+        if block_index > 0:
+            out_block = after(out_block, early_out, out_w_swapped[1], *outs_back[1:2])
+            if block_index == 1 and nodes > 2:
+                home(2, query_blocks_grad[0])
         value_grad = value_grad + jnp.einsum(
             "hqk,qhd->khd", probs_bf, out_block, preferred_element_type=F32
         )
@@ -612,29 +744,27 @@
     ).astype(BF16)
     value_raw_grad = value_grad.reshape(seq_len, local_width).astype(BF16)
     qkv_grad = jnp.concatenate([query_raw_grad, key_raw_grad, value_raw_grad], axis=1)
+    qkv_grad = after(qkv_grad, out_w_out, *(outs_back[2:3] if block_count > 1 else []))
     first_part = dot_nt(qkv_grad, qkv_w).astype(BF16)
     first_grad = scatter_halves(first_part)
+    home(0, first_part)
+    for step in range(3 if block_count > 1 else 2, nodes):
+        home(step, first_part)
+    output = (hidden_res + sum(one.astype(F32) for one in outs_back)).astype(BF16)
     qkv_w_grad = dot_tn(first_all, qkv_grad).astype(BF16)
-    up_w_grad = wide_product(up_kept, first_part, qkv_w_grad)
+    up_w_grad = wide_products(rows_kept, after(up_kept, first_part, qkv_w_grad, outs_back[0], outs_back[-1]), local_experts)
     down_w_grad = down_w_grad.reshape(local_experts, hidden_slice, model_width)
 
     attn_gain_grad = jnp.sum(normed_one * first_grad, axis=0)
     input_grad = residual_grad + norm_back(normed_one, scale_one, first_grad * attn_gain)
 
-    def scatter_fsdp(grad, dimension):
-        return lax.psum_scatter(
-            grad.astype(BF16), "fsdp", scatter_dimension=dimension, tiled=True
-        ).astype(F32)
-
-    qkv_out = scatter_fsdp(qkv_w_grad, 0)
-    out_w_out = scatter_fsdp(out_w_grad, 1)
+    qkv_out = sum_rows(*swap_rows(qkv_w_grad))
 
     def widen(grad):
         return lax.dynamic_update_slice_in_dim(
             jnp.zeros((1, model_width), F32), grad[None], column_start, 1
         )
 
-    early_out = reduce_small(jnp.concatenate([moe_gain_grad[None], router_grad], axis=0))
     late_out = reduce_small(
         jnp.concatenate(
             [attn_gain_grad[None], widen(qgain_local), widen(kgain_local)], axis=0

time: 1510 us -> 1540 us (1.020)
  matrix products: 297 us -> 143 us
  Pallas kernels: 260 us -> 403 us
  waiting for transfers between devices: 515 us -> 621 us
  local copies, waits for them, and re-layouts: 140 us -> 82.9 us
  other arithmetic: 161 us -> 135 us
    pallas_call x0 -> x4, Pallas kernels: none -> 160 us  [the longest x2 106 us: wide_products(): pl.pallas_call(wide_kernel, out_shape=jax.ShapeDtypeStruct((count, width,...]
    dot_general x8 -> x2, matrix products: 160 us -> 14.2 us  [dot_tn(): lax.dot_general(a, b, (((0,), (0,)), ((), ())), preferred_element_type=F32)]
    ppermute x21 -> x30, waiting for transfers between devices: 165 us -> 266 us  [shift_node(): lax.ppermute(operand, 'fsdp', [(i, (i // 2 + step) % nodes * 2 + i % 2) f...]
    reduce_scatter x5 -> x4, waiting for transfers between devices: 75.1 us -> 0.01 us  [outputs_home(): return [lax.psum_scatter(whole, 'tp', scatter_dimension=0, tiled=True)]]
    ppermute x66 -> x69, waiting for transfers between devices: 253 us -> 306 us  [swap_tp(): return lax.ppermute(operand, 'tp', [(i, i ^ mask) for i in range(count)])]
    dot_general x2 -> x0, local copies, waits for them, and re-layouts: 42.3 us -> none  [dot_tn(): lax.dot_general(a, b, (((0,), (0,)), ((), ())), preferred_element_type=F32)]
    another operation x13 -> x8, other arithmetic: 55.6 us -> 21 us  [the longest x6 36.5 us: outputs_home(): jnp.stack([plus(own, swap_core(other)).astype(BF16) for own, other in outs])]
    convert_element_type x3 -> x6, other arithmetic: 5.26 us -> 28.4 us  [the longest x4 22.2 us: outputs_home(): whole = plus(out[0], swap_core(out[1])).astype(BF16)]
  transfers between devices with their start and end apart: 116 -> 130, of which waited for: 47 -> 62; matrix products, arithmetic and copies ran while one was open for 38% -> 22% of each run, Pallas kernels for 17% -> 23%
where the time goes in v2:
time: 1540 us; the launch traced here: 1530 us
  waiting for transfers between devices  621 us (40%)
  Pallas kernels  403 us (26%)
  matrix products  143 us (9%)
  other arithmetic  135 us (9%)
  starting transfers between devices  128 us (8%)
  local copies, waits for them, and re-layouts  82.9 us (5%)
  between operations  16.5 us (1%)
    ppermute x69, waiting for transfers between devices, swap_tp(): return lax.ppermute(operand, 'tp', [(i, i ^ mask) for i in range(count)])  306 us
    ppermute x30, waiting for transfers between devices, shift_node(): lax.ppermute(operand, 'fsdp', [(i, (i // 2 + step) % nodes * 2 + i % 2) f...  266 us
    pallas_call x8, Pallas kernels, expert_products(): pl.pallas_call(functools.partial(expert_kernel, extra, experts), out_shap...  244 us
    pallas_call x2, Pallas kernels, wide_products(): pl.pallas_call(wide_kernel, out_shape=jax.ShapeDtypeStruct((count, width,...  106 us
    ppermute x69, starting transfers between devices, swap_tp(): return lax.ppermute(operand, 'tp', [(i, i ^ mask) for i in range(count)])  74.9 us
    dot_general x7, matrix products, dot_nt(): lax.dot_general(a, b, (((1,), (1,)), ((), ())), preferred_element_type=F32)  61.8 us
    pallas_call x2, Pallas kernels, down_products(): pl.pallas_call(functools.partial(down_kernel, first is not None), out_sha...  53.9 us
    ppermute x30, starting transfers between devices, shift_node(): lax.ppermute(operand, 'fsdp', [(i, (i // 2 + step) % nodes * 2 + i % 2) f...  49.1 us
  transfers between devices with their start and end apart: 130, of which 62 were waited for; matrix products, arithmetic and copies ran while one was open for 22% of the time, Pallas kernels for 23%

profile of v2, /device:TPU:0, one launch (start us, length us, event | category | flops | bytes accessed | tf_op | source)
XLA Modules:
  0.0 1530.7 jit_solution(1749966401128496553)
XLA Ops:
  111.5 32.9 %collective-permute-done.29 = bf16[256,2048]{1,0:T(8,128)(2,1)} collective-permute-done((bf16[256,2048]{1,0:T(8,128)(2,1)S(1)}, bf16[256,2048]{1,0:T(8,128)(2,1)}, u32[]{:S(2)}, u32[]{:S(2)}) %collective-permute-start.29) | collective-permute-done | bytes 1048608 | tf_op jit(solution)/shard_map/ppermute | solution.py:39
  151.0 35.2 %collective-permute-done.30 = bf16[256,2048]{1,0:T(8,128)(2,1)S(1)} collective-permute-done((bf16[256,2048]{1,0:T(8,128)(2,1)}, bf16[256,2048]{1,0:T(8,128)(2,1)S(1)}, u32[]{:S(2)}, u32[]{:S(2)}) %collective-permute-start.30) | collective-permute-done | bytes 1048608 | tf_op jit(solution)/shard_map/ppermute | solution.py:39
  210.9 22.8 %collective-permute-done.14 = bf16[128,2048]{1,0:T(8,128)(2,1)S(1)} collective-permute-done((bf16[128,2048]{1,0:T(8,128)(2,1)S(1)}, bf16[128,2048]{1,0:T(8,128)(2,1)S(1)}, u32[]{:S(2)}, u32[]{:S(2)}) %collective-permute-start.14) | collective-permute-done | bytes 524320 | tf_op jit(solution)/shard_map/ppermute | solution.py:56
  236.0 19.5 %collective-permute-done.13 = bf16[128,2048]{1,0:T(8,128)(2,1)S(1)} collective-permute-done((bf16[128,2048]{1,0:T(8,128)(2,1)S(1)}, bf16[128,2048]{1,0:T(8,128)(2,1)S(1)}, u32[]{:S(2)}, u32[]{:S(2)}) %collective-permute-start.13) | collective-permute-done | bytes 524320 | tf_op jit(solution)/shard_map/ppermute | solution.py:56
  282.1 20.3 %collective-permute-done.25 = bf16[256,2176]{1,0:T(8,128)(2,1)S(1)} collective-permute-done((bf16[256,2176]{1,0:T(8,128)(2,1)S(1)}, bf16[256,2176]{1,0:T(8,128)(2,1)S(1)}, u32[]{:S(2)}, u32[]{:S(2)}) %collective-permute-start.25) | collective-permute-done | bytes 1114144 | tf_op jit(solution)/shard_map/ppermute | solution.py:39
  311.2 19.9 %collective-permute-done.22 = bf16[128,2176]{1,0:T(8,128)(2,1)S(1)} collective-permute-done((bf16[128,2176]{1,0:T(8,128)(2,1)S(1)}, bf16[128,2176]{1,0:T(8,128)(2,1)S(1)}, u32[]{:S(2)}, u32[]{:S(2)}) %collective-permute-start.22) | collective-permute-done | bytes 557088 | tf_op jit(solution)/shard_map/ppermute | solution.py:56
  335.8 20.8 %collective-permute-done.20 = bf16[128,2176]{1,0:T(8,128)(2,1)} collective-permute-done((bf16[128,2176]{1,0:T(8,128)(2,1)S(1)}, bf16[128,2176]{1,0:T(8,128)(2,1)}, u32[]{:S(2)}, u32[]{:S(2)}) %collective-permute-start.20) | collective-permute-done | bytes 557088 | tf_op jit(solution)/shard_map/ppermute | solution.py:56
  356.6 16.0 %all-gather.14.cloned.1.call-done.far = bf16[3,1024,2048]{2,1,0:T(8,128)(2,1)} async-done(((bf16[3,256,2048]{2,1,0:T(8,128)(2,1)}), bf16[3,1024,2048]{2,1,0:T(8,128)(2,1)}) %all-gather.14.cloned.1.call-update) | async-done | bytes 12582928 | tf_op jit(solution)/shard_map/all_gather | solution.py:559
  392.0 38.9 %collective-permute-done.27 = bf16[256,2176]{1,0:T(8,128)(2,1)S(1)} collective-permute-done((bf16[256,2176]{1,0:T(8,128)(2,1)S(1)}, bf16[256,2176]{1,0:T(8,128)(2,1)S(1)}, u32[]{:S(2)}, u32[]{:S(2)}) %collective-permute-start.27) | collective-permute-done | bytes 1114144 | tf_op jit(solution)/shard_map/ppermute | solution.py:39
  431.0 30.4 %shard_map.254 = (bf16[1024,2048]{1,0:T(8,128)(2,1)}, bf16[1024,2048]{1,0:T(8,128)(2,1)}, f32[1024,128]{1,0:T(8,128)}, bf16[8,1024,1024]{2,1,0:T(8,128)(2,1)}, b...) custom-call(s32[1]{0:T(128)} %bitcast.15.base, ...), custom_call_target="tpu_custom_call" | custom-call | flops 21474836480 | bytes 37748736 | tf_op jit(solution)/shard_map/pallas_call | solution.py:290
  470.7 30.3 %shard_map.255 = (bf16[1024,2048]{1,0:T(8,128)(2,1)}, bf16[1024,2048]{1,0:T(8,128)(2,1)}, f32[1024,128]{1,0:T(8,128)}, bf16[8,1024,1024]{2,1,0:T(8,128)(2,1)}, b...) custom-call(s32[1]{0:T(128)} %bitcast.15.base, ...), custom_call_target="tpu_custom_call", output_to_operand_aliasing={{3}: (6, {}), {4}: (7, {}), {5}: (8, {}), {6}: (9, {})} | custom-call | flops 21474836480 | bytes 37748736 | tf_op jit(solution)/shard_map/pallas_call | solution.py:290
  516.1 16.2 %convolution_convert_fusion.2 = bf16[3072,1024]{1,0:T(8,128)(2,1)S(1)} fusion(bf16[3072,2048]{1,0:T(8,128)(2,1)} %bitcast.21, bf16[1024,2048]{1,0:T(8,128)(2,1)S(1)} %bitcast.335), kind=kOutput, calls=%fused_computation.20 | convolution fusion | flops 12888047616 | bytes 23068672 | tf_op jit(solution)/shard_map/dot_general | solution.py:22
  535.1 30.1 %shard_map.256 = (bf16[1024,2048]{1,0:T(8,128)(2,1)}, bf16[1024,2048]{1,0:T(8,128)(2,1)}, f32[1024,128]{1,0:T(8,128)}, bf16[8,1024,1024]{2,1,0:T(8,128)(2,1)}, b...) custom-call(s32[1]{0:T(128)} %bitcast.15.base, ...), custom_call_target="tpu_custom_call", output_to_operand_aliasing={{3}: (6, {}), {4}: (7, {}), {5}: (8, {}), {6}: (9, {})} | custom-call | flops 21474836480 | bytes 37748736 | tf_op jit(solution)/shard_map/pallas_call | solution.py:290
  565.3 17.3 %convolution_convert_fusion.1 = bf16[3072,1024]{1,0:T(8,128)(2,1)S(1)} fusion(bf16[3072,2048]{1,0:T(8,128)(2,1)} %bitcast.421, bf16[1024,2048]{1,0:T(8,128)(2,1)} %bitcast.334), kind=kOutput, calls=%fused_computation.19 | convolution fusion | flops 12888047616 | bytes 23068672 | tf_op jit(solution)/shard_map/dot_general | solution.py:22
  590.2 30.2 %shard_map.257 = (bf16[1024,2048]{1,0:T(8,128)(2,1)}, bf16[1024,2048]{1,0:T(8,128)(2,1)}, f32[1024,128]{1,0:T(8,128)}, bf16[8,1024,1024]{2,1,0:T(8,128)(2,1)}, b...) custom-call(s32[1]{0:T(128)} %bitcast.15.base, ...), custom_call_target="tpu_custom_call", output_to_operand_aliasing={{3}: (6, {}), {4}: (7, {}), {5}: (8, {}), {6}: (9, {})} | custom-call | flops 21474836480 | bytes 37748736 | tf_op jit(solution)/shard_map/pallas_call | solution.py:290
  622.0 30.4 %shard_map.258 = (bf16[1024,2048]{1,0:T(8,128)(2,1)}, bf16[1024,2048]{1,0:T(8,128)(2,1)}, f32[1024,128]{1,0:T(8,128)}, bf16[8,1024,1024]{2,1,0:T(8,128)(2,1)}, b...) custom-call(s32[1]{0:T(128)} %bitcast.15.base, ...), custom_call_target="tpu_custom_call", output_to_operand_aliasing={{3}: (6, {}), {4}: (7, {}), {5}: (8, {}), {6}: (9, {})} | custom-call | flops 21474836480 | bytes 37748736 | tf_op jit(solution)/shard_map/pallas_call | solution.py:290
  689.5 24.0 %collective-permute-done.49 = bf16[128,2048]{1,0:T(8,128)(2,1)S(1)} collective-permute-done((bf16[128,2048]{1,0:T(8,128)(2,1)S(1)}, bf16[128,2048]{1,0:T(8,128)(2,1)S(1)}, u32[]{:S(2)}, u32[]{:S(2)}) %collective-permute-start.49) | collective-permute-done | bytes 524320 | tf_op jit(solution)/shard_map/ppermute | solution.py:56
  713.5 15.2 collective-permute-done.48
  728.7 31.2 %shard_map.259 = (bf16[1024,2048]{1,0:T(8,128)(2,1)}, bf16[1024,2048]{1,0:T(8,128)(2,1)}, f32[1024,128]{1,0:T(8,128)}, bf16[8,1024,1024]{2,1,0:T(8,128)(2,1)}, b...) custom-call(s32[1]{0:T(128)} %bitcast.15.base, ...), custom_call_target="tpu_custom_call", output_to_operand_aliasing={{3}: (6, {}), {4}: (7, {}), {5}: (8, {}), {6}: (9, {})} | custom-call | flops 21474836480 | bytes 37748736 | tf_op jit(solution)/shard_map/pallas_call | solution.py:290
  793.8 20.1 %collective-permute-done.50 = bf16[128,2048]{1,0:T(8,128)(2,1)} collective-permute-done((bf16[128,2048]{1,0:T(8,128)(2,1)S(1)}, bf16[128,2048]{1,0:T(8,128)(2,1)}, u32[]{:S(2)}, u32[]{:S(2)}) %collective-permute-start.50) | collective-permute-done | bytes 524320 | tf_op jit(solution)/shard_map/ppermute | solution.py:56
  815.8 16.4 %collective-permute-done.54 = bf16[128,2048]{1,0:T(8,128)(2,1)} collective-permute-done((bf16[128,2048]{1,0:T(8,128)(2,1)S(1)}, bf16[128,2048]{1,0:T(8,128)(2,1)}, u32[]{:S(2)}, u32[]{:S(2)}) %collective-permute-start.54) | collective-permute-done | bytes 524320 | tf_op jit(solution)/shard_map/ppermute | solution.py:56
  837.3 30.2 %shard_map.260 = (bf16[1024,2048]{1,0:T(8,128)(2,1)}, bf16[1024,2048]{1,0:T(8,128)(2,1)}, f32[1024,128]{1,0:T(8,128)}, bf16[8,1024,1024]{2,1,0:T(8,128)(2,1)}, b...) custom-call(s32[1]{0:T(128)} %bitcast.15.base, ...), custom_call_target="tpu_custom_call", output_to_operand_aliasing={{3}: (6, {}), {4}: (7, {}), {5}: (8, {}), {6}: (9, {})} | custom-call | flops 21474836480 | bytes 37748736 | tf_op jit(solution)/shard_map/pallas_call | solution.py:290
  886.4 19.6 %collective-permute-done.56 = bf16[128,2048]{1,0:T(8,128)(2,1)} collective-permute-done((bf16[128,2048]{1,0:T(8,128)(2,1)}, bf16[128,2048]{1,0:T(8,128)(2,1)}, u32[]{:S(2)}, u32[]{:S(2)}) %collective-permute-start.56) | collective-permute-done | bytes 524320 | tf_op jit(solution)/shard_map/ppermute | solution.py:56
  906.1 30.8 %shard_map.261 = (bf16[1024,2048]{1,0:T(8,128)(2,1)}, bf16[1024,2048]{1,0:T(8,128)(2,1)}, f32[1024,128]{1,0:T(8,128)}, bf16[8,1024,1024]{2,1,0:T(8,128)(2,1)}, b...) custom-call(s32[1]{0:T(128)} %bitcast.15.base, ...), custom_call_target="tpu_custom_call", output_to_operand_aliasing={{3}: (6, {}), {4}: (7, {}), {5}: (8, {}), {6}: (9, {})} | custom-call | flops 21474836480 | bytes 37748736 | tf_op jit(solution)/shard_map/pallas_call | solution.py:290
  949.0 25.5 %shard_map.262.refs_0_ = f32[1024,2048]{1,0:T(8,128)} custom-call(bf16[8,1024,1024]{2,1,0:T(8,128)(2,1)} %get-tuple-element.161.left, bf16[1,1024,2048]{2,1,0:T(8,128)(2,1)} %bitcast.424, bf16[3,1024,2048]{2,1,0:T(8,128)(2,1)} %all-gather.14.cloned.1.call-done.far), custom_call_target="tpu_custom_call" | custom-call | flops 17179869184 | bytes 33554432 | tf_op jit(solution)/shard_map/pallas_call | solution.py:387
  1029.4 28.4 %shard_map.263 = f32[1024,2048]{1,0:T(8,128)} custom-call(bf16[8,1024,1024]{2,1,0:T(8,128)(2,1)} %get-tuple-element.161.left, bf16[1,1024,2048]{2,1,0:T(8,128)(2,1)} %bitcast.23.near, bf16[3,1024,2048]{2,1,0:T(8,128)(2,1)} %collective-permute-done.34.far, f32[1024,2048]{1,0:T(8,128)} %shard_map.262.refs_0_), custom_call_target="tpu_custom_call" | custom-call | flops 17179869184 | bytes 33554432 | tf_op jit(solution)/shard_map/pallas_call | solution.py:387
  1057.7 22.1 %collective-permute-done.59 = bf16[256,2048]{1,0:T(8,128)(2,1)} collective-permute-done((bf16[256,2048]{1,0:T(8,128)(2,1)}, bf16[256,2048]{1,0:T(8,128)(2,1)}, u32[]{:S(2)}, u32[]{:S(2)}) %collective-permute-start.59) | collective-permute-done | bytes 1048608 | tf_op jit(solution)/shard_map/ppermute | solution.py:39
  1102.3 52.7 %shard_map.264 = f32[4,2048,256]{2,1,0:T(8,128)} custom-call(bf16[8,2048,1024]{2,1,0:T(8,128)(2,1)} %get-tuple-element.171.left, bf16[8,1024,1024]{2,1,0:T(8,128)(2,1)} %get-tuple-element.185.right), custom_call_target="tpu_custom_call" | custom-call | flops 34359738368 | bytes 58720256 | tf_op jit(solution)/shard_map/pallas_call | solution.py:340
  1273.0 18.1 %collective-permute-done.98 = bf16[256,512]{0,1:T(8,128)(2,1)S(1)} collective-permute-done((bf16[256,512]{0,1:T(8,128)(2,1)S(1)}, bf16[256,512]{0,1:T(8,128)(2,1)S(1)}, u32[]{:S(2)}, u32[]{:S(2)}) %collective-permute-start.98) | collective-permute-done | bytes 262176 | tf_op jit(solution)/shard_map/ppermute | solution.py:39
  1389.2 14.2 collective-permute-done.118
  1403.4 55.8 %collective-permute-done.117 = bf16[256,1536]{1,0:T(8,128)(2,1)} collective-permute-done((bf16[256,1536]{1,0:T(8,128)(2,1)}, bf16[256,1536]{1,0:T(8,128)(2,1)}, u32[]{:S(2)}, u32[]{:S(2)}) %collective-permute-start.117) | collective-permute-done | bytes 786464 | tf_op jit(solution)/shard_map/ppermute | solution.py:39
  1463.4 53.1 %shard_map.265 = f32[4,2048,256]{2,1,0:T(8,128)} custom-call(bf16[8,2048,1024]{2,1,0:T(8,128)(2,1)} %get-tuple-element.171.left, bf16[8,1024,1024]{2,1,0:T(8,128)(2,1)} %get-tuple-element.193.right), custom_call_target="tpu_custom_call" | custom-call | flops 34359738368 | bytes 58720256 | tf_op jit(solution)/shard_map/pallas_call | solution.py:340
  (743 shorter events, 645.6 us)
Async XLA Ops:
  7.2 71.9 %all-gather.8.cloned.1.call-start = ((), (), s32[]{:S(2)}) async-start(), calls=%async_computation.4 | async-start | bytes 7077888 | tf_op jit(solution)/shard_map/all_gather | solution.py:477
  9.4 192.8 %all-gather.10.cloned.1.call-start = ((), (), s32[]{:S(2)}) async-start(), calls=%async_computation.5 | async-start | bytes 5242880 | tf_op jit(solution)/shard_map/all_gather | solution.py:490
  79.1 123.1 %all-gather.12.cloned.1.call-start = ((), (), s32[]{:S(2)}) async-start(), calls=%async_computation.6 | async-start | bytes 2359296 | tf_op jit(solution)/shard_map/all_gather | solution.py:480
  79.8 292.8 %all-gather.14.cloned.1.call-start = ((), (), s32[]{:S(2)}) async-start(), calls=%async_computation.7 | async-start | bytes 15728640 | tf_op jit(solution)/shard_map/all_gather | solution.py:559
  189.8 311.3 %all-gather.20.cloned.1.call-start = ((), (), s32[]{:S(2)}) async-start(), calls=%async_computation.10 | async-start | bytes 5570560 | tf_op jit(solution)/shard_map/all_gather | solution.py:570
  303.5 261.7 %all-gather.18.cloned.1.call-start = ((), (), s32[]{:S(2)}) async-start(), calls=%async_computation.9 | async-start | bytes 5570560 | tf_op jit(solution)/shard_map/all_gather | solution.py:570
  306.5 155.0 %collective-permute-start.32 = (bf16[1024,2048]{1,0:T(8,128)(2,1)}, bf16[1024,2048]{1,0:T(8,128)(2,1)}, u32[]{:S(2)}, u32[]{:S(2)}) collective-permute-start(bf16[1024,2048]{1,0:T(8,128)(2,1)} %all-gather.10.cloned.1.call-done), channel_id=1, source_target_pairs={{0,4},{4,0},{8,12},{12,8},{16,20},{20,16},{24,28},{28,24},{1,5},{5... | collective-permute-start | bytes 12582920 | tf_op jit(solution)/shard_map/ppermute | solution.py:31
  307.3 67.3 %collective-permute-start.21 = (bf16[128,2176]{1,0:T(8,128)(2,1)S(1)}, bf16[128,2176]{1,0:T(8,128)(2,1)}, u32[]{:S(2)}, u32[]{:S(2)}) collective-permute-start(bf16[128,2176]{1,0:T(8,128)(2,1)S(1)} %get-tuple-element.279), channel_id=1, source_target_pairs={{0,2},{1,3},{2,0},{3,1},{4,6},{5,7},{6,4},{7,5},{8,10},{9,11},{10,... | collective-permute-start | bytes 1671176 | tf_op jit(solution)/shard_map/ppermute | solution.py:56
  372.6 143.3 %collective-permute-start.34 = (bf16[3,1024,2048]{2,1,0:T(8,128)(2,1)}, bf16[3,1024,2048]{2,1,0:T(8,128)(2,1)}, u32[]{:S(2)}, u32[]{:S(2)}) collective-permute-start(bf16[3,1024,2048]{2,1,0:T(8,128)(2,1)} %all-gather.14.cloned.1.call-done.far), channel_id=1, source_target_pairs={{0,4},{4,0},{8,12},{12,8},{16,20},{20,16},{24,28},{28,24},{1,5},{5... | collective-permute-start | bytes 37748744 | tf_op jit(solution)/shard_map/ppermute | solution.py:31
  380.1 90.7 %collective-permute-start.28 = (bf16[1024,2176]{1,0:T(8,128)(2,1)}, bf16[1024,2176]{1,0:T(8,128)(2,1)}, u32[]{:S(2)}, u32[]{:S(2)}) collective-permute-start(bf16[1024,2176]{1,0:T(8,128)(2,1)} %constant_dynamic-update-slice_fusion.9.refs_0_), channel_id=1, source_target_pairs={{0,4},{4,0},{8,12},{12,8},{16,20},{20,16},{24,28},{28,24},{1,5},{5... | collective-permute-start | bytes 13369352 | tf_op jit(solution)/shard_map/ppermute | solution.py:31
  431.0 221.4 %all-gather.16.cloned.1.call-start = ((), (), s32[]{:S(2)}) async-start(), calls=%async_computation.8 | async-start | bytes 5570560 | tf_op jit(solution)/shard_map/all_gather | solution.py:570
  501.6 670.1 %reduce-scatter.7.cloned.1.call-start = ((), (), s32[]{:S(2)}) async-start(), calls=%async_computation.12 | async-start | bytes 5242880 | tf_op jit(solution)/shard_map/reduce_scatter | solution.py:597
  512.0 73.4 %collective-permute-start.42 = (bf16[128,2048]{1,0:T(8,128)(2,1)S(1)}, bf16[128,2048]{1,0:T(8,128)(2,1)}, u32[]{:S(2)}, u32[]{:S(2)}) collective-permute-start(bf16[128,2048]{1,0:T(8,128)(2,1)S(1)} %get-tuple-element.233), channel_id=1, source_target_pairs={{0,1},{1,0},{2,3},{3,2},{4,5},{5,4},{6,7},{7,6},{8,9},{9,8},{10,11... | collective-permute-start | bytes 1572872 | tf_op jit(solution)/shard_map/ppermute | solution.py:56
  513.8 71.6 %collective-permute-start.41 = (bf16[128,2048]{1,0:T(8,128)(2,1)S(1)}, bf16[128,2048]{1,0:T(8,128)(2,1)}, u32[]{:S(2)}, u32[]{:S(2)}) collective-permute-start(bf16[128,2048]{1,0:T(8,128)(2,1)S(1)} %get-tuple-element.234), channel_id=1, source_target_pairs={{0,2},{1,3},{2,0},{3,1},{4,6},{5,7},{6,4},{7,5},{8,10},{9,11},{10,... | collective-permute-start | bytes 1572872 | tf_op jit(solution)/shard_map/ppermute | solution.py:56
  514.7 70.7 %collective-permute-start.39 = (bf16[128,2048]{1,0:T(8,128)(2,1)S(1)}, bf16[128,2048]{1,0:T(8,128)(2,1)S(1)}, u32[]{:S(2)}, u32[]{:S(2)}) collective-permute-start(bf16[128,2048]{1,0:T(8,128)(2,1)S(1)} %get-tuple-element.235), channel_id=1, source_target_pairs={{0,1},{1,0},{2,3},{3,2},{4,5},{5,4},{6,7},{7,6},{8,9},{9,8},{10,11... | collective-permute-start | bytes 1572872 | tf_op jit(solution)/shard_map/ppermute | solution.py:56
  515.9 69.4 %collective-permute-start.37 = (bf16[128,2048]{1,0:T(8,128)(2,1)S(1)}, bf16[128,2048]{1,0:T(8,128)(2,1)S(1)}, u32[]{:S(2)}, u32[]{:S(2)}) collective-permute-start(bf16[128,2048]{1,0:T(8,128)(2,1)S(1)} %get-tuple-element.236), channel_id=1, source_target_pairs={{0,2},{1,3},{2,0},{3,1},{4,6},{5,7},{6,4},{7,5},{8,10},{9,11},{10,... | collective-permute-start | bytes 1572872 | tf_op jit(solution)/shard_map/ppermute | solution.py:56
  565.2 56.0 %collective-permute-start.35 = (bf16[1024,2176]{1,0:T(8,128)(2,1)}, bf16[1024,2176]{1,0:T(8,128)(2,1)}, u32[]{:S(2)}, u32[]{:S(2)}) collective-permute-start(bf16[1024,2176]{1,0:T(8,128)(2,1)} %all-gather.18.cloned.1.call-done.refs_0_), channel_id=1, source_target_pairs={{0,4},{4,0},{8,12},{12,8},{16,20},{20,16},{24,28},{28,24},{1,5},{5... | collective-permute-start | bytes 13369352 | tf_op jit(solution)/shard_map/ppermute | solution.py:31
  590.1 62.8 %collective-permute-start.44 = (bf16[1024,2048]{1,0:T(8,128)(2,1)}, bf16[1024,2048]{1,0:T(8,128)(2,1)}, u32[]{:S(2)}, u32[]{:S(2)}) collective-permute-start(bf16[1024,2048]{1,0:T(8,128)(2,1)} %get-tuple-element.122), channel_id=1, source_target_pairs={{0,4},{4,0},{8,12},{12,8},{16,20},{20,16},{24,28},{28,24},{1,5},{5... | collective-permute-start | bytes 12582920 | tf_op jit(solution)/shard_map/ppermute | solution.py:31
  675.9 543.5 %reduce-scatter.9.cloned.1.call-start = ((), (), s32[]{:S(2)}) async-start(), calls=%async_computation.13 | async-start | bytes 5242880 | tf_op jit(solution)/shard_map/reduce_scatter | solution.py:597
  778.7 593.0 %reduce-scatter.5.cloned.1.call-start = ((), (), s32[]{:S(2)}) async-start(), calls=%async_computation.11 | async-start | bytes 5242880 | tf_op jit(solution)/shard_map/reduce_scatter | solution.py:597
  786.2 87.2 %collective-permute-start.43 = (bf16[1024,2048]{1,0:T(8,128)(2,1)}, bf16[1024,2048]{1,0:T(8,128)(2,1)}, u32[]{:S(2)}, u32[]{:S(2)}) collective-permute-start(bf16[1024,2048]{1,0:T(8,128)(2,1)} %get-tuple-element.138), channel_id=1, source_target_pairs={{0,4},{4,0},{8,12},{12,8},{16,20},{20,16},{24,28},{28,24},{1,5},{5... | collective-permute-start | bytes 12582920 | tf_op jit(solution)/shard_map/ppermute | solution.py:31
  867.5 78.0 %collective-permute-start.61 = (bf16[1024,2048]{1,0:T(8,128)(2,1)}, bf16[1024,2048]{1,0:T(8,128)(2,1)}, u32[]{:S(2)}, u32[]{:S(2)}) collective-permute-start(bf16[1024,2048]{1,0:T(8,128)(2,1)} %get-tuple-element.159), channel_id=1, source_target_pairs={{0,4},{4,0},{8,12},{12,8},{16,20},{20,16},{24,28},{28,24},{1,5},{5... | collective-permute-start | bytes 12582920 | tf_op jit(solution)/shard_map/ppermute | solution.py:31
  879.5 496.7 %reduce-scatter.11.cloned.1.call-start = ((), (), s32[]{:S(2)}) async-start(), calls=%async_computation.14 | async-start | bytes 5242880 | tf_op jit(solution)/shard_map/reduce_scatter | solution.py:597
  943.0 70.9 %collective-permute-start.84 = (bf16[1024,2048]{1,0:T(8,128)(2,1)}, bf16[1024,2048]{1,0:T(8,128)(2,1)}, u32[]{:S(2)}, u32[]{:S(2)}) collective-permute-start(bf16[1024,2048]{1,0:T(8,128)(2,1)} %get-tuple-element.184), channel_id=1, source_target_pairs={{0,4},{4,0},{8,12},{12,8},{16,20},{20,16},{24,28},{28,24},{1,5},{5... | collective-permute-start | bytes 12582920 | tf_op jit(solution)/shard_map/ppermute | solution.py:31
  986.4 71.3 %collective-permute-start.51 = (bf16[256,2048]{1,0:T(8,128)(2,1)}, bf16[256,2048]{1,0:T(8,128)(2,1)}, u32[]{:S(2)}, u32[]{:S(2)}) collective-permute-start(bf16[256,2048]{1,0:T(8,128)(2,1)} %pad_maximum_fusion.4), channel_id=1, source_target_pairs={{0,24},{4,28},{8,0},{12,4},{16,8},{20,12},{24,16},{28,20},{1,25},{... | collective-permute-start | bytes 3145736 | tf_op jit(solution)/shard_map/ppermute | solution.py:39
  1007.2 72.7 %collective-permute-start.59 = (bf16[256,2048]{1,0:T(8,128)(2,1)}, bf16[256,2048]{1,0:T(8,128)(2,1)}, u32[]{:S(2)}, u32[]{:S(2)}) collective-permute-start(bf16[256,2048]{1,0:T(8,128)(2,1)} %pad_maximum_fusion.5), channel_id=1, source_target_pairs={{0,16},{4,20},{8,24},{12,28},{16,0},{20,4},{24,8},{28,12},{1,17},{... | collective-permute-start | bytes 3145736 | tf_op jit(solution)/shard_map/ppermute | solution.py:39
  1097.3 59.1 %collective-permute-start.79 = (bf16[128,2048]{1,0:T(8,128)(2,1)}, bf16[128,2048]{1,0:T(8,128)(2,1)S(1)}, u32[]{:S(2)}, u32[]{:S(2)}) collective-permute-start(bf16[128,2048]{1,0:T(8,128)(2,1)} %get-tuple-element.285), channel_id=1, source_target_pairs={{0,2},{1,3},{2,0},{3,1},{4,6},{5,7},{6,4},{7,5},{8,10},{9,11},{10,... | collective-permute-start | bytes 1572872 | tf_op jit(solution)/shard_map/ppermute | solution.py:56
  1098.4 60.7 %collective-permute-start.77 = (bf16[128,2048]{1,0:T(8,128)(2,1)}, bf16[128,2048]{1,0:T(8,128)(2,1)S(1)}, u32[]{:S(2)}, u32[]{:S(2)}) collective-permute-start(bf16[128,2048]{1,0:T(8,128)(2,1)} %get-tuple-element.285), channel_id=1, source_target_pairs={{0,1},{1,0},{2,3},{3,2},{4,5},{5,4},{6,7},{7,6},{8,9},{9,8},{10,11... | collective-permute-start | bytes 1572872 | tf_op jit(solution)/shard_map/ppermute | solution.py:56
  1099.6 57.8 %collective-permute-start.76 = (bf16[128,2048]{1,0:T(8,128)(2,1)}, bf16[128,2048]{1,0:T(8,128)(2,1)S(1)}, u32[]{:S(2)}, u32[]{:S(2)}) collective-permute-start(bf16[128,2048]{1,0:T(8,128)(2,1)} %get-tuple-element.286), channel_id=1, source_target_pairs={{0,1},{1,0},{2,3},{3,2},{4,5},{5,4},{6,7},{7,6},{8,9},{9,8},{10,11... | collective-permute-start | bytes 1572872 | tf_op jit(solution)/shard_map/ppermute | solution.py:56
  1219.4 73.6 %collective-permute-start.100 = (bf16[256,2048]{1,0:T(8,128)(2,1)}, bf16[256,2048]{1,0:T(8,128)(2,1)}, u32[]{:S(2)}, u32[]{:S(2)}) collective-permute-start(bf16[256,2048]{1,0:T(8,128)(2,1)} %reduce-scatter.9.cloned.1.call-done), channel_id=1, source_target_pairs={{0,16},{4,20},{8,24},{12,28},{16,0},{20,4},{24,8},{28,12},{1,17},{... | collective-permute-start | bytes 3145736 | tf_op jit(solution)/shard_map/ppermute | solution.py:39
  1370.5 88.7 %collective-permute-start.117 = (bf16[256,1536]{1,0:T(8,128)(2,1)}, bf16[256,1536]{1,0:T(8,128)(2,1)}, u32[]{:S(2)}, u32[]{:S(2)}) collective-permute-start(bf16[256,1536]{1,0:T(8,128)(2,1)} %get-tuple-element.215), channel_id=1, source_target_pairs={{0,16},{4,20},{8,24},{12,28},{16,0},{20,4},{24,8},{28,12},{1,17},{... | collective-permute-start | bytes 2359304 | tf_op jit(solution)/shard_map/ppermute | solution.py:39
  1376.2 86.2 %collective-permute-start.101 = (bf16[256,2048]{1,0:T(8,128)(2,1)}, bf16[256,2048]{1,0:T(8,128)(2,1)S(1)}, u32[]{:S(2)}, u32[]{:S(2)}) collective-permute-start(bf16[256,2048]{1,0:T(8,128)(2,1)} %reduce-scatter.11.cloned.1.call-done), channel_id=1, source_target_pairs={{0,8},{4,12},{8,16},{12,20},{16,24},{20,28},{24,0},{28,4},{1,9},{5... | collective-permute-start | bytes 3145736 | tf_op jit(solution)/shard_map/ppermute | solution.py:39
  (216 other events, 4321.3 us)
Sparse Core Ops, SparseCore 0:
  10.3 68.7 all-gather.7
  80.9 52.1 all-gather.9
  134.7 46.4 all-gather.11
  190.0 182.6 all-gather.13
  374.3 53.5 all-gather.19
  431.1 54.2 all-gather.17
  501.8 68.9 all-gather.15
  676.0 72.0 reduce-scatter.6
  778.9 83.6 reduce-scatter.8
  879.6 62.0 reduce-scatter.4
  1020.1 54.2 reduce-scatter.10

commit v3 on v2

--- a/solution.py
+++ b/solution.py
@@ -85,6 +85,19 @@
     ):
         placed = lax.dynamic_update_slice_in_dim(placed, part, (rank ^ mask) * rows + offset, 0)
     return placed
+
+
+def gather_pieces(operand):
+    if lax.axis_size("tp") != 4:
+        return lax.all_gather(operand, "tp", axis=0, tiled=True)
+    one = swap_tp(operand, 1)
+    two = swap_tp(operand, 2)
+    three = swap_tp(one, 2)
+    rank = lax.axis_index("tp")
+    placed = jnp.zeros((4,) + operand.shape, operand.dtype)
+    for mask, part in enumerate((operand, one, two, three)):
+        placed = lax.dynamic_update_slice_in_dim(placed, part[None], rank ^ mask, 0)
+    return placed.reshape(-1, operand.shape[1])
 
 
 def plus(mine, other):
@@ -355,53 +368,57 @@
     )(turned, grads)
 
 
-def down_kernel(has_first, left, near, far, *refs):
+def down_kernel(spans, has_first, left, *refs):
     out_ref = refs[-1]
     step = pl.program_id(0)
-    height, width = out_ref.shape
+    width = out_ref.shape[1]
     tile = min(512, width)
-
-    @pl.when(step == 0)
-    def _():
-        for start in range(0, width, tile):
-            columns = slice(start, start + tile)
-            part = dot(left[0], near[0, :, columns])
-            if has_first:
-                part = part + refs[0][:, columns]
-            out_ref[:, columns] = part
-
-    @pl.when(step > 0)
-    def _():
-        for start in range(0, width, tile):
-            columns = slice(start, start + tile)
-            out_ref[:, columns] += dot(left[0], far[0, :, columns])
-
-
-def down_products(turned, slot, near, far, first=None):
+    for index, (begin, end) in enumerate(spans):
+
+        @pl.when((step >= begin) & (step < end))
+        def _():
+            for start in range(0, width, tile):
+                columns = slice(start, start + tile)
+                part = dot(left[0], refs[index][0, :, columns])
+                if begin > 0:
+                    out_ref[:, columns] += part
+                elif has_first:
+                    out_ref[:, columns] = refs[-2][:, columns] + part
+                else:
+                    out_ref[:, columns] = part
+
+
+def down_products(turned, slot, arrays, first=None):
     _, hidden, rows = turned.shape
-    width = near.shape[1]
-    count = far.shape[0]
-    constant = pl.BlockSpec(
-        (hidden, width), lambda k: (0, 0), pipeline_mode=pl.Buffered(1)
-    )
+    width = arrays[0].shape[2]
+    spans, count = [], 0
+    for array in arrays:
+        spans.append((count, count + array.shape[0]))
+        count += array.shape[0]
+
+    def member(begin, end):
+        return pl.BlockSpec(
+            (1, rows, width),
+            lambda k: (jnp.clip(k - begin, 0, end - begin - 1), 0, 0),
+            pipeline_mode=pl.Buffered(1 if end - begin == 1 else 2),
+        )
+
+    constant = pl.BlockSpec((hidden, width), lambda k: (0, 0), pipeline_mode=pl.Buffered(1))
     return pl.pallas_call(
-        functools.partial(down_kernel, first is not None),
+        functools.partial(down_kernel, spans, first is not None),
         out_shape=jax.ShapeDtypeStruct((hidden, width), F32),
-        grid=(count + 1,),
-        in_specs=[
-            pl.BlockSpec((1, hidden, rows), lambda k: (slot + k, 0, 0)),
-            pl.BlockSpec((1, rows, width), lambda k: (0, 0, 0), pipeline_mode=pl.Buffered(1)),
-            pl.BlockSpec((1, rows, width), lambda k: (jnp.maximum(k - 1, 0), 0, 0)),
-        ]
+        grid=(count,),
+        in_specs=[pl.BlockSpec((1, hidden, rows), lambda k: (slot + k, 0, 0))]
+        + [member(*span) for span in spans]
         + ([constant] if first is not None else []),
         out_specs=pl.BlockSpec((hidden, width), lambda k: (0, 0)),
         cost_estimate=pl.CostEstimate(
-            flops=2 * (count + 1) * rows * width * hidden,
-            bytes_accessed=2 * (count + 1) * rows * (width + hidden) + 4 * width * hidden,
+            flops=2 * count * rows * width * hidden,
+            bytes_accessed=2 * count * rows * (width + hidden) + 4 * width * hidden,
             transcendentals=0,
         ),
         compiler_params=pltpu.CompilerParams(vmem_limit_bytes=60 * 1024 * 1024),
-    )(turned, near[None], far, *(() if first is None else (first,)))
+    )(turned, *arrays, *(() if first is None else (first,)))
 
 
 def swap_rows(grad):
@@ -474,11 +491,11 @@
     local_gains = lax.dynamic_slice_in_dim(small[2:4], column_start, local_width, 1).astype(F32)
     local_qgain, local_kgain = local_gains[0], local_gains[1]
     router_w = small[4:]
-    qkv_w = lax.all_gather(
-        jnp.concatenate([w_query, w_key, w_value], axis=1), "fsdp", axis=0, tiled=True
-    )
-    out_w = lax.all_gather(w_out, "fsdp", axis=1, tiled=True)
-
+    dense_w = lax.all_gather(
+        jnp.concatenate([w_query, w_key, w_value, w_out.T], axis=1), "fsdp", axis=0, tiled=True
+    )
+    dense_w = after(dense_w, tokens)
+    qkv_w, out_w = dense_w[:, : 3 * local_width], dense_w[:, 3 * local_width :]
     down_w = w_down.reshape(hidden_all, model_width)
 
     residual_in = tokens.astype(F32)
@@ -486,7 +503,7 @@
     first_in = (normed_one * attn_gain).astype(BF16)
     first_all = gather_halves(first_in)
 
-    early = after(cotangent, qkv_w, first_all)
+    early = after(cotangent, dense_w, first_all)
     grad_own = lax.all_gather(early, "tp", axis=0, tiled=True)
     qkv_raw = dot(first_all, qkv_w)
     around = around_nodes(early, qkv_raw)
@@ -532,8 +549,28 @@
         )
         log_totals.append(top_score[..., 0] + jnp.log(row_total[..., 0]))
     heads_out = jnp.concatenate(attn_blocks, axis=0).reshape(seq_len, local_width).astype(BF16)
-    heads_out = after(heads_out, grad_own)
-    attn_sum = scatter_halves(dot(heads_out, out_w).astype(BF16))
+    heads_out = after(heads_out, grad_own, *around[:1], *around[2:])
+    attn_sum = scatter_halves(dot_nt(heads_out, out_w).astype(BF16))
+    groups = [[0], [1, 3], [2]] if nodes == 4 else [[0]] + [list(range(1, nodes))] * (nodes > 1)
+    order = [step for group in groups for step in group]
+
+    def grad_products(own):
+        other = swap_core(own)
+        flat = [one.reshape(-1, model_width) for one in (own, other)]
+        return (own, other) + tuple(
+            dot_nt(one, down_w).astype(BF16).reshape(-1, seq_len, hidden_all) for one in flat
+        )
+
+    def grad_group(group, *earlier):
+        pieces = jnp.stack([around[step - 1] for step in group])
+        return grad_products(
+            lax.all_gather(after(pieces, *earlier), "tp", axis=1, tiled=True)
+        )
+
+    grad_sets = [grad_products(grad_own[None])]
+    if nodes > 1:
+        grad_sets.append(grad_group(groups[1], attn_blocks[0]))
+    attn_sum = after(attn_sum, *grad_sets[0][2:])
     hidden_res = residual_in + attn_sum
     normed_two, scale_two = norm_rows(hidden_res)
     second_in = (normed_two * moe_gain).astype(BF16)
@@ -556,64 +593,68 @@
         axis=1,
     )
 
-    grad_around = lax.all_gather(
-        after(jnp.stack(around), attn_blocks[0]), "tp", axis=1, tiled=True
-    )
-    grad_sets = [grad_own, grad_around, swap_core(grad_own), swap_core(grad_around)]
-    down_grads = [
-        dot_nt(one.reshape(-1, model_width), down_w).astype(BF16).reshape(-1, seq_len, hidden_all)
-        for one in grad_sets
-    ]
     sources = around_nodes(sent)
-    owns = [gather_halves(sent)]
-    for source in sources:
-        owns.append(lax.all_gather(source, "tp", axis=0, tiled=True))
+    owns = {0: gather_pieces(sent)}
+    for step in order[1:]:
+        owns[step] = None if step == 2 else lax.all_gather(
+            sources[step - 1], "tp", axis=0, tiled=True
+        )
     defer = nodes <= 4
     by_hops = tp_count == 4
     kept, gate_dots, backs, swaps, hops, lasts, returns = (), [], [], [], [], [], []
     outs, outs_back, wholes = [], [], []
     base = jnp.reshape(fsdp_rank * local_experts, (1,)).astype(jnp.int32)
 
-    def one_sequence(step, other, rows):
+    def one_sequence(place, other, rows):
         nonlocal kept
-        grads = down_grads[(1 if step > 0 else 0) + (2 if other else 0)]
+        index = next(i for i, group in enumerate(groups) if order[place] in group)
+        grads = grad_sets[index][3 if other else 2][groups[index].index(order[place])]
         back, out, dots, kept = expert_products(
             base,
             rows,
-            grads[max(step - 1, 0)],
+            grads,
             w_gate,
             w_up,
             w_down,
             2 * nodes,
-            step + (nodes if other else 0),
+            place + (nodes if other else 0),
             kept,
             expert_count,
         )
         return back, out, dots[:, :local_experts].T
 
-    def outputs_home(out, step):
+    def outputs_home(out, *earlier):
         whole = plus(out[0], swap_core(out[1])).astype(BF16)
         wholes.append(whole)
-        return [lax.psum_scatter(whole, "tp", scatter_dimension=0, tiled=True)]
-
-    for step in range(nodes):
+        return [
+            lax.psum_scatter(after(whole, *earlier), "tp", scatter_dimension=0, tiled=True)
+        ]
+
+    for place, step in enumerate(order):
         own = owns[step]
         other = swap_core(own)
-        if by_hops and step > 1:
-            own = after(own, *hops[step - 2][2])
-            other = after(other, *lasts[step - 2])
-        if step == 0:
-            first = one_sequence(step, False, after(own, *sources))
-            second = one_sequence(step, True, after(other, grad_around))
+        if by_hops and place > 1:
+            own = after(own, *hops[place - 2][2])
+            other = after(other, *lasts[place - 2])
+        if place == 0:
+            own = after(own, *sources[:1], *sources[2:])
+            first = one_sequence(place, False, own)
+            second = one_sequence(place, True, other)
             mine, others = first, second
+            if len(groups) > 2:
+                grad_sets.append(grad_group(groups[2], first[0]))
+            if 2 in order:
+                owns[2] = lax.all_gather(
+                    after(sources[1], second[0]), "tp", axis=0, tiled=True
+                )
         else:
             if by_hops:
-                own = after(own, *hops[step - 1][2])
-            first = one_sequence(step, True, other)
-            second = one_sequence(step, False, own)
+                own = after(own, *hops[place - 1][2])
+            first = one_sequence(place, True, other)
+            second = one_sequence(place, False, own)
             mine, others = second, first
-        if step + 1 < nodes:
-            owns[step + 1] = after(owns[step + 1], first[0])
+        if place + 1 < nodes:
+            owns[order[place + 1]] = after(owns[order[place + 1]], first[0])
         gate_dots.append((mine[2], others[2]))
         backs.append(mine[0])
         swaps.append(swap_core(others[0]))
@@ -627,27 +668,27 @@
             total = lax.psum_scatter(back_own, "tp", scatter_dimension=0, tiled=True)
             returns.append(shift_node(total, -step))
         if not defer:
-            outs_back += [shift_node(outputs_home(outs[step], step)[0], -step)]
+            outs_back += [shift_node(outputs_home(outs[place])[0], -step)]
             kept = after(kept, outs_back[-1], returns[-1])
     if defer:
-        late = owns[-1]
-        for step in range(nodes):
-            outs_back += outputs_home(after(outs[step], late), step)
+        pins = lasts[-1] if by_hops else (returns[-1],)
+        for place in range(nodes):
+            outs_back += outputs_home(outs[place], *pins)
     hidden_kept, gate_kept, up_kept, rows_kept = kept
 
-    down_w_grad = down_products(hidden_kept, 0, grad_own, grad_around)
+    down_w_grad = down_products(hidden_kept, 0, [one[0] for one in grad_sets])
     pins = hops[-1][2] if by_hops else ()
     down_w_grad = down_products(
-        after(hidden_kept, *pins), nodes, grad_sets[2], grad_sets[3], down_w_grad
+        after(hidden_kept, *pins), nodes, [one[1] for one in grad_sets], down_w_grad
     )
     if by_hops and nodes > 1:
         returns[-1] = after(returns[-1], down_w_grad)
 
     back_sum = sum(one.astype(F32) for one in returns)
 
-    def home(step, *earlier):
+    def home(place, *earlier):
         if defer:
-            outs_back[step] = shift_node(after(outs_back[step], *earlier), -step)
+            outs_back[place] = shift_node(after(outs_back[place], *earlier), -order[place])
 
     node, core = fsdp_rank // 2, fsdp_rank % 2
     dots = jnp.stack([one[0] for one in gate_dots] + [one[1] for one in gate_dots], axis=1)
@@ -655,7 +696,7 @@
     mine, others = dots[:, :nodes], swap_core(dots[:, nodes:])
     pair = jnp.where(core == 0, jnp.stack([mine, others]), jnp.stack([others, mine]))
     placed = jnp.stack(
-        [pair[:, :, 0]] + [shift_node(pair[:, :, step], -step) for step in range(1, nodes)]
+        [shift_node(pair[:, :, order.index(step)], -step) for step in range(nodes)]
     )
     placed = lax.dynamic_slice_in_dim(
         jnp.concatenate([placed, placed], axis=0), nodes - node, nodes, 0
@@ -687,9 +728,7 @@
     out_w_swapped = swap_rows(dot_tn(residual_all, heads_out).astype(BF16))
     out_w_out = sum_rows(*out_w_swapped).T
     early_out = reduce_small(jnp.concatenate([moe_gain_grad[None], router_grad], axis=0))
-    heads_grad = dot_nt(residual_all, out_w).astype(BF16).reshape(head_shape)
-    if nodes > 1:
-        home(1, heads_grad)
+    heads_grad = dot(residual_all, out_w).astype(BF16).reshape(head_shape)
     key_rot_grad = jnp.zeros(head_shape, F32)
     value_grad = jnp.zeros(head_shape, F32)
     query_blocks_grad = []
@@ -700,9 +739,7 @@
         probs_bf = probs_full.astype(BF16)
         out_block = block_of(heads_grad, block_index)
         if block_index > 0:
-            out_block = after(out_block, early_out, out_w_swapped[1], *outs_back[1:2])
-            if block_index == 1 and nodes > 2:
-                home(2, query_blocks_grad[0])
+            out_block = after(out_block, early_out, out_w_swapped[1])
         value_grad = value_grad + jnp.einsum(
             "hqk,qhd->khd", probs_bf, out_block, preferred_element_type=F32
         )
@@ -744,15 +781,14 @@
     ).astype(BF16)
     value_raw_grad = value_grad.reshape(seq_len, local_width).astype(BF16)
     qkv_grad = jnp.concatenate([query_raw_grad, key_raw_grad, value_raw_grad], axis=1)
-    qkv_grad = after(qkv_grad, out_w_out, *(outs_back[2:3] if block_count > 1 else []))
+    qkv_grad = after(qkv_grad, out_w_out)
     first_part = dot_nt(qkv_grad, qkv_w).astype(BF16)
     first_grad = scatter_halves(first_part)
-    home(0, first_part)
-    for step in range(3 if block_count > 1 else 2, nodes):
-        home(step, first_part)
+    for place in range(nodes):
+        home(place, query_blocks_grad[0] if place == 1 else first_part)
     output = (hidden_res + sum(one.astype(F32) for one in outs_back)).astype(BF16)
     qkv_w_grad = dot_tn(first_all, qkv_grad).astype(BF16)
-    up_w_grad = wide_products(rows_kept, after(up_kept, first_part, qkv_w_grad, outs_back[0], outs_back[-1]), local_experts)
+    up_w_grad = wide_products(rows_kept, after(up_kept, first_part, qkv_w_grad), local_experts)
     down_w_grad = down_w_grad.reshape(local_experts, hidden_slice, model_width)
 
     attn_gain_grad = jnp.sum(normed_one * first_grad, axis=0)

time: 1540 us -> 1500 us (0.974)
  waiting for transfers between devices: 621 us -> 569 us
    ppermute x30, waiting for transfers between devices: 266 us -> 224 us  [shift_node(): lax.ppermute(operand, 'fsdp', [(i, (i // 2 + step) % nodes * 2 + i % 2) f...]
    dot_general x7 -> x9, matrix products: 61.8 us -> 68.8 us  [dot_nt(): lax.dot_general(a, b, (((1,), (1,)), ((), ())), preferred_element_type=F32)]
    ppermute x69 -> x66, starting transfers between devices: 74.9 us -> 80.8 us  [swap_tp(): return lax.ppermute(operand, 'tp', [(i, i ^ mask) for i in range(count)])]
    ppermute x69 -> x66, waiting for transfers between devices: 306 us -> 302 us  [swap_tp(): return lax.ppermute(operand, 'tp', [(i, i ^ mask) for i in range(count)])]
  transfers between devices with their start and end apart: 130 -> 128, of which waited for: 62 -> 61; matrix products, arithmetic and copies ran while one was open for 22% -> 23% of each run, Pallas kernels for 23% -> 27%
where the time goes in v3:
time: 1500 us; the launch traced here: 1490 us
  waiting for transfers between devices  569 us (38%)
  Pallas kernels  405 us (27%)
  matrix products  155 us (10%)
  other arithmetic  139 us (9%)
  starting transfers between devices  127 us (8%)
  local copies, waits for them, and re-layouts  76.1 us (5%)
  between operations  16.8 us (1%)
    ppermute x66, waiting for transfers between devices, swap_tp(): return lax.ppermute(operand, 'tp', [(i, i ^ mask) for i in range(count)])  302 us
    pallas_call x8, Pallas kernels, expert_products(): pl.pallas_call(functools.partial(expert_kernel, extra, experts), out_shap...  243 us
    ppermute x30, waiting for transfers between devices, shift_node(): lax.ppermute(operand, 'fsdp', [(i, (i // 2 + step) % nodes * 2 + i % 2) f...  224 us
    pallas_call x2, Pallas kernels, wide_products(): pl.pallas_call(wide_kernel, out_shape=jax.ShapeDtypeStruct((count, width,...  106 us
    ppermute x66, starting transfers between devices, swap_tp(): return lax.ppermute(operand, 'tp', [(i, i ^ mask) for i in range(count)])  80.8 us
    dot_general x9, matrix products, dot_nt(): lax.dot_general(a, b, (((1,), (1,)), ((), ())), preferred_element_type=F32)  68.8 us
    pallas_call x2, Pallas kernels, down_products(): pl.pallas_call(functools.partial(down_kernel, spans, first is not None),...  56.1 us
    ppermute x30, starting transfers between devices, shift_node(): lax.ppermute(operand, 'fsdp', [(i, (i // 2 + step) % nodes * 2 + i % 2) f...  41.5 us
  transfers between devices with their start and end apart: 128, of which 61 were waited for; matrix products, arithmetic and copies ran while one was open for 23% of the time, Pallas kernels for 27%

profile of v3, /device:TPU:0, one launch (start us, length us, event | category | flops | bytes accessed | tf_op | source)
XLA Modules:
  0.0 1488.2 jit_solution(12152397549509950554)
XLA Ops:
  64.7 33.3 %all-gather.8.cloned.1.call-done = bf16[2048,2048]{0,1:T(8,128)(2,1)} async-done(((bf16[256,2048]{0,1:T(8,128)(2,1)}), bf16[2048,2048]{0,1:T(8,128)(2,1)}) %all-gather.8.cloned.1.call-update) | async-done | bytes 8388624 | tf_op jit(solution)/shard_map/all_gather | solution.py:494
  138.3 21.0 %collective-permute-done.13 = bf16[256,2048]{1,0:T(8,128)(2,1)} collective-permute-done((bf16[256,2048]{1,0:T(8,128)(2,1)S(1)}, bf16[256,2048]{1,0:T(8,128)(2,1)}, u32[]{:S(2)}, u32[]{:S(2)}) %collective-permute-start.13) | collective-permute-done | bytes 1048608 | tf_op jit(solution)/shard_map/ppermute | solution.py:39
  184.6 22.7 %collective-permute-done.16 = bf16[128,2048]{1,0:T(8,128)(2,1)S(1)} collective-permute-done((bf16[128,2048]{1,0:T(8,128)(2,1)S(1)}, bf16[128,2048]{1,0:T(8,128)(2,1)S(1)}, u32[]{:S(2)}, u32[]{:S(2)}) %collective-permute-start.16) | collective-permute-done | bytes 524320 | tf_op jit(solution)/shard_map/ppermute | solution.py:56
  227.0 17.2 %collective-permute-done.18 = bf16[128,2048]{1,0:T(8,128)(2,1)} collective-permute-done((bf16[128,2048]{1,0:T(8,128)(2,1)}, bf16[128,2048]{1,0:T(8,128)(2,1)}, u32[]{:S(2)}, u32[]{:S(2)}) %collective-permute-start.18) | collective-permute-done | bytes 524320 | tf_op jit(solution)/shard_map/ppermute | solution.py:56
  256.1 22.0 %collective-permute-done.24 = bf16[256,2176]{1,0:T(8,128)(2,1)S(1)} collective-permute-done((bf16[256,2176]{1,0:T(8,128)(2,1)S(1)}, bf16[256,2176]{1,0:T(8,128)(2,1)S(1)}, u32[]{:S(2)}, u32[]{:S(2)}) %collective-permute-start.24) | collective-permute-done | bytes 1114144 | tf_op jit(solution)/shard_map/ppermute | solution.py:39
  281.9 19.7 %collective-permute-done.25 = bf16[256,2176]{1,0:T(8,128)(2,1)} collective-permute-done((bf16[256,2176]{1,0:T(8,128)(2,1)S(1)}, bf16[256,2176]{1,0:T(8,128)(2,1)}, u32[]{:S(2)}, u32[]{:S(2)}) %collective-permute-start.25) | collective-permute-done | bytes 1114144 | tf_op jit(solution)/shard_map/ppermute | solution.py:39
  320.5 24.5 %collective-permute-done.22 = bf16[256,2176]{1,0:T(8,128)(2,1)S(1)} collective-permute-done((bf16[256,2176]{1,0:T(8,128)(2,1)S(1)}, bf16[256,2176]{1,0:T(8,128)(2,1)S(1)}, u32[]{:S(2)}, u32[]{:S(2)}) %collective-permute-start.22) | collective-permute-done | bytes 1114144 | tf_op jit(solution)/shard_map/ppermute | solution.py:56
  346.1 37.3 %collective-permute-done.23 = bf16[256,2176]{1,0:T(8,128)(2,1)S(1)} collective-permute-done((bf16[256,2176]{1,0:T(8,128)(2,1)S(1)}, bf16[256,2176]{1,0:T(8,128)(2,1)S(1)}, u32[]{:S(2)}, u32[]{:S(2)}) %collective-permute-start.23) | collective-permute-done | bytes 1114144 | tf_op jit(solution)/shard_map/ppermute | solution.py:56
  396.0 30.1 %shard_map.254 = (bf16[1024,2048]{1,0:T(8,128)(2,1)}, bf16[1024,2048]{1,0:T(8,128)(2,1)}, f32[1024,128]{1,0:T(8,128)}, bf16[8,1024,1024]{2,1,0:T(8,128)(2,1)}, b...) custom-call(s32[1]{0:T(128)} %bitcast.16.base, ...), custom_call_target="tpu_custom_call" | custom-call | flops 21474836480 | bytes 37748736 | tf_op jit(solution)/shard_map/pallas_call | solution.py:303
  436.7 31.0 %shard_map.255 = (bf16[1024,2048]{1,0:T(8,128)(2,1)}, bf16[1024,2048]{1,0:T(8,128)(2,1)}, f32[1024,128]{1,0:T(8,128)}, bf16[8,1024,1024]{2,1,0:T(8,128)(2,1)}, b...) custom-call(s32[1]{0:T(128)} %bitcast.16.base, ...), custom_call_target="tpu_custom_call", output_to_operand_aliasing={{3}: (6, {}), {4}: (7, {}), {5}: (8, {}), {6}: (9, {})} | custom-call | flops 21474836480 | bytes 37748736 | tf_op jit(solution)/shard_map/pallas_call | solution.py:303
  469.7 27.1 %collective-permute-done.29 = bf16[256,2176]{1,0:T(8,128)(2,1)S(1)} collective-permute-done((bf16[256,2176]{1,0:T(8,128)(2,1)S(1)}, bf16[256,2176]{1,0:T(8,128)(2,1)S(1)}, u32[]{:S(2)}, u32[]{:S(2)}) %collective-permute-start.29) | collective-permute-done | bytes 1114144 | tf_op jit(solution)/shard_map/ppermute | solution.py:39
  503.4 11.7 convolution_convert_fusion.2
  517.6 30.1 %shard_map.256 = (bf16[1024,2048]{1,0:T(8,128)(2,1)}, bf16[1024,2048]{1,0:T(8,128)(2,1)}, f32[1024,128]{1,0:T(8,128)}, bf16[8,1024,1024]{2,1,0:T(8,128)(2,1)}, b...) custom-call(s32[1]{0:T(128)} %bitcast.16.base, ...), custom_call_target="tpu_custom_call", output_to_operand_aliasing={{3}: (6, {}), {4}: (7, {}), {5}: (8, {}), {6}: (9, {})} | custom-call | flops 21474836480 | bytes 37748736 | tf_op jit(solution)/shard_map/pallas_call | solution.py:303
  547.8 13.0 convolution_convert_fusion.1
  578.4 30.2 %shard_map.257 = (bf16[1024,2048]{1,0:T(8,128)(2,1)}, bf16[1024,2048]{1,0:T(8,128)(2,1)}, f32[1024,128]{1,0:T(8,128)}, bf16[8,1024,1024]{2,1,0:T(8,128)(2,1)}, b...) custom-call(s32[1]{0:T(128)} %bitcast.16.base, ...), custom_call_target="tpu_custom_call", output_to_operand_aliasing={{3}: (6, {}), {4}: (7, {}), {5}: (8, {}), {6}: (9, {})} | custom-call | flops 21474836480 | bytes 37748736 | tf_op jit(solution)/shard_map/pallas_call | solution.py:303
  608.6 30.5 %shard_map.258 = (bf16[1024,2048]{1,0:T(8,128)(2,1)}, bf16[1024,2048]{1,0:T(8,128)(2,1)}, f32[1024,128]{1,0:T(8,128)}, bf16[8,1024,1024]{2,1,0:T(8,128)(2,1)}, b...) custom-call(s32[1]{0:T(128)} %bitcast.16.base, ...), custom_call_target="tpu_custom_call", output_to_operand_aliasing={{3}: (6, {}), {4}: (7, {}), {5}: (8, {}), {6}: (9, {})} | custom-call | flops 21474836480 | bytes 37748736 | tf_op jit(solution)/shard_map/pallas_call | solution.py:303
  642.9 12.7 collective-permute-done.42
  675.6 30.3 %shard_map.259 = (bf16[1024,2048]{1,0:T(8,128)(2,1)}, bf16[1024,2048]{1,0:T(8,128)(2,1)}, f32[1024,128]{1,0:T(8,128)}, bf16[8,1024,1024]{2,1,0:T(8,128)(2,1)}, b...) custom-call(s32[1]{0:T(128)} %bitcast.16.base, ...), custom_call_target="tpu_custom_call", output_to_operand_aliasing={{3}: (6, {}), {4}: (7, {}), {5}: (8, {}), {6}: (9, {})} | custom-call | flops 21474836480 | bytes 37748736 | tf_op jit(solution)/shard_map/pallas_call | solution.py:303
  707.7 30.8 %shard_map.260 = (bf16[1024,2048]{1,0:T(8,128)(2,1)}, bf16[1024,2048]{1,0:T(8,128)(2,1)}, f32[1024,128]{1,0:T(8,128)}, bf16[8,1024,1024]{2,1,0:T(8,128)(2,1)}, b...) custom-call(s32[1]{0:T(128)} %bitcast.16.base, ...), custom_call_target="tpu_custom_call", output_to_operand_aliasing={{3}: (6, {}), {4}: (7, {}), {5}: (8, {}), {6}: (9, {})} | custom-call | flops 21474836480 | bytes 37748736 | tf_op jit(solution)/shard_map/pallas_call | solution.py:303
  745.0 11.1 collective-permute-done.61
  756.1 10.8 collective-permute-done.47
  784.1 30.3 %shard_map.261 = (bf16[1024,2048]{1,0:T(8,128)(2,1)}, bf16[1024,2048]{1,0:T(8,128)(2,1)}, f32[1024,128]{1,0:T(8,128)}, bf16[8,1024,1024]{2,1,0:T(8,128)(2,1)}, b...) custom-call(s32[1]{0:T(128)} %bitcast.16.base, ...), custom_call_target="tpu_custom_call", output_to_operand_aliasing={{3}: (6, {}), {4}: (7, {}), {5}: (8, {}), {6}: (9, {})} | custom-call | flops 21474836480 | bytes 37748736 | tf_op jit(solution)/shard_map/pallas_call | solution.py:303
  818.6 12.8 collective-permute-done.56
  914.4 26.8 %shard_map.262.refs_3_ = f32[1024,2048]{1,0:T(8,128)} custom-call(bf16[8,1024,1024]{2,1,0:T(8,128)(2,1)} %get-tuple-element.161.left, bf16[1,1024,2048]{2,1,0:T(8,128)(2,1)} %bitcast.449, bf16[2,1024,2048]{2,1,0:T(8,128)(2,1)} %all-gather.18.cloned.1.call-done.refs_1_, bf16[1,1024,2048]{2,1,0:T(8,128)(2,1)} %all-gather.20.cloned.1.call-done.refs_2_), custom_call_target="tpu_custom_call" | custom-call | flops 17179869184 | bytes 33554432 | tf_op jit(solution)/shard_map/pallas_call | solution.py:407
  954.4 14.2 collective-permute-done.65
  974.0 29.3 %shard_map.263 = f32[1024,2048]{1,0:T(8,128)} custom-call(bf16[8,1024,1024]{2,1,0:T(8,128)(2,1)} %get-tuple-element.161.left, bf16[1,1024,2048]{2,1,0:T(8,128)(2,1)} %collective-permute-done.27.refs_0_, bf16[2,1024,2048]{2,1,0:T(8,128)(2,1)} %collective-permute-done.31.refs_1_, bf16[1,1024,2048]{2,1,0:T(8,128)(2,1)} %collective-permute-done.54.refs_2_, ...), custom_call_target="tpu_custom_call" | custom-call | flops 17179869184 | bytes 33554432 | tf_op jit(solution)/shard_map/pallas_call | solution.py:407
  1003.3 16.8 %collective-permute-done.66 = bf16[256,2048]{1,0:T(8,128)(2,1)} collective-permute-done((bf16[256,2048]{1,0:T(8,128)(2,1)}, bf16[256,2048]{1,0:T(8,128)(2,1)}, u32[]{:S(2)}, u32[]{:S(2)}) %collective-permute-start.66) | collective-permute-done | bytes 1048608 | tf_op jit(solution)/shard_map/ppermute | solution.py:39
  1043.6 53.1 %shard_map.264 = f32[4,2048,256]{2,1,0:T(8,128)} custom-call(bf16[8,2048,1024]{2,1,0:T(8,128)(2,1)} %get-tuple-element.171.left, bf16[8,1024,1024]{2,1,0:T(8,128)(2,1)} %get-tuple-element.179.right), custom_call_target="tpu_custom_call" | custom-call | flops 34359738368 | bytes 58720256 | tf_op jit(solution)/shard_map/pallas_call | solution.py:353
  1240.1 19.1 %collective-permute-done.101 = bf16[128,2048]{1,0:T(8,128)(2,1)} collective-permute-done((bf16[128,2048]{1,0:T(8,128)(2,1)}, bf16[128,2048]{1,0:T(8,128)(2,1)}, u32[]{:S(2)}, u32[]{:S(2)}) %collective-permute-start.101) | collective-permute-done | bytes 524320 | tf_op jit(solution)/shard_map/ppermute | solution.py:56
  1318.4 52.9 %shard_map.265 = f32[4,2048,256]{2,1,0:T(8,128)} custom-call(bf16[8,2048,1024]{2,1,0:T(8,128)(2,1)} %get-tuple-element.171.left, bf16[8,1024,1024]{2,1,0:T(8,128)(2,1)} %get-tuple-element.191.right), custom_call_target="tpu_custom_call" | custom-call | flops 34359738368 | bytes 58720256 | tf_op jit(solution)/shard_map/pallas_call | solution.py:353
  1389.3 39.8 %collective-permute-done.97 = bf16[256,2048]{1,0:T(8,128)(2,1)} collective-permute-done((bf16[256,2048]{1,0:T(8,128)(2,1)}, bf16[256,2048]{1,0:T(8,128)(2,1)}, u32[]{:S(2)}, u32[]{:S(2)}) %collective-permute-start.97) | collective-permute-done | bytes 1048608 | tf_op jit(solution)/shard_map/ppermute | solution.py:39
  1429.1 45.0 %collective-permute-done.99 = bf16[256,2048]{1,0:T(8,128)(2,1)} collective-permute-done((bf16[256,2048]{1,0:T(8,128)(2,1)}, bf16[256,2048]{1,0:T(8,128)(2,1)}, u32[]{:S(2)}, u32[]{:S(2)}) %collective-permute-start.99) | collective-permute-done | bytes 1048608 | tf_op jit(solution)/shard_map/ppermute | solution.py:39
  (772 shorter events, 634.2 us)
Async XLA Ops:
  7.3 90.8 %all-gather.8.cloned.1.call-start = ((), (), s32[]{:S(2)}) async-start(), calls=%async_computation.4 | async-start | bytes 9437184 | tf_op jit(solution)/shard_map/all_gather | solution.py:494
  12.7 163.1 %all-gather.10.cloned.1.call-start = ((), (), s32[]{:S(2)}) async-start(), calls=%async_computation.5 | async-start | bytes 5242880 | tf_op jit(solution)/shard_map/all_gather | solution.py:507
  98.1 297.7 %all-gather.18.cloned.1.call-start = ((), (), s32[]{:S(2)}) async-start(), calls=%async_computation.9 | async-start | bytes 10485760 | tf_op jit(solution)/shard_map/all_gather | solution.py:567
  162.4 305.6 %all-gather.16.cloned.1.call-start = ((), (), s32[]{:S(2)}) async-start(), calls=%async_computation.8 | async-start | bytes 5570560 | tf_op jit(solution)/shard_map/all_gather | solution.py:599
  279.2 268.5 %all-gather.14.cloned.1.call-start = ((), (), s32[]{:S(2)}) async-start(), calls=%async_computation.7 | async-start | bytes 5570560 | tf_op jit(solution)/shard_map/all_gather | solution.py:599
  301.6 263.6 %all-gather.20.cloned.1.call-start = ((), (), s32[]{:S(2)}) async-start(), calls=%async_computation.10 | async-start | bytes 5242880 | tf_op jit(solution)/shard_map/all_gather | solution.py:567
  301.7 125.6 %collective-permute-start.27 = (bf16[1,1024,2048]{2,1,0:T(8,128)(2,1)}, bf16[1,1024,2048]{2,1,0:T(8,128)(2,1)}, u32[]{:S(2)}, u32[]{:S(2)}) collective-permute-start(bf16[1,1024,2048]{2,1,0:T(8,128)(2,1)} %bitcast.448), channel_id=1, source_target_pairs={{0,4},{4,0},{8,12},{12,8},{16,20},{20,16},{24,28},{28,24},{1,5},{5... | collective-permute-start | bytes 12582920 | tf_op jit(solution)/shard_map/ppermute | solution.py:31
  308.7 74.7 %collective-permute-start.23 = (bf16[256,2176]{1,0:T(8,128)(2,1)S(1)}, bf16[256,2176]{1,0:T(8,128)(2,1)S(1)}, u32[]{:S(2)}, u32[]{:S(2)}) collective-permute-start(bf16[256,2176]{1,0:T(8,128)(2,1)S(1)} %collective-permute-done.21), channel_id=1, source_target_pairs={{0,2},{1,3},{2,0},{3,1},{4,6},{5,7},{6,4},{7,5},{8,10},{9,11},{10,... | collective-permute-start | bytes 3342344 | tf_op jit(solution)/shard_map/ppermute | solution.py:56
  395.7 107.7 %collective-permute-start.31 = (bf16[2,1024,2048]{2,1,0:T(8,128)(2,1)}, bf16[2,1024,2048]{2,1,0:T(8,128)(2,1)}, u32[]{:S(2)}, u32[]{:S(2)}) collective-permute-start(bf16[2,1024,2048]{2,1,0:T(8,128)(2,1)} %all-gather.18.cloned.1.call-done.refs_1_), channel_id=1, source_target_pairs={{0,4},{4,0},{8,12},{12,8},{16,20},{20,16},{24,28},{28,24},{1,5},{5... | collective-permute-start | bytes 25165832 | tf_op jit(solution)/shard_map/ppermute | solution.py:31
  427.0 212.2 %all-gather.12.cloned.1.call-start = ((), (), s32[]{:S(2)}) async-start(), calls=%async_computation.6 | async-start | bytes 5570560 | tf_op jit(solution)/shard_map/all_gather | solution.py:647
  497.8 877.8 %reduce-scatter.7.cloned.1.call-start = ((), (), s32[]{:S(2)}) async-start(), calls=%async_computation.12 | async-start | bytes 5242880 | tf_op jit(solution)/shard_map/reduce_scatter | solution.py:630
  501.2 64.0 %collective-permute-start.36 = (bf16[128,2048]{1,0:T(8,128)(2,1)S(1)}, bf16[128,2048]{1,0:T(8,128)(2,1)S(1)}, u32[]{:S(2)}, u32[]{:S(2)}) collective-permute-start(bf16[128,2048]{1,0:T(8,128)(2,1)S(1)} %get-tuple-element.237), channel_id=1, source_target_pairs={{0,1},{1,0},{2,3},{3,2},{4,5},{5,4},{6,7},{7,6},{8,9},{9,8},{10,11... | collective-permute-start | bytes 1572872 | tf_op jit(solution)/shard_map/ppermute | solution.py:56
  502.7 62.5 %collective-permute-start.34 = (bf16[128,2048]{1,0:T(8,128)(2,1)S(1)}, bf16[128,2048]{1,0:T(8,128)(2,1)S(1)}, u32[]{:S(2)}, u32[]{:S(2)}) collective-permute-start(bf16[128,2048]{1,0:T(8,128)(2,1)S(1)} %get-tuple-element.238), channel_id=1, source_target_pairs={{0,2},{1,3},{2,0},{3,1},{4,6},{5,7},{6,4},{7,5},{8,10},{9,11},{10,... | collective-permute-start | bytes 1572872 | tf_op jit(solution)/shard_map/ppermute | solution.py:56
  547.7 60.9 %collective-permute-start.32 = (bf16[1024,2176]{1,0:T(8,128)(2,1)}, bf16[1024,2176]{1,0:T(8,128)(2,1)}, u32[]{:S(2)}, u32[]{:S(2)}) collective-permute-start(bf16[1024,2176]{1,0:T(8,128)(2,1)} %all-gather.14.cloned.1.call-done.refs_0_), channel_id=1, source_target_pairs={{0,4},{4,0},{8,12},{12,8},{16,20},{20,16},{24,28},{28,24},{1,5},{5... | collective-permute-start | bytes 13369352 | tf_op jit(solution)/shard_map/ppermute | solution.py:31
  565.2 96.0 %collective-permute-start.54 = (bf16[1,1024,2048]{2,1,0:T(8,128)(2,1)}, bf16[1,1024,2048]{2,1,0:T(8,128)(2,1)}, u32[]{:S(2)}, u32[]{:S(2)}) collective-permute-start(bf16[1,1024,2048]{2,1,0:T(8,128)(2,1)} %all-gather.20.cloned.1.call-done.refs_2_), channel_id=1, source_target_pairs={{0,4},{4,0},{8,12},{12,8},{16,20},{20,16},{24,28},{28,24},{1,5},{5... | collective-permute-start | bytes 12582920 | tf_op jit(solution)/shard_map/ppermute | solution.py:31
  565.3 74.5 %collective-permute-start.40 = (bf16[1024,2048]{1,0:T(8,128)(2,1)}, bf16[1024,2048]{1,0:T(8,128)(2,1)}, u32[]{:S(2)}, u32[]{:S(2)}) collective-permute-start(bf16[1024,2048]{1,0:T(8,128)(2,1)} %get-tuple-element.122), channel_id=1, source_target_pairs={{0,4},{4,0},{8,12},{12,8},{16,20},{20,16},{24,28},{28,24},{1,5},{5... | collective-permute-start | bytes 12582920 | tf_op jit(solution)/shard_map/ppermute | solution.py:31
  639.1 66.7 %collective-permute-start.45 = (bf16[1024,2048]{1,0:T(8,128)(2,1)}, bf16[1024,2048]{1,0:T(8,128)(2,1)}, u32[]{:S(2)}, u32[]{:S(2)}) collective-permute-start(bf16[1024,2048]{1,0:T(8,128)(2,1)} %get-tuple-element.134), channel_id=1, source_target_pairs={{0,4},{4,0},{8,12},{12,8},{16,20},{20,16},{24,28},{28,24},{1,5},{5... | collective-permute-start | bytes 12582920 | tf_op jit(solution)/shard_map/ppermute | solution.py:31
  639.2 68.5 %collective-permute-start.51 = (bf16[1024,2176]{1,0:T(8,128)(2,1)}, bf16[1024,2176]{1,0:T(8,128)(2,1)}, u32[]{:S(2)}, u32[]{:S(2)}) collective-permute-start(bf16[1024,2176]{1,0:T(8,128)(2,1)} %all-gather.12.cloned.1.call-done.refs_0_), channel_id=1, source_target_pairs={{0,4},{4,0},{8,12},{12,8},{16,20},{20,16},{24,28},{28,24},{1,5},{5... | collective-permute-start | bytes 13369352 | tf_op jit(solution)/shard_map/ppermute | solution.py:31
  738.5 75.9 %collective-permute-start.55 = (bf16[1024,2048]{1,0:T(8,128)(2,1)}, bf16[1024,2048]{1,0:T(8,128)(2,1)}, u32[]{:S(2)}, u32[]{:S(2)}) collective-permute-start(bf16[1024,2048]{1,0:T(8,128)(2,1)} %get-tuple-element.158), channel_id=1, source_target_pairs={{0,4},{4,0},{8,12},{12,8},{16,20},{20,16},{24,28},{28,24},{1,5},{5... | collective-permute-start | bytes 12582920 | tf_op jit(solution)/shard_map/ppermute | solution.py:31
  776.9 81.1 %collective-permute-start.80 = (bf16[1024,2048]{1,0:T(8,128)(2,1)}, bf16[1024,2048]{1,0:T(8,128)(2,1)}, u32[]{:S(2)}, u32[]{:S(2)}) collective-permute-start(bf16[1024,2048]{1,0:T(8,128)(2,1)} %get-tuple-element.174), channel_id=1, source_target_pairs={{0,4},{4,0},{8,12},{12,8},{16,20},{20,16},{24,28},{28,24},{1,5},{5... | collective-permute-start | bytes 12582920 | tf_op jit(solution)/shard_map/ppermute | solution.py:31
  865.6 511.6 %reduce-scatter.11.cloned.1.call-start = ((), (), s32[]{:S(2)}) async-start(), calls=%async_computation.14 | async-start | bytes 5242880 | tf_op jit(solution)/shard_map/reduce_scatter | solution.py:630
  893.9 483.3 %reduce-scatter.9.cloned.1.call-start = ((), (), s32[]{:S(2)}) async-start(), calls=%async_computation.13 | async-start | bytes 5242880 | tf_op jit(solution)/shard_map/reduce_scatter | solution.py:630
  898.7 121.5 %collective-permute-start.60 = (bf16[256,2048]{1,0:T(8,128)(2,1)}, bf16[256,2048]{1,0:T(8,128)(2,1)}, u32[]{:S(2)}, u32[]{:S(2)}) collective-permute-start(bf16[256,2048]{1,0:T(8,128)(2,1)} %pad_maximum_fusion.6), channel_id=1, source_target_pairs={{0,24},{4,28},{8,0},{12,4},{16,8},{20,12},{24,16},{28,20},{1,25},{... | collective-permute-start | bytes 3145736 | tf_op jit(solution)/shard_map/ppermute | solution.py:39
  948.2 71.9 %collective-permute-start.63 = (bf16[256,2048]{1,0:T(8,128)(2,1)}, bf16[256,2048]{1,0:T(8,128)(2,1)}, u32[]{:S(2)}, u32[]{:S(2)}) collective-permute-start(bf16[256,2048]{1,0:T(8,128)(2,1)} %pad_maximum_fusion.7), channel_id=1, source_target_pairs={{0,8},{4,12},{8,16},{12,20},{16,24},{20,28},{24,0},{28,4},{1,9},{5... | collective-permute-start | bytes 3145736 | tf_op jit(solution)/shard_map/ppermute | solution.py:39
  1003.3 386.0 %reduce-scatter.5.cloned.1.call-start = ((), (), s32[]{:S(2)}) async-start(), calls=%async_computation.11 | async-start | bytes 5242880 | tf_op jit(solution)/shard_map/reduce_scatter | solution.py:630
  1037.9 59.3 %collective-permute-start.77 = (bf16[128,2048]{1,0:T(8,128)(2,1)S(1)}, bf16[128,2048]{1,0:T(8,128)(2,1)S(1)}, u32[]{:S(2)}, u32[]{:S(2)}) collective-permute-start(bf16[128,2048]{1,0:T(8,128)(2,1)S(1)} %get-tuple-element.283), channel_id=1, source_target_pairs={{0,2},{1,3},{2,0},{3,1},{4,6},{5,7},{6,4},{7,5},{8,10},{9,11},{10,... | collective-permute-start | bytes 1572872 | tf_op jit(solution)/shard_map/ppermute | solution.py:56
  1038.5 61.7 %collective-permute-start.75 = (bf16[128,2048]{1,0:T(8,128)(2,1)S(1)}, bf16[128,2048]{1,0:T(8,128)(2,1)S(1)}, u32[]{:S(2)}, u32[]{:S(2)}) collective-permute-start(bf16[128,2048]{1,0:T(8,128)(2,1)S(1)} %get-tuple-element.283), channel_id=1, source_target_pairs={{0,1},{1,0},{2,3},{3,2},{4,5},{5,4},{6,7},{7,6},{8,9},{9,8},{10,11... | collective-permute-start | bytes 1572872 | tf_op jit(solution)/shard_map/ppermute | solution.py:56
  1308.9 63.1 %collective-permute-start.112 = (f32[3,256]{1,0:T(4,128)S(1)}, f32[3,256]{1,0:T(4,128)S(1)}, u32[]{:S(2)}, u32[]{:S(2)}) collective-permute-start(f32[3,256]{1,0:T(4,128)S(1)} %fusion.110), channel_id=1, source_target_pairs={{0,3},{1,2},{2,1},{3,0},{4,7},{5,6},{6,5},{7,4},{8,11},{9,10},{10,... | collective-permute-start | bytes 9224 | tf_op jit(solution)/shard_map/ppermute | solution.py:56
  1314.6 63.1 %collective-permute-start.114 = (bf16[256,1536]{1,0:T(8,128)(2,1)}, bf16[256,1536]{1,0:T(8,128)(2,1)S(1)}, u32[]{:S(2)}, u32[]{:S(2)}) collective-permute-start(bf16[256,1536]{1,0:T(8,128)(2,1)} %get-tuple-element.211), channel_id=1, source_target_pairs={{0,8},{4,12},{8,16},{12,20},{16,24},{20,28},{24,0},{28,4},{1,9},{5... | collective-permute-start | bytes 2359304 | tf_op jit(solution)/shard_map/ppermute | solution.py:39
  1315.6 65.5 %collective-permute-start.116 = (bf16[256,1536]{1,0:T(8,128)(2,1)}, bf16[256,1536]{1,0:T(8,128)(2,1)}, u32[]{:S(2)}, u32[]{:S(2)}) collective-permute-start(bf16[256,1536]{1,0:T(8,128)(2,1)} %get-tuple-element.212), channel_id=1, source_target_pairs={{0,24},{4,28},{8,0},{12,4},{16,8},{20,12},{24,16},{28,20},{1,25},{... | collective-permute-start | bytes 2359304 | tf_op jit(solution)/shard_map/ppermute | solution.py:39
  1318.4 67.1 %collective-permute-start.115 = (bf16[256,1536]{1,0:T(8,128)(2,1)}, bf16[256,1536]{1,0:T(8,128)(2,1)}, u32[]{:S(2)}, u32[]{:S(2)}) collective-permute-start(bf16[256,1536]{1,0:T(8,128)(2,1)} %get-tuple-element.213), channel_id=1, source_target_pairs={{0,16},{4,20},{8,24},{12,28},{16,0},{20,4},{24,8},{28,12},{1,17},{... | collective-permute-start | bytes 2359304 | tf_op jit(solution)/shard_map/ppermute | solution.py:39
  1377.6 96.4 %collective-permute-start.99 = (bf16[256,2048]{1,0:T(8,128)(2,1)}, bf16[256,2048]{1,0:T(8,128)(2,1)}, u32[]{:S(2)}, u32[]{:S(2)}) collective-permute-start(bf16[256,2048]{1,0:T(8,128)(2,1)} %reduce-scatter.11.cloned.1.call-done), channel_id=1, source_target_pairs={{0,16},{4,20},{8,24},{12,28},{16,0},{20,4},{24,8},{28,12},{1,17},{... | collective-permute-start | bytes 3145736 | tf_op jit(solution)/shard_map/ppermute | solution.py:39
  (231 other events, 4441.4 us)
Sparse Core Ops, SparseCore 0:
  12.8 85.1 all-gather.7
  99.9 51.2 all-gather.9
  162.6 113.2 all-gather.17
  279.3 95.3 all-gather.15
  376.4 54.8 all-gather.13
  433.0 52.6 all-gather.19
  497.9 58.1 all-gather.11
  865.7 53.7 reduce-scatter.6
  922.7 64.9 reduce-scatter.10
  1003.4 62.5 reduce-scatter.8
  1238.1 72.8 reduce-scatter.4

commit v4 on v3

--- a/solution.py
+++ b/solution.py
@@ -570,7 +570,6 @@
     grad_sets = [grad_products(grad_own[None])]
     if nodes > 1:
         grad_sets.append(grad_group(groups[1], attn_blocks[0]))
-    attn_sum = after(attn_sum, *grad_sets[0][2:])
     hidden_res = residual_in + attn_sum
     normed_two, scale_two = norm_rows(hidden_res)
     second_in = (normed_two * moe_gain).astype(BF16)
@@ -593,8 +592,9 @@
         axis=1,
     )
 
-    sources = around_nodes(sent)
-    owns = {0: gather_pieces(sent)}
+    sent = after(sent, *grad_sets[0][2:])
+    owns = {0: gather_halves(sent)}
+    sources = around_nodes(after(sent, owns[0]))
     for step in order[1:]:
         owns[step] = None if step == 2 else lax.all_gather(
             sources[step - 1], "tp", axis=0, tiled=True
@@ -637,7 +637,6 @@
             own = after(own, *hops[place - 2][2])
             other = after(other, *lasts[place - 2])
         if place == 0:
-            own = after(own, *sources[:1], *sources[2:])
             first = one_sequence(place, False, own)
             second = one_sequence(place, True, other)
             mine, others = first, second
@@ -659,7 +658,9 @@
         backs.append(mine[0])
         swaps.append(swap_core(others[0]))
         outs.append((mine[1], others[1]))
-        if by_hops:
+        if by_hops and defer and place == nodes - 1:
+            hops.append(hop_one(mine[0], swaps[-1]))
+        elif by_hops:
             hops.append(hop_one(mine[0], swaps[-1]))
             lasts.append(hop_two(*hops[-1]))
             returns.append(shift_node(hop_sum(*hops[-1], lasts[-1]).astype(BF16), -step))
@@ -670,20 +671,31 @@
         if not defer:
             outs_back += [shift_node(outputs_home(outs[place])[0], -step)]
             kept = after(kept, outs_back[-1], returns[-1])
-    if defer:
-        pins = lasts[-1] if by_hops else (returns[-1],)
-        for place in range(nodes):
-            outs_back += outputs_home(outs[place], *pins)
     hidden_kept, gate_kept, up_kept, rows_kept = kept
 
     down_w_grad = down_products(hidden_kept, 0, [one[0] for one in grad_sets])
-    pins = hops[-1][2] if by_hops else ()
+    pins = ()
+    if by_hops and defer:
+        part, half, arrived = hops[-1]
+        arrived = tuple(after(one, down_w_grad) for one in arrived)
+        last = hop_two(part, half, arrived)
+        pins = arrived
     down_w_grad = down_products(
         after(hidden_kept, *pins), nodes, [one[1] for one in grad_sets], down_w_grad
     )
-    if by_hops and nodes > 1:
-        returns[-1] = after(returns[-1], down_w_grad)
-
+    if by_hops and defer:
+        last = tuple(after(one, down_w_grad) for one in last)
+        returns.append(shift_node(hop_sum(part, half, arrived, last).astype(BF16), -order[-1]))
+    if defer:
+        pins = last if by_hops else (returns[-1],)
+        wholes = [plus(after(own, *pins), swap_core(other)).astype(BF16) for own, other in outs]
+        pair = lax.psum_scatter(
+            jnp.stack(wholes[:2]), "tp", scatter_dimension=1, tiled=True
+        )
+        outs_back = list(pair) + [
+            lax.psum_scatter(whole, "tp", scatter_dimension=0, tiled=True)
+            for whole in wholes[2:]
+        ]
     back_sum = sum(one.astype(F32) for one in returns)
 
     def home(place, *earlier):
@@ -785,10 +797,10 @@
     first_part = dot_nt(qkv_grad, qkv_w).astype(BF16)
     first_grad = scatter_halves(first_part)
     for place in range(nodes):
-        home(place, query_blocks_grad[0] if place == 1 else first_part)
+        home(place, (heads_grad, heads_grad, query_blocks_grad[-1], first_grad)[min(place, 3)])
     output = (hidden_res + sum(one.astype(F32) for one in outs_back)).astype(BF16)
     qkv_w_grad = dot_tn(first_all, qkv_grad).astype(BF16)
-    up_w_grad = wide_products(rows_kept, after(up_kept, first_part, qkv_w_grad), local_experts)
+    up_w_grad = wide_products(rows_kept, after(up_kept, first_part, qkv_w_grad, outs_back[0]), local_experts)
     down_w_grad = down_w_grad.reshape(local_experts, hidden_slice, model_width)
 
     attn_gain_grad = jnp.sum(normed_one * first_grad, axis=0)

time: 1500 us -> 1520 us (1.013)
    ppermute x30, waiting for transfers between devices: 224 us -> 262 us  [shift_node(): lax.ppermute(operand, 'fsdp', [(i, (i // 2 + step) % nodes * 2 + i % 2) f...]
    ppermute x66 -> x69, waiting for transfers between devices: 302 us -> 271 us  [swap_tp(): return lax.ppermute(operand, 'tp', [(i, i ^ mask) for i in range(count)])]
    convert_element_type x5 -> x4, other arithmetic: 32.6 us -> 26.8 us  [shards(): plus(after(own, *pins), swap_core(other)).astype(BF16)]
    ppermute x66 -> x69, starting transfers between devices: 80.8 us -> 79.5 us  [swap_tp(): return lax.ppermute(operand, 'tp', [(i, i ^ mask) for i in range(count)])]
  transfers between devices with their start and end apart: 128 -> 130, of which waited for: 61 -> 67; matrix products, arithmetic and copies ran while one was open for 23% -> 23% of each run, Pallas kernels for 27% -> 27%
where the time goes in v4:
time: 1520 us; the launch traced here: 1500 us
  waiting for transfers between devices  577 us (38%)
  Pallas kernels  404 us (27%)
  matrix products  152 us (10%)
  other arithmetic  139 us (9%)
  starting transfers between devices  124 us (8%)
  local copies, waits for them, and re-layouts  85.6 us (6%)
  between operations  17.3 us (1%)
    ppermute x69, waiting for transfers between devices, swap_tp(): return lax.ppermute(operand, 'tp', [(i, i ^ mask) for i in range(count)])  271 us
    ppermute x30, waiting for transfers between devices, shift_node(): lax.ppermute(operand, 'fsdp', [(i, (i // 2 + step) % nodes * 2 + i % 2) f...  262 us
    pallas_call x8, Pallas kernels, expert_products(): pl.pallas_call(functools.partial(expert_kernel, extra, experts), out_shap...  242 us
    pallas_call x2, Pallas kernels, wide_products(): pl.pallas_call(wide_kernel, out_shape=jax.ShapeDtypeStruct((count, width,...  106 us
    ppermute x69, starting transfers between devices, swap_tp(): return lax.ppermute(operand, 'tp', [(i, i ^ mask) for i in range(count)])  79.5 us
    dot_general x9, matrix products, dot_nt(): lax.dot_general(a, b, (((1,), (1,)), ((), ())), preferred_element_type=F32)  68.6 us
    pallas_call x2, Pallas kernels, down_products(): pl.pallas_call(functools.partial(down_kernel, spans, first is not None),...  56.3 us
    ppermute x30, starting transfers between devices, shift_node(): lax.ppermute(operand, 'fsdp', [(i, (i // 2 + step) % nodes * 2 + i % 2) f...  39.5 us
  transfers between devices with their start and end apart: 130, of which 67 were waited for; matrix products, arithmetic and copies ran while one was open for 23% of the time, Pallas kernels for 27%

profile of v4, /device:TPU:0, one launch (start us, length us, event | category | flops | bytes accessed | tf_op | source)
XLA Modules:
  0.0 1499.4 jit_solution(13976840162354547773)
XLA Ops:
  64.7 33.3 %all-gather.8.cloned.1.call-done = bf16[2048,2048]{0,1:T(8,128)(2,1)} async-done(((bf16[256,2048]{0,1:T(8,128)(2,1)}), bf16[2048,2048]{0,1:T(8,128)(2,1)}) %all-gather.8.cloned.1.call-update) | async-done | bytes 8388624 | tf_op jit(solution)/shard_map/all_gather | solution.py:494
  138.3 21.0 %collective-permute-done.13 = bf16[256,2048]{1,0:T(8,128)(2,1)} collective-permute-done((bf16[256,2048]{1,0:T(8,128)(2,1)S(1)}, bf16[256,2048]{1,0:T(8,128)(2,1)}, u32[]{:S(2)}, u32[]{:S(2)}) %collective-permute-start.13) | collective-permute-done | bytes 1048608 | tf_op jit(solution)/shard_map/ppermute | solution.py:39
  183.9 22.6 %collective-permute-done.16 = bf16[128,2048]{1,0:T(8,128)(2,1)S(1)} collective-permute-done((bf16[128,2048]{1,0:T(8,128)(2,1)S(1)}, bf16[128,2048]{1,0:T(8,128)(2,1)S(1)}, u32[]{:S(2)}, u32[]{:S(2)}) %collective-permute-start.16) | collective-permute-done | bytes 524320 | tf_op jit(solution)/shard_map/ppermute | solution.py:56
  225.1 17.8 %collective-permute-done.18 = bf16[128,2048]{1,0:T(8,128)(2,1)} collective-permute-done((bf16[128,2048]{1,0:T(8,128)(2,1)}, bf16[128,2048]{1,0:T(8,128)(2,1)}, u32[]{:S(2)}, u32[]{:S(2)}) %collective-permute-start.18) | collective-permute-done | bytes 524320 | tf_op jit(solution)/shard_map/ppermute | solution.py:56
  261.6 19.8 %collective-permute-done.24 = bf16[128,2176]{1,0:T(8,128)(2,1)S(1)} collective-permute-done((bf16[128,2176]{1,0:T(8,128)(2,1)S(1)}, bf16[128,2176]{1,0:T(8,128)(2,1)S(1)}, u32[]{:S(2)}, u32[]{:S(2)}) %collective-permute-start.24) | collective-permute-done | bytes 557088 | tf_op jit(solution)/shard_map/ppermute | solution.py:56
  285.3 16.0 %collective-permute-done.22 = bf16[128,2176]{1,0:T(8,128)(2,1)S(1)} collective-permute-done((bf16[128,2176]{1,0:T(8,128)(2,1)S(1)}, bf16[128,2176]{1,0:T(8,128)(2,1)S(1)}, u32[]{:S(2)}, u32[]{:S(2)}) %collective-permute-start.22) | collective-permute-done | bytes 557088 | tf_op jit(solution)/shard_map/ppermute | solution.py:56
  315.0 25.7 %collective-permute-done.27 = bf16[256,2176]{1,0:T(8,128)(2,1)S(1)} collective-permute-done((bf16[256,2176]{1,0:T(8,128)(2,1)S(1)}, bf16[256,2176]{1,0:T(8,128)(2,1)S(1)}, u32[]{:S(2)}, u32[]{:S(2)}) %collective-permute-start.27) | collective-permute-done | bytes 1114144 | tf_op jit(solution)/shard_map/ppermute | solution.py:39
  343.6 22.7 %collective-permute-done.31 = bf16[256,2176]{1,0:T(8,128)(2,1)S(1)} collective-permute-done((bf16[256,2176]{1,0:T(8,128)(2,1)S(1)}, bf16[256,2176]{1,0:T(8,128)(2,1)S(1)}, u32[]{:S(2)}, u32[]{:S(2)}) %collective-permute-start.31) | collective-permute-done | bytes 1114144 | tf_op jit(solution)/shard_map/ppermute | solution.py:39
  378.4 30.2 %shard_map.254 = (bf16[1024,2048]{1,0:T(8,128)(2,1)}, bf16[1024,2048]{1,0:T(8,128)(2,1)}, f32[1024,128]{1,0:T(8,128)}, bf16[8,1024,1024]{2,1,0:T(8,128)(2,1)}, b...) custom-call(s32[1]{0:T(128)} %bitcast.16.base, ...), custom_call_target="tpu_custom_call" | custom-call | flops 21474836480 | bytes 37748736 | tf_op jit(solution)/shard_map/pallas_call | solution.py:303
  419.2 30.2 %shard_map.255 = (bf16[1024,2048]{1,0:T(8,128)(2,1)}, bf16[1024,2048]{1,0:T(8,128)(2,1)}, f32[1024,128]{1,0:T(8,128)}, bf16[8,1024,1024]{2,1,0:T(8,128)(2,1)}, b...) custom-call(s32[1]{0:T(128)} %bitcast.16.base, ...), custom_call_target="tpu_custom_call", output_to_operand_aliasing={{3}: (6, {}), {4}: (7, {}), {5}: (8, {}), {6}: (9, {})} | custom-call | flops 21474836480 | bytes 37748736 | tf_op jit(solution)/shard_map/pallas_call | solution.py:303
  451.4 27.3 %collective-permute-done.28 = bf16[256,2176]{1,0:T(8,128)(2,1)S(1)} collective-permute-done((bf16[256,2176]{1,0:T(8,128)(2,1)S(1)}, bf16[256,2176]{1,0:T(8,128)(2,1)S(1)}, u32[]{:S(2)}, u32[]{:S(2)}) %collective-permute-start.28) | collective-permute-done | bytes 1114144 | tf_op jit(solution)/shard_map/ppermute | solution.py:39
  485.0 11.3 convolution_convert_fusion.2
  498.8 30.1 %shard_map.256 = (bf16[1024,2048]{1,0:T(8,128)(2,1)}, bf16[1024,2048]{1,0:T(8,128)(2,1)}, f32[1024,128]{1,0:T(8,128)}, bf16[8,1024,1024]{2,1,0:T(8,128)(2,1)}, b...) custom-call(s32[1]{0:T(128)} %bitcast.16.base, ...), custom_call_target="tpu_custom_call", output_to_operand_aliasing={{3}: (6, {}), {4}: (7, {}), {5}: (8, {}), {6}: (9, {})} | custom-call | flops 21474836480 | bytes 37748736 | tf_op jit(solution)/shard_map/pallas_call | solution.py:303
  528.9 13.0 convolution_convert_fusion.1
  550.3 12.9 collective-permute-done.41
  569.0 30.2 %shard_map.257 = (bf16[1024,2048]{1,0:T(8,128)(2,1)}, bf16[1024,2048]{1,0:T(8,128)(2,1)}, f32[1024,128]{1,0:T(8,128)}, bf16[8,1024,1024]{2,1,0:T(8,128)(2,1)}, b...) custom-call(s32[1]{0:T(128)} %bitcast.16.base, ...), custom_call_target="tpu_custom_call", output_to_operand_aliasing={{3}: (6, {}), {4}: (7, {}), {5}: (8, {}), {6}: (9, {})} | custom-call | flops 21474836480 | bytes 37748736 | tf_op jit(solution)/shard_map/pallas_call | solution.py:303
  599.3 30.4 %shard_map.258 = (bf16[1024,2048]{1,0:T(8,128)(2,1)}, bf16[1024,2048]{1,0:T(8,128)(2,1)}, f32[1024,128]{1,0:T(8,128)}, bf16[8,1024,1024]{2,1,0:T(8,128)(2,1)}, b...) custom-call(s32[1]{0:T(128)} %bitcast.16.base, ...), custom_call_target="tpu_custom_call", output_to_operand_aliasing={{3}: (6, {}), {4}: (7, {}), {5}: (8, {}), {6}: (9, {})} | custom-call | flops 21474836480 | bytes 37748736 | tf_op jit(solution)/shard_map/pallas_call | solution.py:303
  633.9 12.3 collective-permute-done.44
  666.1 30.4 %shard_map.259 = (bf16[1024,2048]{1,0:T(8,128)(2,1)}, bf16[1024,2048]{1,0:T(8,128)(2,1)}, f32[1024,128]{1,0:T(8,128)}, bf16[8,1024,1024]{2,1,0:T(8,128)(2,1)}, b...) custom-call(s32[1]{0:T(128)} %bitcast.16.base, ...), custom_call_target="tpu_custom_call", output_to_operand_aliasing={{3}: (6, {}), {4}: (7, {}), {5}: (8, {}), {6}: (9, {})} | custom-call | flops 21474836480 | bytes 37748736 | tf_op jit(solution)/shard_map/pallas_call | solution.py:303
  698.0 30.8 %shard_map.260 = (bf16[1024,2048]{1,0:T(8,128)(2,1)}, bf16[1024,2048]{1,0:T(8,128)(2,1)}, f32[1024,128]{1,0:T(8,128)}, bf16[8,1024,1024]{2,1,0:T(8,128)(2,1)}, b...) custom-call(s32[1]{0:T(128)} %bitcast.16.base, ...), custom_call_target="tpu_custom_call", output_to_operand_aliasing={{3}: (6, {}), {4}: (7, {}), {5}: (8, {}), {6}: (9, {})} | custom-call | flops 21474836480 | bytes 37748736 | tf_op jit(solution)/shard_map/pallas_call | solution.py:303
  774.5 30.1 %shard_map.261 = (bf16[1024,2048]{1,0:T(8,128)(2,1)}, bf16[1024,2048]{1,0:T(8,128)(2,1)}, f32[1024,128]{1,0:T(8,128)}, bf16[8,1024,1024]{2,1,0:T(8,128)(2,1)}, b...) custom-call(s32[1]{0:T(128)} %bitcast.16.base, ...), custom_call_target="tpu_custom_call", output_to_operand_aliasing={{3}: (6, {}), {4}: (7, {}), {5}: (8, {}), {6}: (9, {})} | custom-call | flops 21474836480 | bytes 37748736 | tf_op jit(solution)/shard_map/pallas_call | solution.py:303
  807.6 27.0 %shard_map.262.refs_3_ = f32[1024,2048]{1,0:T(8,128)} custom-call(bf16[8,1024,1024]{2,1,0:T(8,128)(2,1)} %get-tuple-element.168.left, bf16[1,1024,2048]{2,1,0:T(8,128)(2,1)} %bitcast.449, bf16[2,1024,2048]{2,1,0:T(8,128)(2,1)} %all-gather.18.cloned.1.call-done.refs_1_, bf16[1,1024,2048]{2,1,0:T(8,128)(2,1)} %all-gather.20.cloned.1.call-done.refs_2_), custom_call_target="tpu_custom_call" | custom-call | flops 17179869184 | bytes 33554432 | tf_op jit(solution)/shard_map/pallas_call | solution.py:407
  867.4 29.4 %shard_map.263 = f32[1024,2048]{1,0:T(8,128)} custom-call(bf16[8,1024,1024]{2,1,0:T(8,128)(2,1)} %get-tuple-element.168.left, bf16[1,1024,2048]{2,1,0:T(8,128)(2,1)} %collective-permute-done.30.refs_0_, bf16[2,1024,2048]{2,1,0:T(8,128)(2,1)} %collective-permute-done.33.refs_1_, bf16[1,1024,2048]{2,1,0:T(8,128)(2,1)} %collective-permute-done.56.refs_2_, ...), custom_call_target="tpu_custom_call" | custom-call | flops 17179869184 | bytes 33554432 | tf_op jit(solution)/shard_map/pallas_call | solution.py:407
  941.9 17.7 %collective-permute-done.72 = f32[4,8,256]{2,1,0:T(8,128)S(1)} collective-permute-done((f32[4,8,256]{2,1,0:T(8,128)S(1)}, f32[4,8,256]{2,1,0:T(8,128)S(1)}, u32[]{:S(2)}, u32[]{:S(2)}) %collective-permute-start.72) | collective-permute-done | bytes 32800 | tf_op jit(solution)/shard_map/ppermute | solution.py:56
  993.2 22.7 %collective-permute-done.69 = bf16[256,2048]{1,0:T(8,128)(2,1)} collective-permute-done((bf16[256,2048]{1,0:T(8,128)(2,1)}, bf16[256,2048]{1,0:T(8,128)(2,1)}, u32[]{:S(2)}, u32[]{:S(2)}) %collective-permute-start.69) | collective-permute-done | bytes 1048608 | tf_op jit(solution)/shard_map/ppermute | solution.py:39
  1015.9 42.3 %collective-permute-done.70 = bf16[256,2048]{1,0:T(8,128)(2,1)} collective-permute-done((bf16[256,2048]{1,0:T(8,128)(2,1)}, bf16[256,2048]{1,0:T(8,128)(2,1)}, u32[]{:S(2)}, u32[]{:S(2)}) %collective-permute-start.70) | collective-permute-done | bytes 1048608 | tf_op jit(solution)/shard_map/ppermute | solution.py:39
  1082.3 52.9 %shard_map.264 = f32[4,2048,256]{2,1,0:T(8,128)} custom-call(bf16[8,2048,1024]{2,1,0:T(8,128)(2,1)} %get-tuple-element.184.left, bf16[8,1024,1024]{2,1,0:T(8,128)(2,1)} %get-tuple-element.192.right), custom_call_target="tpu_custom_call" | custom-call | flops 34359738368 | bytes 58720256 | tf_op jit(solution)/shard_map/pallas_call | solution.py:353
  1299.0 11.2 collective-permute-done.104
  1348.0 12.5 collective-permute-done.117
  1360.5 12.7 collective-permute-done.119
  1373.2 34.4 %collective-permute-done.118 = bf16[256,1536]{1,0:T(8,128)(2,1)S(1)} collective-permute-done((bf16[256,1536]{1,0:T(8,128)(2,1)S(1)}, bf16[256,1536]{1,0:T(8,128)(2,1)S(1)}, u32[]{:S(2)}, u32[]{:S(2)}) %collective-permute-start.118) | collective-permute-done | bytes 786464 | tf_op jit(solution)/shard_map/ppermute | solution.py:39
  1417.7 52.8 %shard_map.265 = f32[4,2048,256]{2,1,0:T(8,128)} custom-call(bf16[8,2048,1024]{2,1,0:T(8,128)(2,1)} %get-tuple-element.184.left, bf16[8,1024,1024]{2,1,0:T(8,128)(2,1)} %get-tuple-element.201.right), custom_call_target="tpu_custom_call" | custom-call | flops 34359738368 | bytes 58720256 | tf_op jit(solution)/shard_map/pallas_call | solution.py:353
  (769 shorter events, 668.6 us)
Async XLA Ops:
  7.3 90.8 %all-gather.8.cloned.1.call-start = ((), (), s32[]{:S(2)}) async-start(), calls=%async_computation.3 | async-start | bytes 9437184 | tf_op jit(solution)/shard_map/all_gather | solution.py:494
  12.7 162.3 %all-gather.10.cloned.1.call-start = ((), (), s32[]{:S(2)}) async-start(), calls=%async_computation.4 | async-start | bytes 5242880 | tf_op jit(solution)/shard_map/all_gather | solution.py:507
  98.1 280.2 %all-gather.18.cloned.1.call-start = ((), (), s32[]{:S(2)}) async-start(), calls=%async_computation.8 | async-start | bytes 10485760 | tf_op jit(solution)/shard_map/all_gather | solution.py:567
  162.5 287.3 %all-gather.16.cloned.1.call-start = ((), (), s32[]{:S(2)}) async-start(), calls=%async_computation.7 | async-start | bytes 5570560 | tf_op jit(solution)/shard_map/all_gather | solution.py:599
  341.8 187.1 %all-gather.14.cloned.1.call-start = ((), (), s32[]{:S(2)}) async-start(), calls=%async_computation.6 | async-start | bytes 5570560 | tf_op jit(solution)/shard_map/all_gather | solution.py:599
  367.4 180.1 %all-gather.20.cloned.1.call-start = ((), (), s32[]{:S(2)}) async-start(), calls=%async_computation.9 | async-start | bytes 5242880 | tf_op jit(solution)/shard_map/all_gather | solution.py:567
  378.2 106.8 %collective-permute-start.33 = (bf16[2,1024,2048]{2,1,0:T(8,128)(2,1)}, bf16[2,1024,2048]{2,1,0:T(8,128)(2,1)}, u32[]{:S(2)}, u32[]{:S(2)}) collective-permute-start(bf16[2,1024,2048]{2,1,0:T(8,128)(2,1)} %all-gather.18.cloned.1.call-done.refs_1_), channel_id=1, source_target_pairs={{0,4},{4,0},{8,12},{12,8},{16,20},{20,16},{24,28},{28,24},{1,5},{5... | collective-permute-start | bytes 25165832 | tf_op jit(solution)/shard_map/ppermute | solution.py:31
  409.7 220.1 %all-gather.12.cloned.1.call-start = ((), (), s32[]{:S(2)}) async-start(), calls=%async_computation.5 | async-start | bytes 5570560 | tf_op jit(solution)/shard_map/all_gather | solution.py:646
  479.8 930.8 %reduce-scatter.8.cloned.1.call-start = ((), (), s32[]{:S(2)}) async-start(), calls=%async_computation.12 | async-start | bytes 5242880 | tf_op jit(solution)/shard_map/reduce_scatter | solution.py:696
  483.9 63.6 %collective-permute-start.38 = (bf16[128,2048]{1,0:T(8,128)(2,1)S(1)}, bf16[128,2048]{1,0:T(8,128)(2,1)S(1)}, u32[]{:S(2)}, u32[]{:S(2)}) collective-permute-start(bf16[128,2048]{1,0:T(8,128)(2,1)S(1)} %get-tuple-element.248), channel_id=1, source_target_pairs={{0,1},{1,0},{2,3},{3,2},{4,5},{5,4},{6,7},{7,6},{8,9},{9,8},{10,11... | collective-permute-start | bytes 1572872 | tf_op jit(solution)/shard_map/ppermute | solution.py:56
  485.0 62.5 %collective-permute-start.36 = (bf16[128,2048]{1,0:T(8,128)(2,1)S(1)}, bf16[128,2048]{1,0:T(8,128)(2,1)S(1)}, u32[]{:S(2)}, u32[]{:S(2)}) collective-permute-start(bf16[128,2048]{1,0:T(8,128)(2,1)S(1)} %get-tuple-element.249), channel_id=1, source_target_pairs={{0,2},{1,3},{2,0},{3,1},{4,6},{5,7},{6,4},{7,5},{8,10},{9,11},{10,... | collective-permute-start | bytes 1572872 | tf_op jit(solution)/shard_map/ppermute | solution.py:56
  528.9 70.4 %collective-permute-start.34 = (bf16[1024,2176]{1,0:T(8,128)(2,1)}, bf16[1024,2176]{1,0:T(8,128)(2,1)}, u32[]{:S(2)}, u32[]{:S(2)}) collective-permute-start(bf16[1024,2176]{1,0:T(8,128)(2,1)} %all-gather.14.cloned.1.call-done.refs_0_), channel_id=1, source_target_pairs={{0,4},{4,0},{8,12},{12,8},{16,20},{20,16},{24,28},{28,24},{1,5},{5... | collective-permute-start | bytes 13369352 | tf_op jit(solution)/shard_map/ppermute | solution.py:31
  547.5 104.0 %collective-permute-start.56 = (bf16[1,1024,2048]{2,1,0:T(8,128)(2,1)}, bf16[1,1024,2048]{2,1,0:T(8,128)(2,1)}, u32[]{:S(2)}, u32[]{:S(2)}) collective-permute-start(bf16[1,1024,2048]{2,1,0:T(8,128)(2,1)} %all-gather.20.cloned.1.call-done.refs_2_), channel_id=1, source_target_pairs={{0,4},{4,0},{8,12},{12,8},{16,20},{20,16},{24,28},{28,24},{1,5},{5... | collective-permute-start | bytes 12582920 | tf_op jit(solution)/shard_map/ppermute | solution.py:31
  547.5 82.8 %collective-permute-start.42 = (bf16[1024,2048]{1,0:T(8,128)(2,1)}, bf16[1024,2048]{1,0:T(8,128)(2,1)}, u32[]{:S(2)}, u32[]{:S(2)}) collective-permute-start(bf16[1024,2048]{1,0:T(8,128)(2,1)} %get-tuple-element.126), channel_id=1, source_target_pairs={{0,4},{4,0},{8,12},{12,8},{16,20},{20,16},{24,28},{28,24},{1,5},{5... | collective-permute-start | bytes 12582920 | tf_op jit(solution)/shard_map/ppermute | solution.py:31
  629.7 66.8 %collective-permute-start.47 = (bf16[1024,2048]{1,0:T(8,128)(2,1)}, bf16[1024,2048]{1,0:T(8,128)(2,1)}, u32[]{:S(2)}, u32[]{:S(2)}) collective-permute-start(bf16[1024,2048]{1,0:T(8,128)(2,1)} %get-tuple-element.138), channel_id=1, source_target_pairs={{0,4},{4,0},{8,12},{12,8},{16,20},{20,16},{24,28},{28,24},{1,5},{5... | collective-permute-start | bytes 12582920 | tf_op jit(solution)/shard_map/ppermute | solution.py:31
  629.8 68.2 %collective-permute-start.53 = (bf16[1024,2176]{1,0:T(8,128)(2,1)}, bf16[1024,2176]{1,0:T(8,128)(2,1)}, u32[]{:S(2)}, u32[]{:S(2)}) collective-permute-start(bf16[1024,2176]{1,0:T(8,128)(2,1)} %all-gather.12.cloned.1.call-done.refs_0_), channel_id=1, source_target_pairs={{0,4},{4,0},{8,12},{12,8},{16,20},{20,16},{24,28},{28,24},{1,5},{5... | collective-permute-start | bytes 13369352 | tf_op jit(solution)/shard_map/ppermute | solution.py:31
  728.8 75.8 %collective-permute-start.57 = (bf16[1024,2048]{1,0:T(8,128)(2,1)}, bf16[1024,2048]{1,0:T(8,128)(2,1)}, u32[]{:S(2)}, u32[]{:S(2)}) collective-permute-start(bf16[1024,2048]{1,0:T(8,128)(2,1)} %get-tuple-element.162), channel_id=1, source_target_pairs={{0,4},{4,0},{8,12},{12,8},{16,20},{20,16},{24,28},{28,24},{1,5},{5... | collective-permute-start | bytes 12582920 | tf_op jit(solution)/shard_map/ppermute | solution.py:31
  768.2 128.6 %collective-permute-start.85 = (bf16[1024,2048]{1,0:T(8,128)(2,1)}, bf16[1024,2048]{1,0:T(8,128)(2,1)}, u32[]{:S(2)}, u32[]{:S(2)}) collective-permute-start(bf16[1024,2048]{1,0:T(8,128)(2,1)} %get-tuple-element.191), channel_id=1, source_target_pairs={{0,4},{4,0},{8,12},{12,8},{16,20},{20,16},{24,28},{28,24},{1,5},{5... | collective-permute-start | bytes 12582920 | tf_op jit(solution)/shard_map/ppermute | solution.py:31
  840.2 56.5 %collective-permute-start.63 = (bf16[128,2048]{1,0:T(8,128)(2,1)S(1)}, bf16[128,2048]{1,0:T(8,128)(2,1)S(1)}, u32[]{:S(2)}, u32[]{:S(2)}) collective-permute-start(bf16[128,2048]{1,0:T(8,128)(2,1)S(1)} %get-tuple-element.236), channel_id=1, source_target_pairs={{0,2},{1,3},{2,0},{3,1},{4,6},{5,7},{6,4},{7,5},{8,10},{9,11},{10,... | collective-permute-start | bytes 1572872 | tf_op jit(solution)/shard_map/ppermute | solution.py:56
  904.9 505.7 %reduce-scatter.6.cloned.1.call-start = ((), (), s32[]{:S(2)}) async-start(), calls=%async_computation.11 | async-start | bytes 5242880 | tf_op jit(solution)/shard_map/reduce_scatter | solution.py:696
  920.9 491.2 %reduce-scatter.4.cloned.1.call-start = ((), (), s32[]{:S(2)}) async-start(), calls=%async_computation.10 | async-start | bytes 10485760 | tf_op jit(solution)/shard_map/reduce_scatter | solution.py:692
  922.5 58.4 %collective-permute-start.64 = (bf16[1024,2048]{1,0:T(8,128)(2,1)}, bf16[1024,2048]{1,0:T(8,128)(2,1)}, u32[]{:S(2)}, u32[]{:S(2)}) collective-permute-start(bf16[1024,2048]{1,0:T(8,128)(2,1)} %get-tuple-element.172), channel_id=1, source_target_pairs={{0,4},{4,0},{8,12},{12,8},{16,20},{20,16},{24,28},{28,24},{1,5},{5... | collective-permute-start | bytes 12582920 | tf_op jit(solution)/shard_map/ppermute | solution.py:31
  975.3 82.9 %collective-permute-start.70 = (bf16[256,2048]{1,0:T(8,128)(2,1)}, bf16[256,2048]{1,0:T(8,128)(2,1)}, u32[]{:S(2)}, u32[]{:S(2)}) collective-permute-start(bf16[256,2048]{1,0:T(8,128)(2,1)} %pad_maximum_fusion.8), channel_id=1, source_target_pairs={{0,16},{4,20},{8,24},{12,28},{16,0},{20,4},{24,8},{28,12},{1,17},{... | collective-permute-start | bytes 3145736 | tf_op jit(solution)/shard_map/ppermute | solution.py:39
  1077.6 58.8 %collective-permute-start.81 = (bf16[128,2048]{1,0:T(8,128)(2,1)S(1)}, bf16[128,2048]{1,0:T(8,128)(2,1)S(1)}, u32[]{:S(2)}, u32[]{:S(2)}) collective-permute-start(bf16[128,2048]{1,0:T(8,128)(2,1)S(1)} %get-tuple-element.298), channel_id=1, source_target_pairs={{0,2},{1,3},{2,0},{3,1},{4,6},{5,7},{6,4},{7,5},{8,10},{9,11},{10,... | collective-permute-start | bytes 1572872 | tf_op jit(solution)/shard_map/ppermute | solution.py:56
  1077.7 62.0 %collective-permute-start.79 = (bf16[128,2048]{1,0:T(8,128)(2,1)S(1)}, bf16[128,2048]{1,0:T(8,128)(2,1)S(1)}, u32[]{:S(2)}, u32[]{:S(2)}) collective-permute-start(bf16[128,2048]{1,0:T(8,128)(2,1)S(1)} %get-tuple-element.298), channel_id=1, source_target_pairs={{0,1},{1,0},{2,3},{3,2},{4,5},{5,4},{6,7},{7,6},{8,9},{9,8},{10,11... | collective-permute-start | bytes 1572872 | tf_op jit(solution)/shard_map/ppermute | solution.py:56
  1078.4 58.9 %collective-permute-start.78 = (bf16[128,2048]{1,0:T(8,128)(2,1)S(1)}, bf16[128,2048]{1,0:T(8,128)(2,1)S(1)}, u32[]{:S(2)}, u32[]{:S(2)}) collective-permute-start(bf16[128,2048]{1,0:T(8,128)(2,1)S(1)} %get-tuple-element.299), channel_id=1, source_target_pairs={{0,1},{1,0},{2,3},{3,2},{4,5},{5,4},{6,7},{7,6},{8,9},{9,8},{10,11... | collective-permute-start | bytes 1572872 | tf_op jit(solution)/shard_map/ppermute | solution.py:56
  1079.8 55.5 %collective-permute-start.92 = (f32[33,256]{1,0:T(8,128)S(1)}, f32[33,256]{1,0:T(8,128)S(1)}, u32[]{:S(2)}, u32[]{:S(2)}) collective-permute-start(f32[33,256]{1,0:T(8,128)S(1)} %fusion.99), channel_id=1, source_target_pairs={{0,2},{1,3},{2,0},{3,1},{4,6},{5,7},{6,4},{7,5},{8,10},{9,11},{10,... | collective-permute-start | bytes 101384 | tf_op jit(solution)/shard_map/ppermute | solution.py:56
  1081.7 54.7 %collective-permute-start.91 = (f32[33,256]{1,0:T(8,128)S(1)}, f32[33,256]{1,0:T(8,128)S(1)}, u32[]{:S(2)}, u32[]{:S(2)}) collective-permute-start(f32[33,256]{1,0:T(8,128)S(1)} %fusion.99), channel_id=1, source_target_pairs={{0,1},{1,0},{2,3},{3,2},{4,5},{5,4},{6,7},{7,6},{8,9},{9,8},{10,11... | collective-permute-start | bytes 101384 | tf_op jit(solution)/shard_map/ppermute | solution.py:56
  1342.3 65.3 %collective-permute-start.118 = (bf16[256,1536]{1,0:T(8,128)(2,1)S(1)}, bf16[256,1536]{1,0:T(8,128)(2,1)S(1)}, u32[]{:S(2)}, u32[]{:S(2)}) collective-permute-start(bf16[256,1536]{1,0:T(8,128)(2,1)S(1)} %get-tuple-element.223), channel_id=1, source_target_pairs={{0,16},{4,20},{8,24},{12,28},{16,0},{20,4},{24,8},{28,12},{1,17},{... | collective-permute-start | bytes 2359304 | tf_op jit(solution)/shard_map/ppermute | solution.py:39
  1410.6 67.2 %collective-permute-start.108 = (bf16[256,2048]{1,0:T(8,128)(2,1)}, bf16[256,2048]{1,0:T(8,128)(2,1)}, u32[]{:S(2)}, u32[]{:S(2)}) collective-permute-start(bf16[256,2048]{1,0:T(8,128)(2,1)} %reduce-scatter.8.cloned.1.call-done), channel_id=1, source_target_pairs={{0,16},{4,20},{8,24},{12,28},{16,0},{20,4},{24,8},{28,12},{1,17},{... | collective-permute-start | bytes 3145736 | tf_op jit(solution)/shard_map/ppermute | solution.py:39
  1410.6 67.2 %collective-permute-start.95 = (bf16[256,2048]{1,0:T(8,128)(2,1)}, bf16[256,2048]{1,0:T(8,128)(2,1)}, u32[]{:S(2)}, u32[]{:S(2)}) collective-permute-start(bf16[256,2048]{1,0:T(8,128)(2,1)} %reduce-scatter.6.cloned.1.call-done), channel_id=1, source_target_pairs={{0,8},{4,12},{8,16},{12,20},{16,24},{20,28},{24,0},{28,4},{1,9},{5... | collective-permute-start | bytes 3145736 | tf_op jit(solution)/shard_map/ppermute | solution.py:39
  1415.2 69.3 %collective-permute-start.86 = (bf16[256,2048]{1,0:T(8,128)(2,1)}, bf16[256,2048]{1,0:T(8,128)(2,1)}, u32[]{:S(2)}, u32[]{:S(2)}) collective-permute-start(bf16[256,2048]{1,0:T(8,128)(2,1)} %get-tuple-element.195), channel_id=1, source_target_pairs={{0,24},{4,28},{8,0},{12,4},{16,8},{20,12},{24,16},{28,20},{1,25},{... | collective-permute-start | bytes 3145736 | tf_op jit(solution)/shard_map/ppermute | solution.py:39
  (228 other events, 4336.3 us)
Sparse Core Ops, SparseCore 0:
  12.8 85.1 all-gather.7
  99.9 51.2 all-gather.9
  162.6 136.7 all-gather.17
  341.9 53.0 all-gather.15
  396.6 54.8 all-gather.13
  453.3 63.9 all-gather.19
  519.1 73.6 all-gather.11
  905.0 58.1 reduce-scatter.7
  966.4 51.4 reduce-scatter.5
  1020.8 106.2 reduce-scatter.3

commit v5 on v4

--- a/solution.py
+++ b/solution.py
@@ -431,7 +431,7 @@
     )
 
 
-def sum_rows(mine, arrived):
+def sum_rows(mine, arrived, *earlier):
     nodes = mine.shape[0]
     node = lax.axis_index("fsdp") // 2
 
@@ -442,9 +442,11 @@
             lax.dynamic_index_in_dim(arrived, place, 0, keepdims=False),
         )
 
-    total = part(0)
+    total, parts = part(0), []
     for step in range(1, nodes):
-        total = total + shift_node(part(step).astype(BF16), step).astype(F32)
+        parts.append(after(shift_node(part(step).astype(BF16), step), *earlier))
+    for one in parts:
+        total = total + one.astype(F32)
     return total
 
 
@@ -595,10 +597,6 @@
     sent = after(sent, *grad_sets[0][2:])
     owns = {0: gather_halves(sent)}
     sources = around_nodes(after(sent, owns[0]))
-    for step in order[1:]:
-        owns[step] = None if step == 2 else lax.all_gather(
-            sources[step - 1], "tp", axis=0, tiled=True
-        )
     defer = nodes <= 4
     by_hops = tp_count == 4
     kept, gate_dots, backs, swaps, hops, lasts, returns = (), [], [], [], [], [], []
@@ -633,31 +631,48 @@
     for place, step in enumerate(order):
         own = owns[step]
         other = swap_core(own)
-        if by_hops and place > 1:
-            own = after(own, *hops[place - 2][2])
-            other = after(other, *lasts[place - 2])
+        early, late = (other, own) if 0 < place == nodes - 1 else (own, other)
+        if by_hops and defer and place > 1:
+            early = after(early, *lasts[place - 2], wholes[place - 2])
+        if by_hops and place > 0:
+            late = after(late, *hops[place - 1][2])
+        if by_hops and defer and place == nodes - 1 and place > 2:
+            late = after(late, returns[place - 2])
         if place == 0:
-            first = one_sequence(place, False, own)
-            second = one_sequence(place, True, other)
+            first = one_sequence(place, False, early)
+            second = one_sequence(place, True, late)
             mine, others = first, second
+            for later in order[1:]:
+                if later != 2:
+                    owns[later] = lax.all_gather(
+                        after(sources[later - 1], first[0]), "tp", axis=0, tiled=True
+                    )
             if len(groups) > 2:
                 grad_sets.append(grad_group(groups[2], first[0]))
             if 2 in order:
                 owns[2] = lax.all_gather(
                     after(sources[1], second[0]), "tp", axis=0, tiled=True
                 )
+        elif place == nodes - 1:
+            first = one_sequence(place, True, early)
+            second = one_sequence(place, False, late)
+            mine, others = second, first
         else:
-            if by_hops:
-                own = after(own, *hops[place - 1][2])
-            first = one_sequence(place, True, other)
-            second = one_sequence(place, False, own)
-            mine, others = second, first
+            first = one_sequence(place, False, early)
+            second = one_sequence(place, True, late)
+            mine, others = first, second
         if place + 1 < nodes:
             owns[order[place + 1]] = after(owns[order[place + 1]], first[0])
         gate_dots.append((mine[2], others[2]))
         backs.append(mine[0])
         swaps.append(swap_core(others[0]))
         outs.append((mine[1], others[1]))
+        if defer:
+            out_swapped = swap_core(others[1])
+            if place < nodes - 2:
+                wholes.append(plus(mine[1], out_swapped).astype(BF16))
+            else:
+                wholes.append((mine[1], out_swapped))
         if by_hops and defer and place == nodes - 1:
             hops.append(hop_one(mine[0], swaps[-1]))
         elif by_hops:
@@ -674,12 +689,14 @@
     hidden_kept, gate_kept, up_kept, rows_kept = kept
 
     down_w_grad = down_products(hidden_kept, 0, [one[0] for one in grad_sets])
-    pins = ()
+    dots = jnp.stack([one[0] for one in gate_dots] + [one[1] for one in gate_dots], axis=1)
+    dots = scatter_dots(dots)
+    pins = (dots,)
     if by_hops and defer:
         part, half, arrived = hops[-1]
         arrived = tuple(after(one, down_w_grad) for one in arrived)
         last = hop_two(part, half, arrived)
-        pins = arrived
+        pins = arrived + (dots,)
     down_w_grad = down_products(
         after(hidden_kept, *pins), nodes, [one[1] for one in grad_sets], down_w_grad
     )
@@ -688,7 +705,12 @@
         returns.append(shift_node(hop_sum(part, half, arrived, last).astype(BF16), -order[-1]))
     if defer:
         pins = last if by_hops else (returns[-1],)
-        wholes = [plus(after(own, *pins), swap_core(other)).astype(BF16) for own, other in outs]
+        wholes = [
+            plus(after(one[0], *pins), one[1]).astype(BF16)
+            if isinstance(one, tuple)
+            else after(one, *pins)
+            for one in wholes
+        ]
         pair = lax.psum_scatter(
             jnp.stack(wholes[:2]), "tp", scatter_dimension=1, tiled=True
         )
@@ -703,8 +725,6 @@
             outs_back[place] = shift_node(after(outs_back[place], *earlier), -order[place])
 
     node, core = fsdp_rank // 2, fsdp_rank % 2
-    dots = jnp.stack([one[0] for one in gate_dots] + [one[1] for one in gate_dots], axis=1)
-    dots = scatter_dots(dots)
     mine, others = dots[:, :nodes], swap_core(dots[:, nodes:])
     pair = jnp.where(core == 0, jnp.stack([mine, others]), jnp.stack([others, mine]))
     placed = jnp.stack(
@@ -751,7 +771,7 @@
         probs_bf = probs_full.astype(BF16)
         out_block = block_of(heads_grad, block_index)
         if block_index > 0:
-            out_block = after(out_block, early_out, out_w_swapped[1])
+            out_block = after(out_block, early_out, out_w_swapped[1], outs_back[0])
         value_grad = value_grad + jnp.einsum(
             "hqk,qhd->khd", probs_bf, out_block, preferred_element_type=F32
         )
@@ -800,13 +820,13 @@
         home(place, (heads_grad, heads_grad, query_blocks_grad[-1], first_grad)[min(place, 3)])
     output = (hidden_res + sum(one.astype(F32) for one in outs_back)).astype(BF16)
     qkv_w_grad = dot_tn(first_all, qkv_grad).astype(BF16)
-    up_w_grad = wide_products(rows_kept, after(up_kept, first_part, qkv_w_grad, outs_back[0]), local_experts)
+    up_w_grad = wide_products(rows_kept, after(up_kept, first_part, qkv_w_grad), local_experts)
     down_w_grad = down_w_grad.reshape(local_experts, hidden_slice, model_width)
 
     attn_gain_grad = jnp.sum(normed_one * first_grad, axis=0)
     input_grad = residual_grad + norm_back(normed_one, scale_one, first_grad * attn_gain)
 
-    qkv_out = sum_rows(*swap_rows(qkv_w_grad))
+    qkv_out = sum_rows(*swap_rows(qkv_w_grad), up_w_grad)
 
     def widen(grad):
         return lax.dynamic_update_slice_in_dim(

time: 1520 us -> 1570 us (1.033)
  waiting for transfers between devices: 577 us -> 637 us
    ppermute x69, waiting for transfers between devices: 271 us -> 313 us  [swap_tp(): return lax.ppermute(operand, 'tp', [(i, i ^ mask) for i in range(count)])]
    ppermute x30, starting transfers between devices: 39.5 us -> 61.1 us  [shift_node(): lax.ppermute(operand, 'fsdp', [(i, (i // 2 + step) % nodes * 2 + i % 2) f...]
    ppermute x30, waiting for transfers between devices: 262 us -> 281 us  [shift_node(): lax.ppermute(operand, 'fsdp', [(i, (i // 2 + step) % nodes * 2 + i % 2) f...]
    convert_element_type x6 -> x7, other arithmetic: 31.9 us -> 31.6 us  [the longest x2 13.9 us: shards(): plus(after(one[0], *pins), one[1]).astype(BF16)]
  transfers between devices with their start and end apart: 130 -> 130, of which waited for: 67 -> 61; matrix products, arithmetic and copies ran while one was open for 23% -> 20% of each run, Pallas kernels for 27% -> 26%
where the time goes in v5:
time: 1570 us; the launch traced here: 1560 us
  waiting for transfers between devices  637 us (41%)
  Pallas kernels  404 us (26%)
  matrix products  154 us (10%)
  starting transfers between devices  139 us (9%)
  other arithmetic  128 us (8%)
  local copies, waits for them, and re-layouts  80.9 us (5%)
  between operations  17.4 us (1%)
    ppermute x69, waiting for transfers between devices, swap_tp(): return lax.ppermute(operand, 'tp', [(i, i ^ mask) for i in range(count)])  313 us
    ppermute x30, waiting for transfers between devices, shift_node(): lax.ppermute(operand, 'fsdp', [(i, (i // 2 + step) % nodes * 2 + i % 2) f...  281 us
    pallas_call x8, Pallas kernels, expert_products(): pl.pallas_call(functools.partial(expert_kernel, extra, experts), out_shap...  242 us
    pallas_call x2, Pallas kernels, wide_products(): pl.pallas_call(wide_kernel, out_shape=jax.ShapeDtypeStruct((count, width,...  106 us
    dot_general x9, matrix products, dot_nt(): lax.dot_general(a, b, (((1,), (1,)), ((), ())), preferred_element_type=F32)  74.2 us
    ppermute x69, starting transfers between devices, swap_tp(): return lax.ppermute(operand, 'tp', [(i, i ^ mask) for i in range(count)])  72.5 us
    ppermute x30, starting transfers between devices, shift_node(): lax.ppermute(operand, 'fsdp', [(i, (i // 2 + step) % nodes * 2 + i % 2) f...  61.1 us
    pallas_call x2, Pallas kernels, down_products(): pl.pallas_call(functools.partial(down_kernel, spans, first is not None),...  56.5 us
  transfers between devices with their start and end apart: 130, of which 61 were waited for; matrix products, arithmetic and copies ran while one was open for 20% of the time, Pallas kernels for 26%

profile of v5, /device:TPU:0, one launch (start us, length us, event | category | flops | bytes accessed | tf_op | source)
XLA Modules:
  0.0 1559.7 jit_solution(13331967259022530086)
XLA Ops:
  64.8 33.3 %all-gather.8.cloned.1.call-done = bf16[2048,2048]{0,1:T(8,128)(2,1)} async-done(((bf16[256,2048]{0,1:T(8,128)(2,1)}), bf16[2048,2048]{0,1:T(8,128)(2,1)}) %all-gather.8.cloned.1.call-update) | async-done | bytes 8388624 | tf_op jit(solution)/shard_map/all_gather | solution.py:496
  140.9 21.0 %collective-permute-done.13 = bf16[256,2048]{1,0:T(8,128)(2,1)S(1)} collective-permute-done((bf16[256,2048]{1,0:T(8,128)(2,1)S(1)}, bf16[256,2048]{1,0:T(8,128)(2,1)S(1)}, u32[]{:S(2)}, u32[]{:S(2)}) %collective-permute-start.13) | collective-permute-done | bytes 1048608 | tf_op jit(solution)/shard_map/ppermute | solution.py:39
  179.9 22.5 %collective-permute-done.16 = bf16[128,2048]{1,0:T(8,128)(2,1)S(1)} collective-permute-done((bf16[128,2048]{1,0:T(8,128)(2,1)S(1)}, bf16[128,2048]{1,0:T(8,128)(2,1)S(1)}, u32[]{:S(2)}, u32[]{:S(2)}) %collective-permute-start.16) | collective-permute-done | bytes 524320 | tf_op jit(solution)/shard_map/ppermute | solution.py:56
  204.7 17.8 %collective-permute-done.15 = bf16[128,2048]{1,0:T(8,128)(2,1)S(1)} collective-permute-done((bf16[128,2048]{1,0:T(8,128)(2,1)S(1)}, bf16[128,2048]{1,0:T(8,128)(2,1)S(1)}, u32[]{:S(2)}, u32[]{:S(2)}) %collective-permute-start.15) | collective-permute-done | bytes 524320 | tf_op jit(solution)/shard_map/ppermute | solution.py:56
  227.9 13.1 collective-permute-done.18
  284.5 22.4 %collective-permute-done.22 = bf16[128,2176]{1,0:T(8,128)(2,1)S(1)} collective-permute-done((bf16[128,2176]{1,0:T(8,128)(2,1)S(1)}, bf16[128,2176]{1,0:T(8,128)(2,1)S(1)}, u32[]{:S(2)}, u32[]{:S(2)}) %collective-permute-start.22) | collective-permute-done | bytes 557088 | tf_op jit(solution)/shard_map/ppermute | solution.py:56
  319.6 30.1 %shard_map.254 = (bf16[1024,2048]{1,0:T(8,128)(2,1)}, bf16[1024,2048]{1,0:T(8,128)(2,1)}, f32[1024,128]{1,0:T(8,128)}, bf16[8,1024,1024]{2,1,0:T(8,128)(2,1)}, b...) custom-call(s32[1]{0:T(128)} %bitcast.16.base, ...), custom_call_target="tpu_custom_call" | custom-call | flops 21474836480 | bytes 37748736 | tf_op jit(solution)/shard_map/pallas_call | solution.py:303
  354.2 25.5 %collective-permute-done.32 = bf16[256,2176]{1,0:T(8,128)(2,1)S(1)} collective-permute-done((bf16[256,2176]{1,0:T(8,128)(2,1)S(1)}, bf16[256,2176]{1,0:T(8,128)(2,1)S(1)}, u32[]{:S(2)}, u32[]{:S(2)}) %collective-permute-start.32) | collective-permute-done | bytes 1114144 | tf_op jit(solution)/shard_map/ppermute | solution.py:39
  390.5 30.1 %shard_map.255 = (bf16[1024,2048]{1,0:T(8,128)(2,1)}, bf16[1024,2048]{1,0:T(8,128)(2,1)}, f32[1024,128]{1,0:T(8,128)}, bf16[8,1024,1024]{2,1,0:T(8,128)(2,1)}, b...) custom-call(s32[1]{0:T(128)} %bitcast.16.base, ...), custom_call_target="tpu_custom_call", output_to_operand_aliasing={{3}: (6, {}), {4}: (7, {}), {5}: (8, {}), {6}: (9, {})} | custom-call | flops 21474836480 | bytes 37748736 | tf_op jit(solution)/shard_map/pallas_call | solution.py:303
  423.1 25.2 %collective-permute-done.56 = bf16[256,2048]{1,0:T(8,128)(2,1)S(1)} collective-permute-done((bf16[256,2048]{1,0:T(8,128)(2,1)S(1)}, bf16[256,2048]{1,0:T(8,128)(2,1)S(1)}, u32[]{:S(2)}, u32[]{:S(2)}) %collective-permute-start.56) | collective-permute-done | bytes 1048608 | tf_op jit(solution)/shard_map/ppermute | solution.py:39
  476.2 30.1 %shard_map.256 = (bf16[1024,2048]{1,0:T(8,128)(2,1)}, bf16[1024,2048]{1,0:T(8,128)(2,1)}, f32[1024,128]{1,0:T(8,128)}, bf16[8,1024,1024]{2,1,0:T(8,128)(2,1)}, b...) custom-call(s32[1]{0:T(128)} %bitcast.16.base, ...), custom_call_target="tpu_custom_call", output_to_operand_aliasing={{3}: (6, {}), {4}: (7, {}), {5}: (8, {}), {6}: (9, {})} | custom-call | flops 21474836480 | bytes 37748736 | tf_op jit(solution)/shard_map/pallas_call | solution.py:303
  506.4 13.4 convolution_convert_fusion.1
  522.3 30.2 %shard_map.257 = (bf16[1024,2048]{1,0:T(8,128)(2,1)}, bf16[1024,2048]{1,0:T(8,128)(2,1)}, f32[1024,128]{1,0:T(8,128)}, bf16[8,1024,1024]{2,1,0:T(8,128)(2,1)}, b...) custom-call(s32[1]{0:T(128)} %bitcast.16.base, ...), custom_call_target="tpu_custom_call", output_to_operand_aliasing={{3}: (6, {}), {4}: (7, {}), {5}: (8, {}), {6}: (9, {})} | custom-call | flops 21474836480 | bytes 37748736 | tf_op jit(solution)/shard_map/pallas_call | solution.py:303
  554.2 27.1 %collective-permute-done.31 = bf16[256,2176]{1,0:T(8,128)(2,1)S(1)} collective-permute-done((bf16[256,2176]{1,0:T(8,128)(2,1)S(1)}, bf16[256,2176]{1,0:T(8,128)(2,1)S(1)}, u32[]{:S(2)}, u32[]{:S(2)}) %collective-permute-start.31) | collective-permute-done | bytes 1114144 | tf_op jit(solution)/shard_map/ppermute | solution.py:39
  588.1 18.2 %collective-permute-done.44 = bf16[128,2048]{1,0:T(8,128)(2,1)S(1)} collective-permute-done((bf16[128,2048]{1,0:T(8,128)(2,1)S(1)}, bf16[128,2048]{1,0:T(8,128)(2,1)S(1)}, u32[]{:S(2)}, u32[]{:S(2)}) %collective-permute-start.44) | collective-permute-done | bytes 524320 | tf_op jit(solution)/shard_map/ppermute | solution.py:56
  608.9 12.9 collective-permute-done.37
  628.8 14.3 collective-permute-done.46
  653.1 30.4 %shard_map.258 = (bf16[1024,2048]{1,0:T(8,128)(2,1)}, bf16[1024,2048]{1,0:T(8,128)(2,1)}, f32[1024,128]{1,0:T(8,128)}, bf16[8,1024,1024]{2,1,0:T(8,128)(2,1)}, b...) custom-call(s32[1]{0:T(128)} %bitcast.16.base, ...), custom_call_target="tpu_custom_call", output_to_operand_aliasing={{3}: (6, {}), {4}: (7, {}), {5}: (8, {}), {6}: (9, {})} | custom-call | flops 21474836480 | bytes 37748736 | tf_op jit(solution)/shard_map/pallas_call | solution.py:303
  683.7 30.6 %shard_map.259 = (bf16[1024,2048]{1,0:T(8,128)(2,1)}, bf16[1024,2048]{1,0:T(8,128)(2,1)}, f32[1024,128]{1,0:T(8,128)}, bf16[8,1024,1024]{2,1,0:T(8,128)(2,1)}, b...) custom-call(s32[1]{0:T(128)} %bitcast.16.base, ...), custom_call_target="tpu_custom_call", output_to_operand_aliasing={{3}: (6, {}), {4}: (7, {}), {5}: (8, {}), {6}: (9, {})} | custom-call | flops 21474836480 | bytes 37748736 | tf_op jit(solution)/shard_map/pallas_call | solution.py:303
  750.1 30.2 %shard_map.260 = (bf16[1024,2048]{1,0:T(8,128)(2,1)}, bf16[1024,2048]{1,0:T(8,128)(2,1)}, f32[1024,128]{1,0:T(8,128)}, bf16[8,1024,1024]{2,1,0:T(8,128)(2,1)}, b...) custom-call(s32[1]{0:T(128)} %bitcast.16.base, ...), custom_call_target="tpu_custom_call", output_to_operand_aliasing={{3}: (6, {}), {4}: (7, {}), {5}: (8, {}), {6}: (9, {})} | custom-call | flops 21474836480 | bytes 37748736 | tf_op jit(solution)/shard_map/pallas_call | solution.py:303
  826.1 30.5 %shard_map.261 = (bf16[1024,2048]{1,0:T(8,128)(2,1)}, bf16[1024,2048]{1,0:T(8,128)(2,1)}, f32[1024,128]{1,0:T(8,128)}, bf16[8,1024,1024]{2,1,0:T(8,128)(2,1)}, b...) custom-call(s32[1]{0:T(128)} %bitcast.16.base, ...), custom_call_target="tpu_custom_call", output_to_operand_aliasing={{3}: (6, {}), {4}: (7, {}), {5}: (8, {}), {6}: (9, {})} | custom-call | flops 21474836480 | bytes 37748736 | tf_op jit(solution)/shard_map/pallas_call | solution.py:303
  859.7 27.0 %shard_map.262.refs_3_ = f32[1024,2048]{1,0:T(8,128)} custom-call(bf16[8,1024,1024]{2,1,0:T(8,128)(2,1)} %get-tuple-element.184.left, bf16[1,1024,2048]{2,1,0:T(8,128)(2,1)} %bitcast.450, bf16[2,1024,2048]{2,1,0:T(8,128)(2,1)} %all-gather.18.cloned.1.call-done.refs_1_, bf16[1,1024,2048]{2,1,0:T(8,128)(2,1)} %all-gather.20.cloned.1.call-done.refs_2_), custom_call_target="tpu_custom_call" | custom-call | flops 17179869184 | bytes 33554432 | tf_op jit(solution)/shard_map/pallas_call | solution.py:407
  920.0 29.6 %shard_map.263 = f32[1024,2048]{1,0:T(8,128)} custom-call(bf16[8,1024,1024]{2,1,0:T(8,128)(2,1)} %get-tuple-element.184.left, bf16[1,1024,2048]{2,1,0:T(8,128)(2,1)} %collective-permute-done.28.refs_0_, bf16[2,1024,2048]{2,1,0:T(8,128)(2,1)} %collective-permute-done.41.refs_1_, bf16[1,1024,2048]{2,1,0:T(8,128)(2,1)} %collective-permute-done.59.refs_2_, ...), custom_call_target="tpu_custom_call" | custom-call | flops 17179869184 | bytes 33554432 | tf_op jit(solution)/shard_map/pallas_call | solution.py:407
  975.7 22.7 %collective-permute-done.71 = bf16[128,2048]{1,0:T(8,128)(2,1)S(1)} collective-permute-done((bf16[128,2048]{1,0:T(8,128)(2,1)}, bf16[128,2048]{1,0:T(8,128)(2,1)S(1)}, u32[]{:S(2)}, u32[]{:S(2)}) %collective-permute-start.71) | collective-permute-done | bytes 524320 | tf_op jit(solution)/shard_map/ppermute | solution.py:56
  1031.7 42.7 %collective-permute-done.73 = bf16[256,2048]{1,0:T(8,128)(2,1)} collective-permute-done((bf16[256,2048]{1,0:T(8,128)(2,1)}, bf16[256,2048]{1,0:T(8,128)(2,1)}, u32[]{:S(2)}, u32[]{:S(2)}) %collective-permute-start.73) | collective-permute-done | bytes 1048608 | tf_op jit(solution)/shard_map/ppermute | solution.py:39
  1095.7 52.8 %shard_map.264 = f32[4,2048,256]{2,1,0:T(8,128)} custom-call(bf16[8,2048,1024]{2,1,0:T(8,128)(2,1)} %get-tuple-element.189.left, bf16[8,1024,1024]{2,1,0:T(8,128)(2,1)} %get-tuple-element.197.right), custom_call_target="tpu_custom_call" | custom-call | flops 34359738368 | bytes 58720256 | tf_op jit(solution)/shard_map/pallas_call | solution.py:353
  1167.4 18.7 %collective-permute-done.82 = bf16[128,2048]{1,0:T(8,128)(2,1)S(1)} collective-permute-done((bf16[128,2048]{1,0:T(8,128)(2,1)S(1)}, bf16[128,2048]{1,0:T(8,128)(2,1)S(1)}, u32[]{:S(2)}, u32[]{:S(2)}) %collective-permute-start.82) | collective-permute-done | bytes 524320 | tf_op jit(solution)/shard_map/ppermute | solution.py:56
  1356.9 37.1 %collective-permute-done.110 = f32[3,256]{1,0:T(4,128)S(1)} collective-permute-done((f32[3,256]{1,0:T(4,128)S(1)}, f32[3,256]{1,0:T(4,128)S(1)}, u32[]{:S(2)}, u32[]{:S(2)}) %collective-permute-start.110) | collective-permute-done | bytes 3104 | tf_op jit(solution)/shard_map/ppermute | solution.py:39
  1394.0 24.1 %collective-permute-start.111 = (f32[3,256]{1,0:T(4,128)S(1)}, f32[3,256]{1,0:T(4,128)S(1)}, u32[]{:S(2)}, u32[]{:S(2)}) collective-permute-start(f32[3,256]{1,0:T(4,128)S(1)} %bitcast.440), channel_id=1, source_target_pairs={{0,16},{4,20},{8,24},{12,28},{16,0},{20,4},{24,8},{28,12},{1,17},{... | collective-permute-start | bytes 9224 | tf_op jit(solution)/shard_map/ppermute | solution.py:39
  1418.1 53.0 %shard_map.265 = f32[4,2048,256]{2,1,0:T(8,128)} custom-call(bf16[8,2048,1024]{2,1,0:T(8,128)(2,1)} %get-tuple-element.189.left, bf16[8,1024,1024]{2,1,0:T(8,128)(2,1)} %get-tuple-element.206.right), custom_call_target="tpu_custom_call" | custom-call | flops 34359738368 | bytes 58720256 | tf_op jit(solution)/shard_map/pallas_call | solution.py:353
  1490.9 12.7 collective-permute-done.117
  1516.2 33.2 %collective-permute-done.118 = bf16[256,1536]{1,0:T(8,128)(2,1)S(1)} collective-permute-done((bf16[256,1536]{1,0:T(8,128)(2,1)S(1)}, bf16[256,1536]{1,0:T(8,128)(2,1)S(1)}, u32[]{:S(2)}, u32[]{:S(2)}) %collective-permute-start.118) | collective-permute-done | bytes 786464 | tf_op jit(solution)/shard_map/ppermute | solution.py:39
  (766 shorter events, 680.1 us)
Async XLA Ops:
  7.3 90.8 %all-gather.8.cloned.1.call-start = ((), (), s32[]{:S(2)}) async-start(), calls=%async_computation.3 | async-start | bytes 9437184 | tf_op jit(solution)/shard_map/all_gather | solution.py:496
  12.7 158.3 %all-gather.10.cloned.1.call-start = ((), (), s32[]{:S(2)}) async-start(), calls=%async_computation.4 | async-start | bytes 5242880 | tf_op jit(solution)/shard_map/all_gather | solution.py:509
  114.8 306.0 %all-gather.18.cloned.1.call-start = ((), (), s32[]{:S(2)}) async-start(), calls=%async_computation.8 | async-start | bytes 10485760 | tf_op jit(solution)/shard_map/all_gather | solution.py:569
  116.1 45.8 %collective-permute-start.13 = (bf16[256,2048]{1,0:T(8,128)(2,1)S(1)}, bf16[256,2048]{1,0:T(8,128)(2,1)S(1)}, u32[]{:S(2)}, u32[]{:S(2)}) collective-permute-start(bf16[256,2048]{1,0:T(8,128)(2,1)S(1)} %copy-done.19), channel_id=1, source_target_pairs={{0,8},{4,12},{8,16},{12,20},{16,24},{20,28},{24,0},{28,4},{1,9},{5... | collective-permute-start | bytes 3145736 | tf_op jit(solution)/shard_map/ppermute | solution.py:39
  164.4 285.3 %all-gather.16.cloned.1.call-start = ((), (), s32[]{:S(2)}) async-start(), calls=%async_computation.7 | async-start | bytes 5570560 | tf_op jit(solution)/shard_map/all_gather | solution.py:647
  177.9 44.6 %collective-permute-start.15 = (bf16[128,2048]{1,0:T(8,128)(2,1)S(1)}, bf16[128,2048]{1,0:T(8,128)(2,1)S(1)}, u32[]{:S(2)}, u32[]{:S(2)}) collective-permute-start(bf16[128,2048]{1,0:T(8,128)(2,1)S(1)} %get-tuple-element.274), channel_id=1, source_target_pairs={{0,2},{1,3},{2,0},{3,1},{4,6},{5,7},{6,4},{7,5},{8,10},{9,11},{10,... | collective-permute-start | bytes 1572872 | tf_op jit(solution)/shard_map/ppermute | solution.py:56
  350.7 231.7 %all-gather.14.cloned.1.call-start = ((), (), s32[]{:S(2)}) async-start(), calls=%async_computation.6 | async-start | bytes 5570560 | tf_op jit(solution)/shard_map/all_gather | solution.py:647
  380.8 247.9 %all-gather.20.cloned.1.call-start = ((), (), s32[]{:S(2)}) async-start(), calls=%async_computation.9 | async-start | bytes 5242880 | tf_op jit(solution)/shard_map/all_gather | solution.py:569
  420.8 85.6 %collective-permute-start.41 = (bf16[2,1024,2048]{2,1,0:T(8,128)(2,1)}, bf16[2,1024,2048]{2,1,0:T(8,128)(2,1)}, u32[]{:S(2)}, u32[]{:S(2)}) collective-permute-start(bf16[2,1024,2048]{2,1,0:T(8,128)(2,1)} %all-gather.18.cloned.1.call-done.refs_1_), channel_id=1, source_target_pairs={{0,4},{4,0},{8,12},{12,8},{16,20},{20,16},{24,28},{28,24},{1,5},{5... | collective-permute-start | bytes 25165832 | tf_op jit(solution)/shard_map/ppermute | solution.py:31
  449.2 234.3 %all-gather.12.cloned.1.call-start = ((), (), s32[]{:S(2)}) async-start(), calls=%async_computation.5 | async-start | bytes 5570560 | tf_op jit(solution)/shard_map/all_gather | solution.py:653
  449.7 56.7 %collective-permute-start.38 = (bf16[1024,2176]{1,0:T(8,128)(2,1)}, bf16[1024,2176]{1,0:T(8,128)(2,1)}, u32[]{:S(2)}, u32[]{:S(2)}) collective-permute-start(bf16[1024,2176]{1,0:T(8,128)(2,1)} %all-gather.16.cloned.1.call-done.refs_0_), channel_id=1, source_target_pairs={{0,4},{4,0},{8,12},{12,8},{16,20},{20,16},{24,28},{28,24},{1,5},{5... | collective-permute-start | bytes 13369352 | tf_op jit(solution)/shard_map/ppermute | solution.py:31
  554.1 54.8 %collective-permute-start.29 = (bf16[1024,2048]{1,0:T(8,128)(2,1)}, bf16[1024,2048]{1,0:T(8,128)(2,1)}, u32[]{:S(2)}, u32[]{:S(2)}) collective-permute-start(bf16[1024,2048]{1,0:T(8,128)(2,1)} %get-tuple-element.120), channel_id=1, source_target_pairs={{0,4},{4,0},{8,12},{12,8},{16,20},{20,16},{24,28},{28,24},{1,5},{5... | collective-permute-start | bytes 12582920 | tf_op jit(solution)/shard_map/ppermute | solution.py:31
  582.4 665.9 %reduce-scatter.4.cloned.1.call-start = ((), (), s32[]{:S(2)}) async-start(), calls=%async_computation.10 | async-start | bytes 10485760 | tf_op jit(solution)/shard_map/reduce_scatter | solution.py:714
  582.4 101.2 %collective-permute-start.42 = (bf16[1024,2176]{1,0:T(8,128)(2,1)}, bf16[1024,2176]{1,0:T(8,128)(2,1)}, u32[]{:S(2)}, u32[]{:S(2)}) collective-permute-start(bf16[1024,2176]{1,0:T(8,128)(2,1)} %all-gather.14.cloned.1.call-done.refs_0_), channel_id=1, source_target_pairs={{0,4},{4,0},{8,12},{12,8},{16,20},{20,16},{24,28},{28,24},{1,5},{5... | collective-permute-start | bytes 13369352 | tf_op jit(solution)/shard_map/ppermute | solution.py:31
  628.7 96.2 %collective-permute-start.59 = (bf16[1,1024,2048]{2,1,0:T(8,128)(2,1)}, bf16[1,1024,2048]{2,1,0:T(8,128)(2,1)}, u32[]{:S(2)}, u32[]{:S(2)}) collective-permute-start(bf16[1,1024,2048]{2,1,0:T(8,128)(2,1)} %all-gather.20.cloned.1.call-done.refs_2_), channel_id=1, source_target_pairs={{0,4},{4,0},{8,12},{12,8},{16,20},{20,16},{24,28},{28,24},{1,5},{5... | collective-permute-start | bytes 12582920 | tf_op jit(solution)/shard_map/ppermute | solution.py:31
  643.1 91.6 %collective-permute-start.58 = (bf16[1024,2048]{1,0:T(8,128)(2,1)}, bf16[1024,2048]{1,0:T(8,128)(2,1)}, u32[]{:S(2)}, u32[]{:S(2)}) collective-permute-start(bf16[1024,2048]{1,0:T(8,128)(2,1)} %get-tuple-element.159), channel_id=1, source_target_pairs={{0,4},{4,0},{8,12},{12,8},{16,20},{20,16},{24,28},{28,24},{1,5},{5... | collective-permute-start | bytes 12582920 | tf_op jit(solution)/shard_map/ppermute | solution.py:31
  683.5 57.2 %collective-permute-start.57 = (bf16[1024,2176]{1,0:T(8,128)(2,1)}, bf16[1024,2176]{1,0:T(8,128)(2,1)}, u32[]{:S(2)}, u32[]{:S(2)}) collective-permute-start(bf16[1024,2176]{1,0:T(8,128)(2,1)} %all-gather.12.cloned.1.call-done.refs_0_), channel_id=1, source_target_pairs={{0,4},{4,0},{8,12},{12,8},{16,20},{20,16},{24,28},{28,24},{1,5},{5... | collective-permute-start | bytes 13369352 | tf_op jit(solution)/shard_map/ppermute | solution.py:31
  780.3 76.4 %collective-permute-start.60 = (bf16[1024,2048]{1,0:T(8,128)(2,1)}, bf16[1024,2048]{1,0:T(8,128)(2,1)}, u32[]{:S(2)}, u32[]{:S(2)}) collective-permute-start(bf16[1024,2048]{1,0:T(8,128)(2,1)} %get-tuple-element.170), channel_id=1, source_target_pairs={{0,4},{4,0},{8,12},{12,8},{16,20},{20,16},{24,28},{28,24},{1,5},{5... | collective-permute-start | bytes 12582920 | tf_op jit(solution)/shard_map/ppermute | solution.py:31
  958.0 373.9 %reduce-scatter.8.cloned.1.call-start = ((), (), s32[]{:S(2)}) async-start(), calls=%async_computation.12 | async-start | bytes 5242880 | tf_op jit(solution)/shard_map/reduce_scatter | solution.py:718
  971.7 361.8 %reduce-scatter.6.cloned.1.call-start = ((), (), s32[]{:S(2)}) async-start(), calls=%async_computation.11 | async-start | bytes 5242880 | tf_op jit(solution)/shard_map/reduce_scatter | solution.py:718
  1010.9 63.5 %collective-permute-start.73 = (bf16[256,2048]{1,0:T(8,128)(2,1)}, bf16[256,2048]{1,0:T(8,128)(2,1)}, u32[]{:S(2)}, u32[]{:S(2)}) collective-permute-start(bf16[256,2048]{1,0:T(8,128)(2,1)} %pad_maximum_fusion.8), channel_id=1, source_target_pairs={{0,16},{4,20},{8,24},{12,28},{16,0},{20,4},{24,8},{28,12},{1,17},{... | collective-permute-start | bytes 3145736 | tf_op jit(solution)/shard_map/ppermute | solution.py:39
  1090.5 59.5 %collective-permute-start.81 = (bf16[128,2048]{1,0:T(8,128)(2,1)S(1)}, bf16[128,2048]{1,0:T(8,128)(2,1)S(1)}, u32[]{:S(2)}, u32[]{:S(2)}) collective-permute-start(bf16[128,2048]{1,0:T(8,128)(2,1)S(1)} %get-tuple-element.304), channel_id=1, source_target_pairs={{0,2},{1,3},{2,0},{3,1},{4,6},{5,7},{6,4},{7,5},{8,10},{9,11},{10,... | collective-permute-start | bytes 1572872 | tf_op jit(solution)/shard_map/ppermute | solution.py:56
  1091.9 60.7 %collective-permute-start.79 = (bf16[128,2048]{1,0:T(8,128)(2,1)S(1)}, bf16[128,2048]{1,0:T(8,128)(2,1)S(1)}, u32[]{:S(2)}, u32[]{:S(2)}) collective-permute-start(bf16[128,2048]{1,0:T(8,128)(2,1)S(1)} %get-tuple-element.304), channel_id=1, source_target_pairs={{0,1},{1,0},{2,3},{3,2},{4,5},{5,4},{6,7},{7,6},{8,9},{9,8},{10,11... | collective-permute-start | bytes 1572872 | tf_op jit(solution)/shard_map/ppermute | solution.py:56
  1093.2 57.7 %collective-permute-start.78 = (bf16[128,2048]{1,0:T(8,128)(2,1)S(1)}, bf16[128,2048]{1,0:T(8,128)(2,1)S(1)}, u32[]{:S(2)}, u32[]{:S(2)}) collective-permute-start(bf16[128,2048]{1,0:T(8,128)(2,1)S(1)} %get-tuple-element.305), channel_id=1, source_target_pairs={{0,1},{1,0},{2,3},{3,2},{4,5},{5,4},{6,7},{7,6},{8,9},{9,8},{10,11... | collective-permute-start | bytes 1572872 | tf_op jit(solution)/shard_map/ppermute | solution.py:56
  1094.0 54.5 %collective-permute-start.92 = (f32[33,256]{1,0:T(8,128)S(1)}, f32[33,256]{1,0:T(8,128)S(1)}, u32[]{:S(2)}, u32[]{:S(2)}) collective-permute-start(f32[33,256]{1,0:T(8,128)S(1)} %fusion.99), channel_id=1, source_target_pairs={{0,2},{1,3},{2,0},{3,1},{4,6},{5,7},{6,4},{7,5},{8,10},{9,11},{10,... | collective-permute-start | bytes 101384 | tf_op jit(solution)/shard_map/ppermute | solution.py:56
  1094.8 55.2 %collective-permute-start.91 = (f32[33,256]{1,0:T(8,128)S(1)}, f32[33,256]{1,0:T(8,128)S(1)}, u32[]{:S(2)}, u32[]{:S(2)}) collective-permute-start(f32[33,256]{1,0:T(8,128)S(1)} %fusion.99), channel_id=1, source_target_pairs={{0,1},{1,0},{2,3},{3,2},{4,5},{5,4},{6,7},{7,6},{8,9},{9,8},{10,11... | collective-permute-start | bytes 101384 | tf_op jit(solution)/shard_map/ppermute | solution.py:56
  1331.9 148.9 %collective-permute-start.108 = (bf16[256,2048]{1,0:T(8,128)(2,1)}, bf16[256,2048]{1,0:T(8,128)(2,1)}, u32[]{:S(2)}, u32[]{:S(2)}) collective-permute-start(bf16[256,2048]{1,0:T(8,128)(2,1)} %reduce-scatter.8.cloned.1.call-done), channel_id=1, source_target_pairs={{0,16},{4,20},{8,24},{12,28},{16,0},{20,4},{24,8},{28,12},{1,17},{... | collective-permute-start | bytes 3145736 | tf_op jit(solution)/shard_map/ppermute | solution.py:39
  1331.9 149.4 %collective-permute-start.86 = (bf16[256,2048]{1,0:T(8,128)(2,1)}, bf16[256,2048]{1,0:T(8,128)(2,1)}, u32[]{:S(2)}, u32[]{:S(2)}) collective-permute-start(bf16[256,2048]{1,0:T(8,128)(2,1)} %get-tuple-element.200), channel_id=1, source_target_pairs={{0,24},{4,28},{8,0},{12,4},{16,8},{20,12},{24,16},{28,20},{1,25},{... | collective-permute-start | bytes 3145736 | tf_op jit(solution)/shard_map/ppermute | solution.py:39
  1333.5 147.8 %collective-permute-start.95 = (bf16[256,2048]{1,0:T(8,128)(2,1)}, bf16[256,2048]{1,0:T(8,128)(2,1)}, u32[]{:S(2)}, u32[]{:S(2)}) collective-permute-start(bf16[256,2048]{1,0:T(8,128)(2,1)} %reduce-scatter.6.cloned.1.call-done), channel_id=1, source_target_pairs={{0,8},{4,12},{8,16},{12,20},{16,24},{20,28},{24,0},{28,4},{1,9},{5... | collective-permute-start | bytes 3145736 | tf_op jit(solution)/shard_map/ppermute | solution.py:39
  1356.4 120.6 %collective-permute-start.116 = (bf16[4,256,1536]{2,1,0:T(8,128)(2,1)}, bf16[4,256,1536]{2,1,0:T(8,128)(2,1)}, u32[]{:S(2)}, u32[]{:S(2)}) collective-permute-start(bf16[4,256,1536]{2,1,0:T(8,128)(2,1)} %dynamic-slice_bitcast_fusion), channel_id=1, source_target_pairs={{0,4},{4,0},{8,12},{12,8},{16,20},{20,16},{24,28},{28,24},{1,5},{5... | collective-permute-start | bytes 9437192 | tf_op jit(solution)/shard_map/ppermute | solution.py:31
  1394.0 77.1 %collective-permute-start.111 = (f32[3,256]{1,0:T(4,128)S(1)}, f32[3,256]{1,0:T(4,128)S(1)}, u32[]{:S(2)}, u32[]{:S(2)}) collective-permute-start(f32[3,256]{1,0:T(4,128)S(1)} %bitcast.440), channel_id=1, source_target_pairs={{0,16},{4,20},{8,24},{12,28},{16,0},{20,4},{24,8},{28,12},{1,17},{... | collective-permute-start | bytes 9224 | tf_op jit(solution)/shard_map/ppermute | solution.py:39
  1485.1 64.3 %collective-permute-start.118 = (bf16[256,1536]{1,0:T(8,128)(2,1)S(1)}, bf16[256,1536]{1,0:T(8,128)(2,1)S(1)}, u32[]{:S(2)}, u32[]{:S(2)}) collective-permute-start(bf16[256,1536]{1,0:T(8,128)(2,1)S(1)} %get-tuple-element.231), channel_id=1, source_target_pairs={{0,16},{4,20},{8,24},{12,28},{16,0},{20,4},{24,8},{28,12},{1,17},{... | collective-permute-start | bytes 2359304 | tf_op jit(solution)/shard_map/ppermute | solution.py:39
  (226 other events, 4239.1 us)
Sparse Core Ops, SparseCore 0:
  12.8 85.1 all-gather.7
  114.9 50.8 all-gather.9
  167.7 145.5 all-gather.17
  350.8 56.1 all-gather.15
  408.7 62.2 all-gather.13
  473.3 60.1 all-gather.19
  582.5 82.2 all-gather.11
  958.2 94.2 reduce-scatter.3
  1055.7 63.8 reduce-scatter.7
  1122.4 66.2 reduce-scatter.5
